TPU v7x, 32 devices: a whole 2x2x4 slice. The times are simulated.
32 devices in a mesh: blk: 8 (over z, y), rep: 4 (over x, core).
Axes of the slice: x: 2, y: 2, z: 4, core: 2. Of those that a mesh axis runs over, the one named last changes fastest.
Arguments:
- features: bfloat16 [8192, 256], P(('blk', 'rep')), may hold values from -6 to 6
- node_type: int32 [8192], P(('blk', 'rep')), may hold values from 0 to 3, as said below
- time_gap: int32 [8192], P(('blk', 'rep')), may hold values from 0 to 15
- node_valid: int32 [8192], P(('blk', 'rep')), may hold values from 0 to 1, as said below
- edge_codes: int32 [8192, 2048], P(('blk', 'rep')), may hold values from 0 to 2, as said below
- query_w: bfloat16 [4, 256, 256], replicated, may hold values from -0.375 to 0.375
- key_w: bfloat16 [4, 256, 256], replicated, may hold values from -0.375 to 0.375
- value_w: bfloat16 [4, 256, 256], replicated, may hold values from -0.375 to 0.375
- out_w: bfloat16 [4, 256, 256], replicated, may hold values from -1.5 to 1.5
- rel_att: bfloat16 [8, 8, 32, 32], replicated, may hold values from -1 to 1
- rel_msg: bfloat16 [8, 8, 32, 32], replicated, may hold values from -1 to 1
- rel_prior: float32 [8, 8], replicated, may hold values from 0.5 to 2
- skip_logit: float32 [4], replicated, may hold values from -1.5 to 1.5
- rte_w: bfloat16 [256, 256], replicated, may hold values from -0.375 to 0.375
- ln_gain: float32 [256], replicated, may hold values from 0.5 to 1.5
- ln_bias: float32 [256], replicated, may hold values from -3 to 3
- cotangent: bfloat16 [8192, 256], P(('blk', 'rep')), may hold values from -6 to 6
Outputs:
- layer_out: bfloat16 [8192, 256], P(('blk', 'rep'))
- input_grad: bfloat16 [8192, 256], P(('blk', 'rep'))
- query_grad: float32 [4, 256, 256], replicated
- key_grad: float32 [4, 256, 256], replicated
- value_grad: float32 [4, 256, 256], replicated
- out_grad: float32 [4, 256, 256], replicated
- att_grad: float32 [8, 8, 32, 32], replicated
- msg_grad: float32 [8, 8, 32, 32], replicated
- prior_grad: float32 [8, 8], replicated
- skip_grad: float32 [4], replicated
- rte_grad: float32 [256, 256], replicated
- gain_grad: float32 [256], replicated
- bias_grad: float32 [256], replicated
Inputs may be any that keep to these rules, and one draw needn't show every extreme that they name: `node_type`: 0 paper, 1 author, 2 field, 3 institution. `node_valid`: each device's 256 rows hold its real nodes first and its padding after them. `edge_codes`: 0 no edge, 1 an edge whose relation follows from the two types, 2 a cited_by edge between two papers; edges join only real nodes and only the type pairs of the relation list.
All inputs are finite; a program needn't handle non-finite values.
Results may differ from a plain program's by a relative error of at most 0.022.
The roundings to bfloat16 on the way count: a program that leaves them out, or rounds other values in their place, can miss the bound.
Values may be sent and summed in bfloat16 or wider, within the bound.
A program may use at most 128 MiB of HBM per device.

v0:
```python
import math

import jax
import jax.numpy as jnp
import numpy as np
from jax import lax
from jax.sharding import PartitionSpec as P

LEVELS = 16


NEG_FILL = -1e30
LN_EPS = 1e-05
HIGH = lax.Precision.HIGHEST


def from_behind(block, axis, distance):
    devices = range(lax.axis_size(axis))
    route = [((i - distance) % len(devices), i) for i in devices]
    return lax.ppermute(block, axis, route)


def relation_table():
    rel_tab = np.zeros((4, 4, 8), np.float32)
    rel_tab[0, 1, 0] = 1.0
    rel_tab[1, 0, 1] = 1.0
    rel_tab[0, 0, 2] = 1.0
    rel_tab[2, 0, 4] = 1.0
    rel_tab[0, 2, 5] = 1.0
    rel_tab[3, 1, 6] = 1.0
    rel_tab[1, 3, 7] = 1.0
    return rel_tab


def time_table(level_count, feat_width):
    positions = jnp.arange(level_count, dtype=jnp.float32)[:, None]
    freq_idx = jnp.arange(feat_width // 2, dtype=jnp.float32)[None, :]
    phases = positions / jnp.power(10000.0, 2.0 * freq_idx / feat_width)
    return jnp.stack([jnp.sin(phases), jnp.cos(phases)], axis=2).reshape(level_count, feat_width)


def slot_spread(heads_arr, kind_hot):
    spread_out = heads_arr[:, :, None, :] * kind_hot[:, None, :, None]
    return spread_out.reshape(heads_arr.shape[0], heads_arr.shape[1], -1)


def slot_collapse(slot_arr, kind_hot):
    src_rows, head_count = (slot_arr.shape[0], slot_arr.shape[1])
    kind_count = kind_hot.shape[1]
    shaped = slot_arr.reshape(src_rows, head_count, kind_count, -1)
    return jnp.sum(shaped * kind_hot.astype(jnp.float32)[:, None, :, None], axis=2)


def block_scores(kv_blk, q_four, q_cite, code_blk, kind_count):
    key_blk, value_blk, kind_blk = kv_blk
    src_rows = key_blk.shape[0]
    head_count = q_four.shape[1]
    key_heads = key_blk.reshape(src_rows, head_count, -1)
    value_heads = value_blk.reshape(src_rows, head_count, -1)
    kind_hot = (kind_blk[:, None] == jnp.arange(kind_count).astype(jnp.bfloat16)[None, :]).astype(
        jnp.bfloat16
    )
    key_four = slot_spread(key_heads, kind_hot)
    value_four = slot_spread(value_heads, kind_hot)
    is_one = (code_blk == 1)[None]
    is_two = (code_blk == 2)[None]
    slot_dot = jnp.einsum("thc,shc->hts", q_four, key_four, preferred_element_type=jnp.float32)
    cite_dot = jnp.einsum("thd,shd->hts", q_cite, key_heads, preferred_element_type=jnp.float32)
    scores = jnp.where(is_one, slot_dot, jnp.where(is_two, cite_dot, NEG_FILL))
    return (scores, is_one, is_two, key_heads, value_heads, key_four, value_four, kind_hot)


def attend_block(run_state, kv_blk, q_four, q_cite, code_blk, kind_count):
    run_max, run_sum, acc_four, acc_cite = run_state
    scores, is_one, is_two, key_heads, value_heads, key_four, value_four, kind_hot = block_scores(
        kv_blk, q_four, q_cite, code_blk, kind_count
    )
    new_max = jnp.maximum(run_max, jnp.max(scores, axis=2))
    expd = jnp.where((code_blk > 0)[None], jnp.exp(scores - new_max[:, :, None]), 0.0)
    rescale = jnp.exp(run_max - new_max)
    run_sum = run_sum * rescale + jnp.sum(expd, axis=2)
    prob_low = expd.astype(jnp.bfloat16)
    zero_low = jnp.zeros_like(prob_low)
    p_one = jnp.where(is_one, prob_low, zero_low)
    p_two = jnp.where(is_two, prob_low, zero_low)
    rescale_t = rescale.T[:, :, None]
    acc_four = acc_four * rescale_t + jnp.einsum(
        "hts,shc->thc", p_one, value_four, preferred_element_type=jnp.float32
    )
    acc_cite = acc_cite * rescale_t + jnp.einsum(
        "hts,shd->thd", p_two, value_heads, preferred_element_type=jnp.float32
    )
    return (new_max, run_sum, acc_four, acc_cite)


def back_block(
    kv_blk, q_four, q_cite, grad_four, grad_cite, log_total, row_delta, code_blk, kind_count
):
    scores, is_one, is_two, key_heads, value_heads, key_four, value_four, kind_hot = block_scores(
        kv_blk, q_four, q_cite, code_blk, kind_count
    )
    prob_full = jnp.where((code_blk > 0)[None], jnp.exp(scores - log_total[:, :, None]), 0.0)
    prob_low = prob_full.astype(jnp.bfloat16)
    zero_low = jnp.zeros_like(prob_low)
    p_one = jnp.where(is_one, prob_low, zero_low)
    p_two = jnp.where(is_two, prob_low, zero_low)
    grad_slot = jnp.einsum(
        "thc,shc->hts", grad_four, value_four, preferred_element_type=jnp.float32
    )
    grad_other = jnp.einsum(
        "thd,shd->hts", grad_cite, value_heads, preferred_element_type=jnp.float32
    )
    grad_probs = jnp.where(is_one, grad_slot, jnp.where(is_two, grad_other, 0.0))
    grad_scores = (prob_full * (grad_probs - row_delta[:, :, None])).astype(jnp.bfloat16)
    d_one = jnp.where(is_one, grad_scores, zero_low)
    d_two = jnp.where(is_two, grad_scores, zero_low)
    qf_grad = jnp.einsum("hts,shc->thc", d_one, key_four, preferred_element_type=jnp.float32)
    qc_grad = jnp.einsum("hts,shd->thd", d_two, key_heads, preferred_element_type=jnp.float32)
    k_grad = slot_collapse(
        jnp.einsum("hts,thc->shc", d_one, q_four, preferred_element_type=jnp.float32), kind_hot
    )
    k_grad = k_grad + jnp.einsum("hts,thd->shd", d_two, q_cite, preferred_element_type=jnp.float32)
    v_grad = slot_collapse(
        jnp.einsum("hts,thc->shc", p_one, grad_four, preferred_element_type=jnp.float32), kind_hot
    )
    v_grad = v_grad + jnp.einsum(
        "hts,thd->shd", p_two, grad_cite, preferred_element_type=jnp.float32
    )
    src_rows = k_grad.shape[0]
    return (k_grad.reshape(src_rows, -1), v_grad.reshape(src_rows, -1), qf_grad, qc_grad)


def body(
    features,
    node_type,
    time_gap,
    node_valid,
    edge_codes,
    query_w,
    key_w,
    value_w,
    out_w,
    rel_att,
    rel_msg,
    rel_prior,
    skip_logit,
    rte_w,
    ln_gain,
    ln_bias,
    cotangent,
):
    tgt_rows, feat_dim = features.shape
    kind_count = query_w.shape[0]
    rel_count = rel_att.shape[0]
    head_count = rel_att.shape[1]
    head_size = rel_att.shape[2]
    n_blk = lax.axis_size("blk")
    my_blk = lax.axis_index("blk")
    type_hot = (node_type[:, None] == jnp.arange(kind_count)[None, :]).astype(jnp.float32)
    type_low = type_hot.astype(jnp.bfloat16)
    gap_hot = (time_gap[:, None] == jnp.arange(LEVELS)[None, :]).astype(jnp.float32)
    time_low = time_table(LEVELS, feat_dim).astype(jnp.bfloat16).astype(jnp.float32)
    rte_table = jnp.dot(time_low, rte_w.astype(jnp.float32), precision=HIGH)
    x_f = features.astype(jnp.float32)
    shifted = x_f + jnp.dot(gap_hot, rte_table, precision=HIGH)
    shifted_b = shifted.astype(jnp.bfloat16)

    def typed(inp, weights):
        parts = jnp.einsum("th,khd->tkd", inp, weights, preferred_element_type=jnp.float32)
        return jnp.sum(parts * type_hot[:, :, None], axis=1)

    def typed_grad(inp, grad_low):
        masked = inp[:, None, :] * type_low[:, :, None]
        return jnp.einsum("tkh,td->khd", masked, grad_low, preferred_element_type=jnp.float32)

    def typed_back(grad_low, weights):
        parts = jnp.einsum("td,khd->tkh", grad_low, weights, preferred_element_type=jnp.float32)
        return jnp.sum(parts * type_hot[:, :, None], axis=1)

    q_low = typed(features, query_w).astype(jnp.bfloat16)
    key_low = typed(shifted_b, key_w).astype(jnp.bfloat16)
    value_low = typed(shifted_b, value_w).astype(jnp.bfloat16)
    kind_low = node_type.astype(jnp.bfloat16)
    q_heads = q_low.reshape(tgt_rows, head_count, head_size).astype(jnp.float32)
    att_f = rel_att.astype(jnp.float32)
    factor = rel_prior / math.sqrt(head_size)
    rel_raw = jnp.einsum("thj,rhjk->rthk", q_heads, att_f, precision=HIGH)
    rel_query = (rel_raw * factor[:, None, :, None]).astype(jnp.bfloat16)
    select = jnp.einsum("tk,ksr->tsr", type_hot, jnp.asarray(relation_table()), precision=HIGH)
    select_low = select.astype(jnp.bfloat16)
    cite_hot = (jnp.arange(rel_count) == 3).astype(jnp.float32)
    q_four = (
        jnp.einsum("tsr,rthd->thsd", select_low, rel_query, preferred_element_type=jnp.float32)
        .astype(jnp.bfloat16)
        .reshape(tgt_rows, head_count, kind_count * head_size)
    )
    q_cite = rel_query[3]

    def block_codes(source):
        return lax.dynamic_slice_in_dim(edge_codes, source * tgt_rows, tgt_rows, 1)

    def forward_block(run_state, kv_blk, qf_part, qc_part, code_blk):
        result = attend_block(run_state, kv_blk, qf_part, qc_part, code_blk, kind_count)
        return result

    def backward_block(kv_blk, qf_part, qc_part, gf_part, gc_part, lse_part, delta_part, code_blk):
        return back_block(
            kv_blk, qf_part, qc_part, gf_part, gc_part, lse_part, delta_part, code_blk, kind_count
        )

    whole_kv = (key_low, value_low, kind_low)

    def forward_turn(step_idx, loop_state):
        run_state, kv_blk = loop_state
        run_state = forward_block(
            run_state, kv_blk, q_four, q_cite, block_codes((my_blk - step_idx) % n_blk)
        )
        kv_blk = from_behind((kv_blk[0], kv_blk[1], kv_blk[2]), "blk", 1)
        return (run_state, kv_blk)

    run_state, kv_last = lax.fori_loop(
        0,
        n_blk,
        forward_turn,
        (
            (
                jnp.full((head_count, tgt_rows), NEG_FILL, jnp.float32),
                jnp.zeros((head_count, tgt_rows), jnp.float32),
                jnp.zeros((tgt_rows, head_count, kind_count * head_size), jnp.float32),
                jnp.zeros((tgt_rows, head_count, head_size), jnp.float32),
            ),
            whole_kv,
        ),
    )
    run_max, run_sum, acc_four, acc_cite = run_state
    floor_sum = jnp.maximum(run_sum, 1.0)
    log_total = run_max + jnp.log(floor_sum)
    norm_t = floor_sum.T[:, :, None]
    u_four = acc_four / norm_t
    u_cite = acc_cite / norm_t
    u_rel = jnp.einsum(
        "tsr,thsd->rthd",
        select,
        u_four.reshape(tgt_rows, head_count, kind_count, head_size),
        precision=HIGH,
    )
    u_rel = u_rel + cite_hot[:, None, None, None] * u_cite[None]
    u_rel_b = u_rel.astype(jnp.bfloat16)
    agg_sum = jnp.einsum(
        "rthd,rhde->the", u_rel_b, rel_msg, preferred_element_type=jnp.float32
    ).reshape(tgt_rows, feat_dim)
    act_full, gelu_back = jax.vjp(jax.nn.gelu, agg_sum)
    act_low = act_full.astype(jnp.bfloat16)
    branch = typed(act_low, out_w)
    skip_all = jax.nn.sigmoid(skip_logit)
    skip_gate = jnp.sum(type_hot * skip_all[None, :], axis=1)[:, None]
    mixed_sum = skip_gate * branch + (1.0 - skip_gate) * x_f
    centered = mixed_sum - jnp.mean(mixed_sum, axis=1, keepdims=True)
    inv_std = lax.rsqrt(jnp.mean(centered * centered, axis=1, keepdims=True) + LN_EPS)
    normed = centered * inv_std
    valid_col = node_valid.astype(jnp.float32)[:, None]
    layer_out = (valid_col * (normed * ln_gain + ln_bias)).astype(jnp.bfloat16)
    grad_y = cotangent.astype(jnp.float32) * valid_col
    gain_grad = jnp.sum(grad_y * normed, axis=0)
    bias_grad = jnp.sum(grad_y, axis=0)
    grad_norm = grad_y * ln_gain
    grad_mix = inv_std * (
        grad_norm
        - jnp.mean(grad_norm, axis=1, keepdims=True)
        - normed * jnp.mean(grad_norm * normed, axis=1, keepdims=True)
    )
    grad_branch = (skip_gate * grad_mix).astype(jnp.bfloat16)
    gate_term = (
        jnp.sum(grad_mix * (branch - x_f), axis=1, keepdims=True) * skip_gate * (1.0 - skip_gate)
    )
    skip_grad = jnp.sum(type_hot * gate_term, axis=0)
    out_grad = typed_grad(act_low, grad_branch)
    grad_agg = gelu_back(typed_back(grad_branch, out_w))[0].astype(jnp.bfloat16)
    grad_agg_heads = grad_agg.reshape(tgt_rows, head_count, head_size)
    msg_grad = jnp.einsum(
        "rthd,the->rhde", u_rel_b, grad_agg_heads, preferred_element_type=jnp.float32
    )
    grad_urel = jnp.einsum(
        "the,rhde->rthd", grad_agg_heads, rel_msg, preferred_element_type=jnp.float32
    ).astype(jnp.bfloat16)
    grad_four = (
        jnp.einsum("tsr,rthd->thsd", select_low, grad_urel, preferred_element_type=jnp.float32)
        .astype(jnp.bfloat16)
        .reshape(tgt_rows, head_count, kind_count * head_size)
    )
    grad_cite = grad_urel[3]
    row_delta = (
        jnp.sum(grad_four.astype(jnp.float32) * u_four, axis=2)
        + jnp.sum(grad_cite.astype(jnp.float32) * u_cite, axis=2)
    ).T
    zero_four = jnp.zeros((tgt_rows, head_count, kind_count * head_size), jnp.float32)
    zero_cite = jnp.zeros((tgt_rows, head_count, head_size), jnp.float32)

    def back_turn(step_idx, loop_state):
        kv_blk, travel, acc_qf, acc_qc = loop_state
        k_grad, v_grad, qf_grad, qc_grad = backward_block(
            kv_blk,
            q_four,
            q_cite,
            grad_four,
            grad_cite,
            log_total,
            row_delta,
            block_codes((my_blk - step_idx) % n_blk),
        )
        travel = (
            from_behind((travel[0] + k_grad).astype(jnp.bfloat16), "blk", 1).astype(jnp.float32),
            from_behind((travel[1] + v_grad).astype(jnp.bfloat16), "blk", 1).astype(jnp.float32),
        )
        kv_blk = from_behind((kv_blk[0], kv_blk[1], kv_blk[2]), "blk", 1)
        return (kv_blk, travel, acc_qf + qf_grad, acc_qc + qc_grad)

    zero_kv = jnp.zeros((tgt_rows, feat_dim), jnp.float32)
    loop_state = lax.fori_loop(
        0, n_blk, back_turn, (whole_kv, (zero_kv, zero_kv), zero_four, zero_cite)
    )
    key_acc, value_acc = loop_state[1]
    acc_qf, acc_qc = (loop_state[2], loop_state[3])
    grad_key = key_acc.astype(jnp.bfloat16)
    grad_value = value_acc.astype(jnp.bfloat16)
    grad_relq = jnp.einsum(
        "tsr,thsd->rthd",
        select,
        acc_qf.reshape(tgt_rows, head_count, kind_count, head_size),
        precision=HIGH,
    )
    grad_relq = (
        (grad_relq + cite_hot[:, None, None, None] * acc_qc[None])
        .astype(jnp.bfloat16)
        .astype(jnp.float32)
    )
    prior_grad = jnp.sum(grad_relq * rel_raw, axis=(1, 3)) / math.sqrt(head_size)
    grad_raw = grad_relq * factor[:, None, :, None]
    att_grad = jnp.einsum("thj,rthk->rhjk", q_heads, grad_raw, precision=HIGH)
    grad_query = (
        jnp.einsum("rthk,rhjk->thj", grad_raw, att_f, precision=HIGH)
        .reshape(tgt_rows, feat_dim)
        .astype(jnp.bfloat16)
    )
    query_grad = typed_grad(features, grad_query)
    key_grad = typed_grad(shifted_b, grad_key)
    value_grad = typed_grad(shifted_b, grad_value)
    grad_shift = typed_back(grad_key, key_w) + typed_back(grad_value, value_w)
    table_grad = jnp.dot(gap_hot.T, grad_shift, precision=HIGH)
    rte_grad = jnp.dot(time_low.T, table_grad, precision=HIGH)
    input_grad = (
        (1.0 - skip_gate) * grad_mix + typed_back(grad_query, query_w) + grad_shift
    ).astype(jnp.bfloat16)
    summed = lax.psum(
        (
            query_grad,
            key_grad,
            value_grad,
            out_grad,
            att_grad,
            msg_grad,
            prior_grad,
            skip_grad,
            rte_grad,
            gain_grad,
            bias_grad,
        ),
        ("blk", "rep"),
    )
    return (
        layer_out,
        input_grad,
        summed[0],
        summed[1],
        summed[2],
        summed[3],
        summed[4],
        summed[5],
        summed[6],
        summed[7],
        summed[8],
        summed[9],
        summed[10],
    )


def solution(mesh):
    in_specs = (
        P(("blk", "rep"), None),
        P(("blk", "rep")),
        P(("blk", "rep")),
        P(("blk", "rep")),
        P(("blk", "rep"), None),
        P(),
        P(),
        P(),
        P(),
        P(),
        P(),
        P(),
        P(),
        P(),
        P(),
        P(),
        P(("blk", "rep"), None),
    )
    out_specs = (
        P(("blk", "rep"), None),
        P(("blk", "rep"), None),
        P(),
        P(),
        P(),
        P(),
        P(),
        P(),
        P(),
        P(),
        P(),
        P(),
        P(),
    )
    return jax.shard_map(body, mesh=mesh, in_specs=in_specs, out_specs=out_specs, check_vma=False)
```

profile of v0, /device:TPU:0, one launch (start us, length us, event | category | flops | bytes accessed | tf_op | source)
XLA Modules:
  0.0 631.8 jit_solution(6288788230206053555)
XLA Ops:
  14.0 6.5 %copy.213 = bf16[8,256,8,32]{3,0,2,1:T(8,128)(2,1)} copy(bf16[8,256,8,32]{1,3,0,2:T(8,128)(2,1)S(1)} %get-tuple-element.1045) | data formatting | bytes 2097152 | tf_op jit(solution)/shard_map/convert_element_type | solution.py:188
  31.9 4.8 convert_bitcast_fusion.1
  40.0 107.4 %while.56 = (s32[]{:T(128)}, f32[8,256]{1,0:T(8,128)S(1)}, f32[8,256]{1,0:T(8,128)}, f32[256,8,128]{0,2,1:T(8,128)}, f32[256,8,32]{0,2,1:T(8,128)}, /*index=5*/b...) while((s32[]{:T(128)}, f32[8,256]{1,0:T(8,128)S(1)}, ...), condition=%wide.region_7.8_spmd.clone, body=%wide.region_4.7_spmd.clone.sunk | while | flops 344602624 | bytes 31809676 | solution.py:221
  151.0 4.7 copy.220
  156.0 11.7 %fusion.154 = f32[256,8,32,8]{2,3,1,0:T(8,128)} fusion(f32[256,8,4,32]{3,2,1,0:T(4,128)} %copy.220, f32[256,4,8,1]{2,1,3,0:T(4,128)S(1)} %copy.271), kind=kOutput, calls=%fused_computation.242 | convolution fusion | flops 25165824 | bytes 3178496 | tf_op jit(solution)/shard_map/tsr,thsd->rthd/dot_general | solution.py:241
  167.7 7.4 %copy.222 = f32[256,8,32,8]{0,2,3,1:T(8,128)} copy(f32[256,8,32,8]{2,3,1,0:T(8,128)} %fusion.154) | data formatting | bytes 4194304 | tf_op jit(solution)/shard_map/tsr,thsd->rthd/dot_general | solution.py:241
  188.8 7.3 %copy.231 = bf16[8,256,8,32]{3,0,2,1:T(8,128)(2,1)} copy(bf16[8,256,8,32]{1,3,0,2:T(8,128)(2,1)} %fusion.57) | data formatting | bytes 2097152 | tf_op jit(solution)/shard_map/convert_element_type | solution.py:285
  199.5 4.8 convert_bitcast_fusion
  208.7 204.5 %while.57 = (s32[]{:T(128)}, bf16[256,256]{0,1:T(8,128)(2,1)S(1)}, bf16[256,256]{0,1:T(8,128)(2,1)}, bf16[256]{0:T(256)(128)(2,1)}, f32[256,256]{0,1:T(8,128)S(1...) while((s32[]{:T(128)}, bf16[256,256]{0,1:T(8,128)(2,1)S(1)}, ...), condition=%wide.region_19.20_spmd.clone, body=%wide.region_16.19_spmd.clone.sunk | while | flops 850725888 | bytes 45547712 | solution.py:319
  252.7 4.0 collective-permute-done.6
  278.3 3.4 collective-permute-done.6
  297.2 3.4 collective-permute-start.6
  306.1 3.6 collective-permute-done.7
  331.0 3.6 collective-permute-done.7
  347.1 3.4 collective-permute-start.6
  356.0 4.8 collective-permute-done.7
  372.4 3.4 collective-permute-start.6
  381.8 3.7 collective-permute-done.7
  399.1 3.4 collective-permute-start.6
  408.0 3.6 collective-permute-done.7
  422.4 11.5 %fusion.155 = f32[256,8,32,8]{2,3,1,0:T(8,128)} fusion(f32[256,8,4,32]{3,2,1,0:T(4,128)} %copy.237, f32[256,4,8,1]{2,1,3,0:T(4,128)S(1)} %copy-done.10), kind=kOutput, calls=%fused_computation.243 | convolution fusion | flops 25165824 | bytes 3178496 | tf_op jit(solution)/shard_map/tsr,thsd->rthd/dot_general | solution.py:326
  433.9 7.6 %copy.239 = f32[256,8,32,8]{0,2,3,1:T(8,128)} copy(f32[256,8,32,8]{2,3,1,0:T(8,128)} %fusion.155) | data formatting | bytes 4194304 | tf_op jit(solution)/shard_map/tsr,thsd->rthd/dot_general | solution.py:326
  456.6 38.6 %all-reduce = (f32[8,8]{0,1:T(8,128)S(1)}, f32[4]{0:T(128)}, f32[256]{0:T(256)}, f32[256]{0:T(256)}) all-reduce(f32[8,8]{0,1:T(8,128)S(1)} %broadcast_multiply_fusion, f32[4]{0:T(128)S(1)} %select_reduce_fusion, f32[256]{0:T(256)S(1)} %get-tuple-element.945, ...), channel_id=1, replica_groups=mesh['blk'=8,'rep'=4] {'blk','rep'}, use_global_device_ids=true, to_apply=%region_30.31 | all-reduce | flops 580 | bytes 4640 | tf_op jit(solution)/shard_map/psum | solution.py:354
  495.8 118.8 %all-reduce.4.cloned.1.call-done = (f32[4,256,256]{2,1,0:T(8,128)}, f32[4,256,256]{2,1,0:T(8,128)}, f32[4,256,256]{2,1,0:T(8,128)}, f32[4,256,256]{2,1,0:T(8,128...) async-done(((f32[4,256,256]{2,1,0:T(8,128)}, f32[4,256,256]{2,1,0:T(8,128)}, f32[4,256,256]{2,1,0:T(8,128)}, f32[4,256,256]{2,1,0:T(8,128)}, ...) | async-done | bytes 4980752 | tf_op jit(solution)/shard_map/psum | solution.py:354
  (838 shorter events, 349.7 us)
Async XLA Ops:
  7.2 607.4 %all-reduce.4.cloned.1.call-start = ((), (), s32[]{:S(2)}) async-start(), calls=%async_computation | async-start | bytes 13107200 | tf_op jit(solution)/shard_map/psum | solution.py:354
  209.0 27.9 %collective-permute-start.3 = (bf16[256,256]{0,1:T(8,128)(2,1)S(1)}, bf16[256,256]{0,1:T(8,128)(2,1)S(1)}, u32[]{:S(2)}, u32[]{:S(2)}) collective-permute-start(bf16[256,256]{0,1:T(8,128)(2,1)S(1)} %copy.343), channel_id=1, source_target_pairs={{28,0},{0,4},{4,8},{8,12},{12,16},{16,20},{20,24},{24,28},{29,1},{... | collective-permute-start | bytes 393224 | tf_op jit(solution)/shard_map/while/body/eval_jaxpr/ppermute | solution.py:20
  211.6 25.2 %collective-permute-start.4 = (bf16[256,256]{0,1:T(8,128)(2,1)S(1)}, bf16[256,256]{0,1:T(8,128)(2,1)}, u32[]{:S(2)}, u32[]{:S(2)}) collective-permute-start(bf16[256,256]{0,1:T(8,128)(2,1)S(1)} %copy.344), channel_id=1, source_target_pairs={{28,0},{0,4},{4,8},{8,12},{12,16},{16,20},{20,24},{24,28},{29,1},{... | collective-permute-start | bytes 393224 | tf_op jit(solution)/shard_map/while/body/eval_jaxpr/ppermute | solution.py:20
  214.2 22.6 %collective-permute-start.5 = (bf16[256]{0:T(256)(128)(2,1)}, bf16[256]{0:T(256)(128)(2,1)}, u32[]{:S(2)}, u32[]{:S(2)}) collective-permute-start(bf16[256]{0:T(256)(128)(2,1)} %copy.345), channel_id=1, source_target_pairs={{28,0},{0,4},{4,8},{8,12},{12,16},{16,20},{20,24},{24,28},{29,1},{... | collective-permute-start | bytes 1544 | tf_op jit(solution)/shard_map/while/body/eval_jaxpr/ppermute | solution.py:20
  236.9 24.8 %collective-permute-start.3 = (bf16[256,256]{0,1:T(8,128)(2,1)S(1)}, bf16[256,256]{0,1:T(8,128)(2,1)S(1)}, u32[]{:S(2)}, u32[]{:S(2)}) collective-permute-start(bf16[256,256]{0,1:T(8,128)(2,1)S(1)} %copy.343), channel_id=1, source_target_pairs={{28,0},{0,4},{4,8},{8,12},{12,16},{16,20},{20,24},{24,28},{29,1},{... | collective-permute-start | bytes 393224 | tf_op jit(solution)/shard_map/while/body/eval_jaxpr/ppermute | solution.py:20
  237.8 23.8 %collective-permute-start.4 = (bf16[256,256]{0,1:T(8,128)(2,1)S(1)}, bf16[256,256]{0,1:T(8,128)(2,1)}, u32[]{:S(2)}, u32[]{:S(2)}) collective-permute-start(bf16[256,256]{0,1:T(8,128)(2,1)S(1)} %copy.344), channel_id=1, source_target_pairs={{28,0},{0,4},{4,8},{8,12},{12,16},{16,20},{20,24},{24,28},{29,1},{... | collective-permute-start | bytes 393224 | tf_op jit(solution)/shard_map/while/body/eval_jaxpr/ppermute | solution.py:20
  261.7 24.8 %collective-permute-start.3 = (bf16[256,256]{0,1:T(8,128)(2,1)S(1)}, bf16[256,256]{0,1:T(8,128)(2,1)S(1)}, u32[]{:S(2)}, u32[]{:S(2)}) collective-permute-start(bf16[256,256]{0,1:T(8,128)(2,1)S(1)} %copy.343), channel_id=1, source_target_pairs={{28,0},{0,4},{4,8},{8,12},{12,16},{16,20},{20,24},{24,28},{29,1},{... | collective-permute-start | bytes 393224 | tf_op jit(solution)/shard_map/while/body/eval_jaxpr/ppermute | solution.py:20
  262.7 23.8 %collective-permute-start.4 = (bf16[256,256]{0,1:T(8,128)(2,1)S(1)}, bf16[256,256]{0,1:T(8,128)(2,1)}, u32[]{:S(2)}, u32[]{:S(2)}) collective-permute-start(bf16[256,256]{0,1:T(8,128)(2,1)S(1)} %copy.344), channel_id=1, source_target_pairs={{28,0},{0,4},{4,8},{8,12},{12,16},{16,20},{20,24},{24,28},{29,1},{... | collective-permute-start | bytes 393224 | tf_op jit(solution)/shard_map/while/body/eval_jaxpr/ppermute | solution.py:20
  263.8 22.7 %collective-permute-start.5 = (bf16[256]{0:T(256)(128)(2,1)}, bf16[256]{0:T(256)(128)(2,1)}, u32[]{:S(2)}, u32[]{:S(2)}) collective-permute-start(bf16[256]{0:T(256)(128)(2,1)} %copy.345), channel_id=1, source_target_pairs={{28,0},{0,4},{4,8},{8,12},{12,16},{16,20},{20,24},{24,28},{29,1},{... | collective-permute-start | bytes 1544 | tf_op jit(solution)/shard_map/while/body/eval_jaxpr/ppermute | solution.py:20
  286.5 24.8 %collective-permute-start.3 = (bf16[256,256]{0,1:T(8,128)(2,1)S(1)}, bf16[256,256]{0,1:T(8,128)(2,1)S(1)}, u32[]{:S(2)}, u32[]{:S(2)}) collective-permute-start(bf16[256,256]{0,1:T(8,128)(2,1)S(1)} %copy.343), channel_id=1, source_target_pairs={{28,0},{0,4},{4,8},{8,12},{12,16},{16,20},{20,24},{24,28},{29,1},{... | collective-permute-start | bytes 393224 | tf_op jit(solution)/shard_map/while/body/eval_jaxpr/ppermute | solution.py:20
  287.5 23.8 %collective-permute-start.4 = (bf16[256,256]{0,1:T(8,128)(2,1)S(1)}, bf16[256,256]{0,1:T(8,128)(2,1)}, u32[]{:S(2)}, u32[]{:S(2)}) collective-permute-start(bf16[256,256]{0,1:T(8,128)(2,1)S(1)} %copy.344), channel_id=1, source_target_pairs={{28,0},{0,4},{4,8},{8,12},{12,16},{16,20},{20,24},{24,28},{29,1},{... | collective-permute-start | bytes 393224 | tf_op jit(solution)/shard_map/while/body/eval_jaxpr/ppermute | solution.py:20
  288.6 22.7 %collective-permute-start.5 = (bf16[256]{0:T(256)(128)(2,1)}, bf16[256]{0:T(256)(128)(2,1)}, u32[]{:S(2)}, u32[]{:S(2)}) collective-permute-start(bf16[256]{0:T(256)(128)(2,1)} %copy.345), channel_id=1, source_target_pairs={{28,0},{0,4},{4,8},{8,12},{12,16},{16,20},{20,24},{24,28},{29,1},{... | collective-permute-start | bytes 1544 | tf_op jit(solution)/shard_map/while/body/eval_jaxpr/ppermute | solution.py:20
  311.4 24.8 %collective-permute-start.3 = (bf16[256,256]{0,1:T(8,128)(2,1)S(1)}, bf16[256,256]{0,1:T(8,128)(2,1)S(1)}, u32[]{:S(2)}, u32[]{:S(2)}) collective-permute-start(bf16[256,256]{0,1:T(8,128)(2,1)S(1)} %copy.343), channel_id=1, source_target_pairs={{28,0},{0,4},{4,8},{8,12},{12,16},{16,20},{20,24},{24,28},{29,1},{... | collective-permute-start | bytes 393224 | tf_op jit(solution)/shard_map/while/body/eval_jaxpr/ppermute | solution.py:20
  312.4 23.8 %collective-permute-start.4 = (bf16[256,256]{0,1:T(8,128)(2,1)S(1)}, bf16[256,256]{0,1:T(8,128)(2,1)}, u32[]{:S(2)}, u32[]{:S(2)}) collective-permute-start(bf16[256,256]{0,1:T(8,128)(2,1)S(1)} %copy.344), channel_id=1, source_target_pairs={{28,0},{0,4},{4,8},{8,12},{12,16},{16,20},{20,24},{24,28},{29,1},{... | collective-permute-start | bytes 393224 | tf_op jit(solution)/shard_map/while/body/eval_jaxpr/ppermute | solution.py:20
  313.5 22.7 %collective-permute-start.5 = (bf16[256]{0:T(256)(128)(2,1)}, bf16[256]{0:T(256)(128)(2,1)}, u32[]{:S(2)}, u32[]{:S(2)}) collective-permute-start(bf16[256]{0:T(256)(128)(2,1)} %copy.345), channel_id=1, source_target_pairs={{28,0},{0,4},{4,8},{8,12},{12,16},{16,20},{20,24},{24,28},{29,1},{... | collective-permute-start | bytes 1544 | tf_op jit(solution)/shard_map/while/body/eval_jaxpr/ppermute | solution.py:20
  336.2 26.2 %collective-permute-start.3 = (bf16[256,256]{0,1:T(8,128)(2,1)S(1)}, bf16[256,256]{0,1:T(8,128)(2,1)S(1)}, u32[]{:S(2)}, u32[]{:S(2)}) collective-permute-start(bf16[256,256]{0,1:T(8,128)(2,1)S(1)} %copy.343), channel_id=1, source_target_pairs={{28,0},{0,4},{4,8},{8,12},{12,16},{16,20},{20,24},{24,28},{29,1},{... | collective-permute-start | bytes 393224 | tf_op jit(solution)/shard_map/while/body/eval_jaxpr/ppermute | solution.py:20
  337.2 25.3 %collective-permute-start.4 = (bf16[256,256]{0,1:T(8,128)(2,1)S(1)}, bf16[256,256]{0,1:T(8,128)(2,1)}, u32[]{:S(2)}, u32[]{:S(2)}) collective-permute-start(bf16[256,256]{0,1:T(8,128)(2,1)S(1)} %copy.344), channel_id=1, source_target_pairs={{28,0},{0,4},{4,8},{8,12},{12,16},{16,20},{20,24},{24,28},{29,1},{... | collective-permute-start | bytes 393224 | tf_op jit(solution)/shard_map/while/body/eval_jaxpr/ppermute | solution.py:20
  338.3 24.1 %collective-permute-start.5 = (bf16[256]{0:T(256)(128)(2,1)}, bf16[256]{0:T(256)(128)(2,1)}, u32[]{:S(2)}, u32[]{:S(2)}) collective-permute-start(bf16[256]{0:T(256)(128)(2,1)} %copy.345), channel_id=1, source_target_pairs={{28,0},{0,4},{4,8},{8,12},{12,16},{16,20},{20,24},{24,28},{29,1},{... | collective-permute-start | bytes 1544 | tf_op jit(solution)/shard_map/while/body/eval_jaxpr/ppermute | solution.py:20
  362.5 24.6 %collective-permute-start.3 = (bf16[256,256]{0,1:T(8,128)(2,1)S(1)}, bf16[256,256]{0,1:T(8,128)(2,1)S(1)}, u32[]{:S(2)}, u32[]{:S(2)}) collective-permute-start(bf16[256,256]{0,1:T(8,128)(2,1)S(1)} %copy.343), channel_id=1, source_target_pairs={{28,0},{0,4},{4,8},{8,12},{12,16},{16,20},{20,24},{24,28},{29,1},{... | collective-permute-start | bytes 393224 | tf_op jit(solution)/shard_map/while/body/eval_jaxpr/ppermute | solution.py:20
  363.5 23.7 %collective-permute-start.4 = (bf16[256,256]{0,1:T(8,128)(2,1)S(1)}, bf16[256,256]{0,1:T(8,128)(2,1)}, u32[]{:S(2)}, u32[]{:S(2)}) collective-permute-start(bf16[256,256]{0,1:T(8,128)(2,1)S(1)} %copy.344), channel_id=1, source_target_pairs={{28,0},{0,4},{4,8},{8,12},{12,16},{16,20},{20,24},{24,28},{29,1},{... | collective-permute-start | bytes 393224 | tf_op jit(solution)/shard_map/while/body/eval_jaxpr/ppermute | solution.py:20
  364.6 22.5 %collective-permute-start.5 = (bf16[256]{0:T(256)(128)(2,1)}, bf16[256]{0:T(256)(128)(2,1)}, u32[]{:S(2)}, u32[]{:S(2)}) collective-permute-start(bf16[256]{0:T(256)(128)(2,1)} %copy.345), channel_id=1, source_target_pairs={{28,0},{0,4},{4,8},{8,12},{12,16},{16,20},{20,24},{24,28},{29,1},{... | collective-permute-start | bytes 1544 | tf_op jit(solution)/shard_map/while/body/eval_jaxpr/ppermute | solution.py:20
  387.2 26.1 %collective-permute-start.3 = (bf16[256,256]{0,1:T(8,128)(2,1)S(1)}, bf16[256,256]{0,1:T(8,128)(2,1)S(1)}, u32[]{:S(2)}, u32[]{:S(2)}) collective-permute-start(bf16[256,256]{0,1:T(8,128)(2,1)S(1)} %copy.343), channel_id=1, source_target_pairs={{28,0},{0,4},{4,8},{8,12},{12,16},{16,20},{20,24},{24,28},{29,1},{... | collective-permute-start | bytes 393224 | tf_op jit(solution)/shard_map/while/body/eval_jaxpr/ppermute | solution.py:20
  388.1 25.1 %collective-permute-start.4 = (bf16[256,256]{0,1:T(8,128)(2,1)S(1)}, bf16[256,256]{0,1:T(8,128)(2,1)}, u32[]{:S(2)}, u32[]{:S(2)}) collective-permute-start(bf16[256,256]{0,1:T(8,128)(2,1)S(1)} %copy.344), channel_id=1, source_target_pairs={{28,0},{0,4},{4,8},{8,12},{12,16},{16,20},{20,24},{24,28},{29,1},{... | collective-permute-start | bytes 393224 | tf_op jit(solution)/shard_map/while/body/eval_jaxpr/ppermute | solution.py:20
  389.3 24.0 %collective-permute-start.5 = (bf16[256]{0:T(256)(128)(2,1)}, bf16[256]{0:T(256)(128)(2,1)}, u32[]{:S(2)}, u32[]{:S(2)}) collective-permute-start(bf16[256]{0:T(256)(128)(2,1)} %copy.345), channel_id=1, source_target_pairs={{28,0},{0,4},{4,8},{8,12},{12,16},{16,20},{20,24},{24,28},{29,1},{... | collective-permute-start | bytes 1544 | tf_op jit(solution)/shard_map/while/body/eval_jaxpr/ppermute | solution.py:20
  (199 other events, 831.2 us)
Sparse Core Ops, SparseCore 0:
  454.1 160.4 all-reduce.3
where the time goes:
time: 642 us; the launch traced here: 632 us
  waiting for transfers between devices  166 us (26%)
  local copies, waits for them, and re-layouts  126 us (20%)
  matrix products  121 us (19%)
  other arithmetic  87.9 us (14%)
  starting transfers between devices  74.5 us (12%)
  blocking collectives  38.6 us (6%)
  between operations  15.4 us (2%)
    psum x1, waiting for transfers between devices, body(): lax.psum((query_grad, key_grad, value_grad, out_grad, att_grad, msg_grad,...  119 us
    ppermute x64, starting transfers between devices, from_behind(): return lax.ppermute(block, axis, route)  74.5 us
    while x216, local copies, waits for them, and re-layouts  56.6 us
    ppermute x64, waiting for transfers between devices, from_behind(): return lax.ppermute(block, axis, route)  47.1 us
    psum x1, blocking collectives, body(): lax.psum((query_grad, key_grad, value_grad, out_grad, att_grad, msg_grad,...  38.6 us
    unnamed x172, local copies, waits for them, and re-layouts  22.1 us
    convert_element_type x8, other arithmetic, back_turn(): from_behind((travel[1] + v_grad).astype(jnp.bfloat16), 'blk', 1)  13 us
  transfers between devices with their start and end apart: 65, of which 17 were waited for; matrix products, arithmetic and copies ran while one was open for 26% of the time, Pallas kernels for 0%

commit v1 on v0

--- a/solution.py
+++ b/solution.py
@@ -4,6 +4,8 @@
 import jax.numpy as jnp
 import numpy as np
 from jax import lax
+from jax.experimental import pallas as pl
+from jax.experimental.pallas import tpu as pltpu
 from jax.sharding import PartitionSpec as P
 
 LEVELS = 16
@@ -384,6 +386,557 @@
     )
 
 
+REL_TAB = relation_table()
+HALF = 128
+F32 = jnp.float32
+LOW = jnp.bfloat16
+VMEM_CAP = 65000 * 2**10
+
+
+def nn(a, b):
+    return lax.dot_general(a, b, (((1,), (0,)), ((), ())), preferred_element_type=F32)
+
+
+def nt(a, b):
+    return lax.dot_general(a, b, (((1,), (1,)), ((), ())), preferred_element_type=F32)
+
+
+def tn(a, b):
+    return lax.dot_general(a, b, (((0,), (0,)), ((), ())), preferred_element_type=F32)
+
+
+def pick(kinds, kind, value):
+    return jnp.where(kinds == kind, value, jnp.zeros_like(value))
+
+
+def relation_of(kind, slot):
+    hit = np.nonzero(REL_TAB[kind, slot])[0]
+    return int(hit[0]) if len(hit) else None
+
+
+def to_slots(rel_rows, kinds, kind_count):
+    slots = []
+    for slot in range(kind_count):
+        rows = jnp.zeros(kinds.shape, F32)
+        for kind in range(kind_count):
+            rel = relation_of(kind, slot)
+            if rel is not None:
+                rows = jnp.where(kinds == kind, rel_rows(rel), rows)
+        slots.append(rows)
+    return slots, pick(kinds, 0, rel_rows(3))
+
+
+def to_relations(slot_rows, cite_rows, kinds, kind_count, rel_count):
+    out = []
+    for rel in range(rel_count):
+        if rel == 3:
+            out.append(pick(kinds, 0, cite_rows))
+            continue
+        (kind, slot) = [
+            (k, s) for k in range(kind_count) for s in range(kind_count) if relation_of(k, s) == rel
+        ][0]
+        out.append(pick(kinds, kind, slot_rows(slot)))
+    return out
+
+
+def prep_kernel(x_ref, meta_ref, rte_ref, time_ref, shifted_ref, xt_ref):
+    levels = time_ref.shape[1]
+    x_t = x_ref[...].astype(F32).T
+    xt_ref[...] = x_t.astype(LOW)
+    table = tn(rte_ref[...], time_ref[...])
+    table_hi = table.astype(LOW)
+    table_lo = (table - table_hi.astype(F32)).astype(LOW)
+    gaps = jnp.broadcast_to(meta_ref[1:2, :], (levels, x_t.shape[1]))
+    hot = (lax.broadcasted_iota(jnp.int32, gaps.shape, 0) == gaps).astype(F32).astype(LOW)
+    shifted_ref[...] = (x_t + nn(table_hi, hot) + nn(table_lo, hot)).astype(LOW)
+
+
+def layer_kernel(
+    xt_ref,
+    shifted_ref,
+    meta_ref,
+    metas_ref,
+    codes_ref,
+    cot_ref,
+    qw_ref,
+    kw_ref,
+    vw_ref,
+    ow_ref,
+    att_ref,
+    msg_ref,
+    factor_ref,
+    gate_ref,
+    gain_ref,
+    bias_ref,
+    out_ref,
+    base_ref,
+    gsh_ref,
+    qg_ref,
+    kg_ref,
+    vg_ref,
+    og_ref,
+    atta_ref,
+    msga_ref,
+    pack_ref,
+    kt,
+    vx,
+    sbuf,
+    probs,
+    mx,
+    sm,
+    qs,
+    qt2,
+    qh,
+    gs,
+    gt2,
+    acc,
+    urel,
+    dka,
+    dva,
+    two,
+    wkt,
+    wvt,
+    agg,
+):
+    feat, rows = xt_ref.shape
+    n_blk = shifted_ref.shape[0]
+    kind_count = qw_ref.shape[0]
+    heads, size = qh.shape[0], qh.shape[1]
+    rel_count = att_ref.shape[1] // size
+    kinds = jnp.broadcast_to(meta_ref[0:1, :], (size, rows))
+    kinds_f = jnp.broadcast_to(meta_ref[0:1, :], (feat, rows))
+    valid_f = jnp.broadcast_to(meta_ref[2:3, :], (feat, rows)).astype(F32)
+    lane = lax.broadcasted_iota(jnp.int32, (rows, HALF), 1)
+    ones_pad = (lax.broadcasted_iota(jnp.int32, (16, rows), 0) < 2).astype(F32).astype(LOW)
+
+    def cols(j):
+        return pl.ds(pl.multiple_of(j * rows, rows), rows)
+
+    for k in range(kind_count):
+        wkt[pl.ds(k * feat, feat), :] = kw_ref[k].astype(F32).T.astype(LOW)
+        wvt[pl.ds(k * feat, feat), :] = vw_ref[k].astype(F32).T.astype(LOW)
+
+    x_t = xt_ref[...]
+    q_full = jnp.zeros((feat, rows), F32)
+    for k in range(kind_count):
+        q_full = jnp.where(kinds_f == k, tn(qw_ref[k], x_t), q_full)
+    for h in range(heads):
+        qh[h] = q_full[h * size : (h + 1) * size].astype(LOW)
+
+    def query_head(h, carry):
+        raw = nn(att_ref[h], qh[h])
+
+        def rel_rows(r):
+            return (raw[r * size : (r + 1) * size] * factor_ref[r, h]).astype(LOW).astype(F32)
+
+        slots, cite = to_slots(rel_rows, kinds, kind_count)
+        slot_t = jnp.concatenate(slots, axis=0)
+        cite_t = jnp.concatenate([cite, jnp.zeros((HALF - size, rows), F32)], axis=0)
+        qt2[h, :, 0:rows] = slot_t.astype(LOW)
+        qt2[h, :, rows:] = cite_t.astype(LOW)
+        qs[h, 0:rows, :] = slot_t.T.astype(LOW)
+        qs[h, rows:, :] = cite_t.T.astype(LOW)
+        return carry
+
+    lax.fori_loop(0, heads, query_head, 0)
+
+    def expand(j, carry):
+        src = jnp.broadcast_to(metas_ref[j, 0:1, :], (size, rows))
+        block = shifted_ref[j]
+        for k in range(kind_count):
+            key = nn(wkt[pl.ds(k * feat, feat), :], block)
+            value = nn(wvt[pl.ds(k * feat, feat), :], block)
+            for h in range(heads):
+                part = slice(h * size, (h + 1) * size)
+                kt[j, h, pl.ds(k * size, size), :] = pick(src, k, key[part]).astype(LOW)
+                vx[j, h, pl.ds(k * size, size), :] = pick(src, k, value[part]).astype(LOW)
+        for h in range(heads):
+            vx[j, h, pl.ds(HALF, 16), :] = ones_pad
+        two[j] = (codes_ref[:, cols(j)] == 2).astype(F32).astype(LOW)
+        return carry
+
+    lax.fori_loop(0, n_blk, expand, 0)
+
+    def score_block(h, j):
+        both = nn(qs[h], kt[j, h])
+        code = codes_ref[:, cols(j)]
+        val = jnp.where(code == 2, both[rows:], both[:rows])
+        val = jnp.where(code > 0, val, NEG_FILL)
+        sbuf[h % 2, j] = val
+        top = jnp.maximum(val[:, :HALF], val[:, HALF:])
+        for c in range(2 * HALF, rows, HALF):
+            top = jnp.maximum(top, val[:, c : c + HALF])
+        mx[h % 2] = jnp.maximum(mx[h % 2], top)
+
+    def prob_block(h, j):
+        top = sm[h % 2]
+        val = jnp.exp(sbuf[h % 2, j] - jnp.concatenate([top] * (rows // HALF), axis=1))
+        total = val[:, :HALF]
+        for c in range(HALF, rows, HALF):
+            total = total + val[:, c : c + HALF]
+        mx[2 + h % 2] = mx[2 + h % 2] + total
+        low = val.astype(LOW)
+        second = low * two[j]
+        probs[j, h, 0:rows, :] = low - second
+        probs[j, h, rows:, :] = second
+        acc[h] = acc[h] + nt(vx[j, h, 0:HALF, :], probs[j, h])
+
+    def open_head(h):
+        mx[h % 2] = jnp.full((rows, HALF), NEG_FILL, F32)
+
+    def close_scores(h):
+        top = jnp.max(mx[h % 2], axis=1, keepdims=True)
+        sm[h % 2] = jnp.broadcast_to(jnp.maximum(top, 0.1 * NEG_FILL), (rows, HALF))
+        mx[2 + h % 2] = jnp.zeros((rows, HALF), F32)
+        acc[h] = jnp.zeros(acc.shape[1:], F32)
+
+    def close_probs(h):
+        total = jnp.sum(mx[2 + h % 2], axis=1, keepdims=True)
+        sm[2] = jnp.where(lane == h, jnp.broadcast_to(total, (rows, HALF)), sm[2])
+
+    sm[2] = jnp.zeros((rows, HALF), F32)
+    open_head(0)
+
+    def first(j, carry):
+        score_block(0, j)
+        return carry
+
+    lax.fori_loop(0, n_blk, first, 0)
+
+    def forward_head(h, carry):
+        close_scores(h)
+        open_head(h + 1)
+
+        def step(j, carry):
+            score_block(h + 1, j)
+            prob_block(h, j)
+            return carry
+
+        lax.fori_loop(0, n_blk, step, 0)
+        close_probs(h)
+        return carry
+
+    lax.fori_loop(0, heads - 1, forward_head, 0)
+    close_scores(heads - 1)
+
+    def last(j, carry):
+        prob_block(heads - 1, j)
+        return carry
+
+    lax.fori_loop(0, n_blk, last, 0)
+    close_probs(heads - 1)
+
+    denom = jnp.maximum(sm[2].T, 1.0)
+    inverse = 1.0 / denom
+    sm[2, 0:HALF, :] = inverse[:, 0:HALF]
+    sm[2, HALF : 2 * HALF, :] = inverse[:, HALF : 2 * HALF]
+
+    def inv_row(h, count):
+        row = jnp.concatenate([sm[2, pl.ds(h, 1), :], sm[2, pl.ds(HALF + h, 1), :]], axis=1)
+        return jnp.broadcast_to(row, (count, rows))
+
+    for h in range(heads):
+        inv = inv_row(h, HALF)
+        u_slot = acc[h, :, 0:rows] * inv
+        u_cite = acc[h, 0:size, rows:] * inv[0:size]
+        acc[h, :, 0:rows] = u_slot
+        acc[h, 0:size, rows:] = u_cite
+        rel = to_relations(
+            lambda s: u_slot[s * size : (s + 1) * size], u_cite, kinds, kind_count, rel_count
+        )
+        urel[h] = jnp.concatenate(rel, axis=0).astype(LOW)
+        agg[pl.ds(h * size, size), :] = tn(msg_ref[h], urel[h])
+    agg_t = agg[...]
+    slope = 0.7978845608028654
+    inner = jnp.tanh(slope * (agg_t + 0.044715 * agg_t * agg_t * agg_t))
+    act_t = (0.5 * agg_t * (1.0 + inner)).astype(LOW)
+    gelu_back = 0.5 * (1.0 + inner) + 0.5 * agg_t * (1.0 - inner * inner) * slope * (
+        1.0 + 3.0 * 0.044715 * agg_t * agg_t
+    )
+    x_f = x_t.astype(F32)
+    gate = jnp.zeros((feat, rows), F32)
+    branch = jnp.zeros((feat, rows), F32)
+    for k in range(kind_count):
+        gate = jnp.where(kinds_f == k, gate_ref[k], gate)
+        branch = jnp.where(kinds_f == k, tn(ow_ref[k], act_t), branch)
+    mixed = gate * branch + (1.0 - gate) * x_f
+    centered = mixed - jnp.mean(mixed, axis=0, keepdims=True)
+    inv_std = lax.rsqrt(jnp.mean(centered * centered, axis=0, keepdims=True) + LN_EPS)
+    normed = centered * inv_std
+    gain = gain_ref[...]
+    out_t = valid_f * (normed * gain + bias_ref[...])
+    out_ref[...] = out_t.T.astype(LOW)
+    grad_y = cot_ref[...].astype(F32).T * valid_f
+    gain_col = jnp.sum(grad_y * normed, axis=1, keepdims=True)
+    bias_col = jnp.sum(grad_y, axis=1, keepdims=True)
+    grad_norm = grad_y * gain
+    grad_mix = inv_std * (
+        grad_norm
+        - jnp.mean(grad_norm, axis=0, keepdims=True)
+        - normed * jnp.mean(grad_norm * normed, axis=0, keepdims=True)
+    )
+    gate_row = gate[0:1]
+    skip_row = (
+        jnp.sum(grad_mix * (branch - x_f), axis=0, keepdims=True) * gate_row * (1.0 - gate_row)
+    )
+    base_ref[...] = (1.0 - gate) * grad_mix
+    grad_branch = (gate * grad_mix).astype(LOW)
+    grad_act = jnp.zeros((feat, rows), F32)
+    for k in range(kind_count):
+        masked = pick(kinds_f, k, grad_branch.astype(F32)).astype(LOW)
+        og_ref[k] = nt(act_t, masked)
+        grad_act = grad_act + nn(ow_ref[k], masked)
+    agg[...] = gelu_back * grad_act
+
+    def grad_head(h, carry):
+        grad_agg = agg[pl.ds(pl.multiple_of(h * size, size), size), :].astype(LOW)
+        msga_ref[pl.ds(pl.multiple_of(h * size, size), size), :] = nt(grad_agg, urel[h])
+        inv = inv_row(h, size)
+        grad_u = nn(msg_ref[h], grad_agg)
+
+        def rel_rows(r):
+            return grad_u[r * size : (r + 1) * size] * inv
+
+        slots, cite = to_slots(rel_rows, kinds, kind_count)
+        slot_t = jnp.concatenate(slots, axis=0).astype(LOW)
+        cite_t = jnp.concatenate([cite, jnp.zeros((HALF - size, rows), F32)], axis=0).astype(LOW)
+        gt2[h, :, 0:rows] = slot_t
+        gt2[h, :, rows:] = cite_t
+        slot_f = slot_t.astype(F32)
+        cite_f = cite_t.astype(F32)
+        delta = -(
+            jnp.sum(slot_f * acc[h, :, 0:rows], axis=0, keepdims=True)
+            + jnp.sum(cite_f[0:size] * acc[h, 0:size, rows:], axis=0, keepdims=True)
+        )
+        delta_hi = delta.astype(LOW).astype(F32)
+        tail = jnp.concatenate(
+            [delta_hi, delta - delta_hi, jnp.zeros((HALF - 2, rows), F32)], axis=0
+        )
+        tail_t = tail.T.astype(LOW)
+        gs[h, 0:rows, 0:HALF] = slot_f.T.astype(LOW)
+        gs[h, rows:, 0:HALF] = cite_f.T.astype(LOW)
+        gs[h, 0:rows, HALF:] = tail_t[:, 0:16]
+        gs[h, rows:, HALF:] = tail_t[:, 0:16]
+        acc[h] = jnp.zeros(acc.shape[1:], F32)
+        return carry
+
+    lax.fori_loop(0, heads, grad_head, 0)
+
+    slot_id = lax.broadcasted_iota(jnp.int32, (HALF, rows), 0) // size
+
+    def back_block(j, carry):
+        src = jnp.broadcast_to(metas_ref[j, 0:1, :], (HALF, rows))
+        own = slot_id == src
+
+        def back_head(h, carry):
+            pair = probs[j, h]
+            grad = pair * nn(gs[h], vx[j, h]).astype(LOW)
+            d_key = jnp.where(own, nn(qt2[h], grad), 0.0).astype(LOW)
+            d_value = jnp.where(own, nn(gt2[h], pair), 0.0).astype(LOW)
+            for k in range(kind_count):
+                at = pl.ds(pl.multiple_of(k * feat + h * size, size), size)
+                dka[at, cols(j)] = d_key[k * size : (k + 1) * size]
+                dva[at, cols(j)] = d_value[k * size : (k + 1) * size]
+            acc[h] = acc[h] + nt(kt[j, h], grad)
+            return carry
+
+        lax.fori_loop(0, heads, back_head, 0)
+        return carry
+
+    lax.fori_loop(0, n_blk, back_block, 0)
+
+    level_count = 16
+    table = jnp.zeros((feat, level_count), F32)
+    for k in range(kind_count):
+        at = pl.ds(k * feat, feat)
+        k_sum = jnp.zeros((feat, feat), F32)
+        v_sum = jnp.zeros((feat, feat), F32)
+        for j in range(n_blk):
+            k_sum = k_sum + nt(shifted_ref[j], dka[at, pl.ds(j * rows, rows)])
+            v_sum = v_sum + nt(shifted_ref[j], dva[at, pl.ds(j * rows, rows)])
+        kg_ref[k] = k_sum
+        vg_ref[k] = v_sum
+    pack_ref[...] = jnp.zeros_like(pack_ref)
+
+    def shift_block(j, carry):
+        total = jnp.zeros((feat, rows), F32)
+        for k in range(kind_count):
+            at = pl.ds(k * feat, feat)
+            total = total + nn(kw_ref[k], dka[at, cols(j)]) + nn(vw_ref[k], dva[at, cols(j)])
+        low = total.astype(LOW)
+        gsh_ref[j] = low
+        gaps = jnp.broadcast_to(metas_ref[j, 1:2, :], (level_count, rows))
+        hot = (lax.broadcasted_iota(jnp.int32, gaps.shape, 0) == gaps).astype(F32).astype(LOW)
+        pack_ref[:, 0:level_count] = pack_ref[:, 0:level_count] + nt(low, hot)
+        return carry
+
+    lax.fori_loop(0, n_blk, shift_block, 0)
+    wide = lax.broadcasted_iota(jnp.int32, (feat, HALF), 1)
+    row_at = lax.broadcasted_iota(jnp.int32, (feat, HALF), 0)
+    pack = pack_ref[...]
+    pack = jnp.where(wide == level_count, jnp.broadcast_to(gain_col, (feat, HALF)), pack)
+    pack = jnp.where(wide == level_count + 1, jnp.broadcast_to(bias_col, (feat, HALF)), pack)
+    for k in range(kind_count):
+        mine = jnp.sum(pick(kinds[0:1], k, skip_row), axis=1, keepdims=True)
+        pack = jnp.where(
+            (wide == level_count + 2) & (row_at == k), jnp.broadcast_to(mine, (feat, HALF)), pack
+        )
+    pack_ref[...] = pack
+
+    def query_back(h, carry):
+        slot = acc[h, :, 0:rows]
+        rel = to_relations(
+            lambda s: slot[s * size : (s + 1) * size],
+            acc[h, 0:size, rows:],
+            kinds,
+            kind_count,
+            rel_count,
+        )
+        rel = [part.astype(LOW) for part in rel]
+        at = pl.ds(pl.multiple_of(h * size, size), size)
+        atta_ref[at, :] = nt(qh[h], jnp.concatenate(rel, axis=0))
+        raw = [(part.astype(F32) * factor_ref[r, h]).astype(LOW) for r, part in enumerate(rel)]
+        agg[at, :] = tn(att_ref[h], jnp.concatenate(raw, axis=0))
+        return carry
+
+    lax.fori_loop(0, heads, query_back, 0)
+    grad_q = agg[...].astype(LOW).astype(F32)
+    base = base_ref[...]
+    for k in range(kind_count):
+        masked = pick(kinds_f, k, grad_q).astype(LOW)
+        qg_ref[k] = nt(x_t, masked)
+        base = base + nn(qw_ref[k], masked)
+    base_ref[...] = base
+
+
+def fast_body(
+    features,
+    node_type,
+    time_gap,
+    node_valid,
+    edge_codes,
+    query_w,
+    key_w,
+    value_w,
+    out_w,
+    rel_att,
+    rel_msg,
+    rel_prior,
+    skip_logit,
+    rte_w,
+    ln_gain,
+    ln_bias,
+    cotangent,
+):
+    rows, feat = features.shape
+    n_blk = lax.axis_size("blk")
+    kind_count = query_w.shape[0]
+    rel_count, heads, size = rel_att.shape[:3]
+    time_low = time_table(LEVELS, feat).astype(LOW)
+    meta = jnp.concatenate(
+        [node_type[None], time_gap[None], node_valid[None], jnp.zeros((5, rows), jnp.int32)], axis=0
+    )
+    vmem = pl.BlockSpec(memory_space=pltpu.VMEM)
+    smem = pl.BlockSpec(memory_space=pltpu.SMEM)
+    shifted, x_t = pl.pallas_call(
+        prep_kernel,
+        out_shape=[jax.ShapeDtypeStruct((feat, rows), LOW)] * 2,
+        in_specs=[vmem] * 4,
+        out_specs=[vmem] * 2,
+        name="prep",
+    )(features, meta, rte_w, time_low.T)
+    shifted_all = lax.all_gather(shifted, "blk")
+    meta_all = lax.all_gather(meta, "blk")
+    att_rows = rel_att.transpose(1, 0, 3, 2).reshape(heads, rel_count * size, size)
+    msg_rows = rel_msg.transpose(1, 0, 2, 3).reshape(heads, rel_count * size, size)
+    factor = rel_prior / math.sqrt(size)
+    gate = jax.nn.sigmoid(skip_logit)
+
+    def shape(dims, kind):
+        return jax.ShapeDtypeStruct(dims, kind)
+
+    square = (feat, feat)
+    outs = pl.pallas_call(
+        layer_kernel,
+        out_shape=[
+            shape((rows, feat), LOW),
+            shape((feat, rows), F32),
+            shape((n_blk, feat, rows), LOW),
+        ]
+        + [shape((kind_count,) + square, F32)] * 4
+        + [shape(square, F32)] * 2
+        + [shape((feat, HALF), F32)],
+        in_specs=[vmem] * 12 + [smem] * 2 + [vmem] * 2,
+        out_specs=[vmem] * 10,
+        scratch_shapes=[
+            pltpu.VMEM((n_blk, heads, HALF, rows), LOW),
+            pltpu.VMEM((n_blk, heads, HALF + 16, rows), LOW),
+            pltpu.VMEM((2, n_blk, rows, rows), F32),
+            pltpu.VMEM((n_blk, heads, 2 * rows, rows), LOW),
+            pltpu.VMEM((4, rows, HALF), F32),
+            pltpu.VMEM((3, rows, HALF), F32),
+            pltpu.VMEM((heads, 2 * rows, HALF), LOW),
+            pltpu.VMEM((heads, HALF, 2 * rows), LOW),
+            pltpu.VMEM((heads, size, rows), LOW),
+            pltpu.VMEM((heads, 2 * rows, HALF + 16), LOW),
+            pltpu.VMEM((heads, HALF, 2 * rows), LOW),
+            pltpu.VMEM((heads, HALF, 2 * rows), F32),
+            pltpu.VMEM((heads, rel_count * size, rows), LOW),
+            pltpu.VMEM((kind_count * feat, n_blk * rows), LOW),
+            pltpu.VMEM((kind_count * feat, n_blk * rows), LOW),
+            pltpu.VMEM((n_blk, rows, rows), LOW),
+            pltpu.VMEM((kind_count * feat, feat), LOW),
+            pltpu.VMEM((kind_count * feat, feat), LOW),
+            pltpu.VMEM(square, F32),
+        ],
+        compiler_params=pltpu.CompilerParams(vmem_limit_bytes=VMEM_CAP),
+        name="layer",
+    )(
+        x_t,
+        shifted_all,
+        meta,
+        meta_all,
+        edge_codes,
+        cotangent,
+        query_w,
+        key_w,
+        value_w,
+        out_w,
+        att_rows,
+        msg_rows,
+        factor,
+        gate,
+        ln_gain[:, None],
+        ln_bias[:, None],
+    )
+    layer_out, base, gsh, qg, kg, vg, og, att_a, msg_a, pack = outs
+    own = lax.psum_scatter(gsh.astype(F32), "blk", scatter_dimension=0)
+    input_grad = (base + own).T.astype(LOW)
+    qg, kg, vg, og, att_a, msg_a, pack = lax.psum(
+        (qg, kg, vg, og, att_a, msg_a, pack), ("blk", "rep")
+    )
+    att_grad = att_a.reshape(heads, size, rel_count, size).transpose(2, 0, 1, 3)
+    prior_grad = jnp.sum(att_grad * rel_att.astype(F32), axis=(2, 3)) / math.sqrt(size)
+    att_grad = att_grad * factor[:, :, None, None]
+    msg_grad = msg_a.reshape(heads, size, rel_count, size).transpose(2, 0, 3, 1)
+    rte_grad = jnp.dot(time_low.astype(F32).T, pack[:, :LEVELS].T, precision=HIGH)
+    return (
+        layer_out,
+        input_grad,
+        qg,
+        kg,
+        vg,
+        og,
+        att_grad,
+        msg_grad,
+        prior_grad,
+        pack[:kind_count, LEVELS + 2],
+        rte_grad,
+        pack[:, LEVELS],
+        pack[:, LEVELS + 1],
+    )
+
+
 def solution(mesh):
     in_specs = (
         P(("blk", "rep"), None),
@@ -419,4 +972,5 @@
         P(),
         P(),
     )
-    return jax.shard_map(body, mesh=mesh, in_specs=in_specs, out_specs=out_specs, check_vma=False)
+    plan = fast_body if mesh.shape["blk"] <= 8 else body
+    return jax.shard_map(plan, mesh=mesh, in_specs=in_specs, out_specs=out_specs, check_vma=False)

time: 642 us -> 404 us (0.63); the launches traced: 632 us -> 404 us
  matrix products: 121 us -> 0.99 us
  local copies, waits for them, and re-layouts: 126 us -> 20.6 us
  Pallas kernels: 0 us -> 102 us
  other arithmetic: 87.9 us -> 8.19 us
  starting transfers between devices: 74.5 us -> 0.12 us
  waiting for transfers between devices: 166 us -> 224 us
    dot_general x139 -> x1, matrix products: 121 us -> 0.99 us  [fast_body(): jnp.dot(time_low.astype(F32).T, pack[:, :LEVELS].T, precision=HIGH)]
    pallas_call x0 -> x2, Pallas kernels: none -> 102 us  [the longest x1 99.9 us: fast_body(): pl.pallas_call(layer_kernel, out_shape=[shape((rows, feat), LOW), shape((...]
    ppermute x64 -> x0, starting transfers between devices: 74.5 us -> none  [from_behind(): return lax.ppermute(block, axis, route)]
    reduce_scatter x0 -> x1, waiting for transfers between devices: none -> 64 us  [fast_body(): own = lax.psum_scatter(gsh.astype(F32), 'blk', scatter_dimension=0)]
    while x216 -> x0, local copies, waits for them, and re-layouts: 56.6 us -> none
    convert_element_type x71 -> x2, other arithmetic: 52.7 us -> 2.5 us  [the longest x1 1.53 us: fast_body(): own = lax.psum_scatter(gsh.astype(F32), 'blk', scatter_dimension=0)]
    ppermute x64 -> x0, waiting for transfers between devices: 47.1 us -> none  [from_behind(): return lax.ppermute(block, axis, route)]
    psum x1 -> x0, blocking collectives: 38.6 us -> none  [body(): lax.psum((query_grad, key_grad, value_grad, out_grad, att_grad, msg_grad,...]
  transfers between devices with their start and end apart: 65 -> 3, of which waited for: 17 -> 3; matrix products, arithmetic and copies ran while one was open for 26% -> 4% of each run, Pallas kernels for 0% -> 0%
where the time goes in v1:
time: 404 us
  waiting for transfers between devices  224 us (55%)
  Pallas kernels  102 us (25%)
  blocking collectives  34.3 us (8%)
  local copies, waits for them, and re-layouts  20.6 us (5%)
  between operations  13.9 us (3%)
  other arithmetic  8.19 us (2%)
    psum x1, waiting for transfers between devices, fast_body(): lax.psum((qg, kg, vg, og, att_a, msg_a, pack), ('blk', 'rep'))  157 us
    pallas_call x1, Pallas kernels, fast_body(): pl.pallas_call(layer_kernel, out_shape=[shape((rows, feat), LOW), shape((...  99.9 us
    reduce_scatter x1, waiting for transfers between devices, fast_body(): own = lax.psum_scatter(gsh.astype(F32), 'blk', scatter_dimension=0)  64 us
    all_gather x1, blocking collectives, fast_body(): meta_all = lax.all_gather(meta, 'blk')  34.3 us
  transfers between devices with their start and end apart: 3, of which 3 were waited for; matrix products, arithmetic and copies ran while one was open for 4% of the time, Pallas kernels for 0%

profile of v1, /device:TPU:0, one launch (start us, length us, event | category | flops | bytes accessed | tf_op | source)
XLA Modules:
  0.0 403.6 jit_solution(13094249810378899784)
XLA Ops:
  8.2 1.4 add_add_fusion.meta_ref
  9.6 2.1 prep.1
  11.7 2.0 copy.43
  13.8 1.9 copy.44
  17.3 34.3 %all-gather.1 = s32[64,256]{1,0:T(8,128)} all-gather(s32[8,256]{1,0:T(8,128)S(1)} %copy-done.11), channel_id=3, replica_groups=mesh['blk'=8,'rep'=4] {'blk'}, dimensions={0}, use_global_device_ids=true | all-gather | bytes 73728 | tf_op jit(solution)/shard_map/all_gather | solution.py:849
  52.7 2.1 all-gather.4.cloned.1.call-done
  54.8 99.9 %layer.1 = (bf16[256,256]{1,0:T(8,128)(2,1)}, f32[256,256]{1,0:T(8,128)}, bf16[8,256,256]{2,1,0:T(8,128)(2,1)}, f32[4,256,256]{2,1,0:T(8,128)}, f32[4,256,256]{2...) custom-call(bf16[256,256]{1,0:T(8,128)(2,1)} %get-tuple-element.25.x, ...), custom_call_target="tpu_custom_call" | custom-call | tf_op jit(solution)/shard_map/layer/pallas_call | solution.py:859
  154.7 1.3 reshape.109
  156.0 1.2 copy.51
  157.4 1.5 copy.48
  159.0 1.1 copy-done.2
  160.1 1.5 convert_element_type.18
  161.7 157.4 %all-reduce.3.cloned.1.call-done = (f32[4,256,256]{2,1,0:T(8,128)}, f32[4,256,256]{2,1,0:T(8,128)}, f32[4,256,256]{2,1,0:T(8,128)}, f32[4,256,256]{2,1,0:T(8,128...) async-done(((f32[4,256,256]{2,1,0:T(8,128)}, f32[4,256,256]{2,1,0:T(8,128)}, f32[4,256,256]{2,1,0:T(8,128)}, f32[4,256,256]{2,1,0:T(8,128)}, ...) | async-done | bytes 4849680 | tf_op jit(solution)/shard_map/psum | solution.py:915
  319.0 1.4 slice_reduce_fusion.2
  320.5 1.9 slice_reduce_fusion
  322.4 2.5 multiply_reduce_fusion
  325.5 1.0 fusion.2
  326.5 64.0 %reduce-scatter.2.cloned.1.call-done = f32[1,256,256]{2,1,0:T(8,128)} async-done(((f32[8,256,256]{2,1,0:T(8,128)}), f32[1,256,256]{2,1,0:T(8,128)}) %reduce-scatter.2.cloned.1.call-update) | async-done | bytes 262160 | tf_op jit(solution)/shard_map/reduce_scatter | solution.py:913
  390.5 1.0 fusion.1
  392.2 1.0 copy.59
  393.2 1.0 copy.60
  394.2 1.0 copy.61
  395.2 1.0 copy.62
  396.1 1.0 copy.63
  (52 shorter events, 5.4 us)
Async XLA Ops:
  7.2 8.5 %copy-start.14 = (f32[256]{0:T(256)S(1)}, f32[256]{0:T(256)}, u32[]{:S(2)}) copy-start(f32[256]{0:T(256)} %param.31) | copy-start | bytes 3076
  7.2 9.3 %copy-start.15 = (f32[256]{0:T(256)S(1)}, f32[256]{0:T(256)}, u32[]{:S(2)}) copy-start(f32[256]{0:T(256)} %param.32) | copy-start | bytes 3076
  7.2 44.4 %copy-start.16 = (f32[4]{0:T(128)S(1)}, f32[4]{0:T(128)}, u32[]{:S(2)}) copy-start(f32[4]{0:T(128)} %param.29) | copy-start | bytes 52
  7.2 44.9 %copy-start.13 = (f32[8,8]{1,0:T(8,128)S(1)}, f32[8,8]{1,0:T(8,128)}, u32[]{:S(2)}) copy-start(f32[8,8]{1,0:T(8,128)} %param.28) | copy-start | bytes 772
  7.2 47.6 %all-gather.4.cloned.1.call-start = ((), (), s32[]{:S(2)}) async-start(), calls=%async_computation.2 | async-start | bytes 1179648 | tf_op jit(solution)/shard_map/all_gather | solution.py:848
  9.6 7.7 %copy-start.11 = (s32[8,256]{1,0:T(8,128)S(1)}, s32[8,256]{1,0:T(8,128)}, u32[]{:S(2)}) copy-start(s32[8,256]{1,0:T(8,128)} %add_add_fusion.meta_ref) | copy-start | bytes 24580
  11.7 307.4 %all-reduce.3.cloned.1.call-start = ((), (), s32[]{:S(2)}) async-start(), calls=%async_computation.3 | async-start | bytes 12845056 | tf_op jit(solution)/shard_map/psum | solution.py:915
  154.7 2.4 copy-start.9
  158.9 1.2 copy-start.2
  158.9 231.6 %reduce-scatter.2.cloned.1.call-start = ((), (), s32[]{:S(2)}) async-start(), calls=%async_computation.1 | async-start | bytes 2359296 | tf_op jit(solution)/shard_map/reduce_scatter | solution.py:913
  160.1 162.3 %copy-start = (bf16[8,8,32,32]{3,2,1,0:T(8,128)(2,1)S(1)}, bf16[8,8,32,32]{3,2,1,0:T(8,128)(2,1)}, u32[]{:S(2)}) copy-start(bf16[8,8,32,32]{3,2,1,0:T(8,128)(2,1)} %param.26) | copy-start | bytes 393220
  160.1 162.3 %copy-start.12 = (f32[8,8]{1,0:T(8,128)S(1)}, f32[8,8]{1,0:T(8,128)}, u32[]{:S(2)}) copy-start(f32[8,8]{1,0:T(8,128)} %broadcast_multiply_fusion.2.factor_ref) | copy-start | bytes 772
  161.6 163.8 %copy-start.8 = (bf16[16,128,2]{0,2,1:T(2,128)(2,1)S(1)}, bf16[16,128,2]{0,2,1:T(2,128)(2,1)}, u32[]{:S(2)}) copy-start(bf16[16,128,2]{0,2,1:T(2,128)(2,1)} %copy.42) | copy-start | bytes 24580
  161.7 228.8 %copy-start.10 = (f32[256,256]{1,0:T(8,128)S(1)}, f32[256,256]{1,0:T(8,128)}, u32[]{:S(2)}) copy-start(f32[256,256]{1,0:T(8,128)} %get-tuple-element.28) | copy-start | bytes 786436
  319.0 6.4 %copy-start.1 = (f32[256,128]{1,0:T(8,128)S(1)}, f32[256,128]{1,0:T(8,128)}, u32[]{:S(2)}) copy-start(f32[256,128]{1,0:T(8,128)} %get-tuple-element.84) | copy-start | bytes 393220
  320.5 71.7 %copy-start.7 = (f32[4,256,256]{2,1,0:T(8,128)S(1)}, f32[4,256,256]{2,1,0:T(8,128)}, u32[]{:S(2)}) copy-start(f32[4,256,256]{2,1,0:T(8,128)} %get-tuple-element.91) | copy-start | bytes 3145732
  324.9 68.3 %copy-start.6 = (f32[4,256,256]{2,1,0:T(8,128)S(1)}, f32[4,256,256]{2,1,0:T(8,128)}, u32[]{:S(2)}) copy-start(f32[4,256,256]{2,1,0:T(8,128)} %get-tuple-element.92) | copy-start | bytes 3145732
  392.2 1.9 copy-start.5
  393.2 1.9 copy-start.4
  394.2 1.9 copy-start.3
Sparse Core Ops, SparseCore 0:
  11.8 43.0 all-gather.3
  159.0 159.9 all-reduce.2
  322.6 67.8 reduce-scatter.1

commit v2 on v1

--- a/solution.py
+++ b/solution.py
@@ -439,23 +439,40 @@
     return out
 
 
-def prep_kernel(x_ref, meta_ref, rte_ref, time_ref, shifted_ref, xt_ref):
-    levels = time_ref.shape[1]
-    x_t = x_ref[...].astype(F32).T
-    xt_ref[...] = x_t.astype(LOW)
-    table = tn(rte_ref[...], time_ref[...])
-    table_hi = table.astype(LOW)
-    table_lo = (table - table_hi.astype(F32)).astype(LOW)
-    gaps = jnp.broadcast_to(meta_ref[1:2, :], (levels, x_t.shape[1]))
-    hot = (lax.broadcasted_iota(jnp.int32, gaps.shape, 0) == gaps).astype(F32).astype(LOW)
-    shifted_ref[...] = (x_t + nn(table_hi, hot) + nn(table_lo, hot)).astype(LOW)
+def flip(index, mask):
+    return sum(((index // bit + mask // bit) % 2) * bit for bit in (1, 2, 4))
+
+
+def gap_hot(gap_row, levels):
+    gaps = jnp.broadcast_to(gap_row, (levels, gap_row.shape[1]))
+    return (lax.broadcasted_iota(jnp.int32, gaps.shape, 0) == gaps).astype(F32).astype(LOW)
+
+
+def remote(src, dst, sends, recvs, send_at, recv_at, device):
+    return pltpu.make_async_remote_copy(
+        src_ref=src,
+        dst_ref=dst,
+        send_sem=sends.at[send_at],
+        recv_sem=recvs.at[recv_at],
+        device_id=device,
+        device_id_type=pl.DeviceIdType.MESH,
+    )
+
+
+def greet(devices):
+    barrier = pltpu.get_barrier_semaphore()
+    for device in devices:
+        pl.semaphore_signal(
+            barrier, inc=1, device_id=device, device_id_type=pl.DeviceIdType.MESH
+        )
+    pl.semaphore_wait(barrier, len(devices))
 
 
 def layer_kernel(
-    xt_ref,
-    shifted_ref,
+    x_ref,
     meta_ref,
-    metas_ref,
+    rte_ref,
+    time_ref,
     codes_ref,
     cot_ref,
     qw_ref,
@@ -469,15 +486,18 @@
     gain_ref,
     bias_ref,
     out_ref,
-    base_ref,
-    gsh_ref,
-    qg_ref,
-    kg_ref,
-    vg_ref,
-    og_ref,
-    atta_ref,
-    msga_ref,
+    input_ref,
+    grads_ref,
     pack_ref,
+    shifted,
+    xt,
+    base,
+    shift_out,
+    shift_in,
+    gather_send,
+    gather_recv,
+    back_send,
+    back_recv,
     kt,
     vx,
     sbuf,
@@ -487,7 +507,6 @@
     qs,
     qt2,
     qh,
-    gs,
     gt2,
     acc,
     urel,
@@ -498,11 +517,43 @@
     wvt,
     agg,
 ):
-    feat, rows = xt_ref.shape
-    n_blk = shifted_ref.shape[0]
+    rows, feat = x_ref.shape
+    n_blk = shifted.shape[0]
+    levels = time_ref.shape[1]
+    me = lax.axis_index("blk")
+    rep = lax.axis_index("rep")
+    greet([(flip(me, mask), rep) for mask in range(1, n_blk)])
+    x_f = x_ref[...].astype(F32).T
+    x_t = x_f.astype(LOW)
+    xt[...] = x_t
+    table = tn(rte_ref[...], time_ref[...])
+    table_hi = table.astype(LOW)
+    table_lo = (table - table_hi.astype(F32)).astype(LOW)
+    hot = gap_hot(meta_ref[1:2, :], levels)
+    shifted[me, 0:feat, :] = (x_f + nn(table_hi, hot) + nn(table_lo, hot)).astype(LOW)
+    shifted[me, feat:, :] = jnp.concatenate(
+        [meta_ref[...].astype(F32), jnp.zeros((8, rows), F32)], axis=0
+    ).astype(LOW)
+
+    def hand_on(block, mask, send_at):
+        return remote(
+            shifted.at[block],
+            shifted.at[block],
+            gather_send,
+            gather_recv,
+            send_at,
+            block,
+            (flip(me, mask), rep),
+        )
+
+    for mask in (1, 2, 6, 4):
+        hand_on(me, mask, mask).start()
+
+    def source_row(j, row):
+        return shifted[j, feat : feat + 16, :].astype(F32)[row : row + 1].astype(jnp.int32)
     kind_count = qw_ref.shape[0]
     heads, size = qh.shape[0], qh.shape[1]
-    rel_count = att_ref.shape[1] // size
+    rel_count = att_ref.shape[2] // size
     kinds = jnp.broadcast_to(meta_ref[0:1, :], (size, rows))
     kinds_f = jnp.broadcast_to(meta_ref[0:1, :], (feat, rows))
     valid_f = jnp.broadcast_to(meta_ref[2:3, :], (feat, rows)).astype(F32)
@@ -512,11 +563,22 @@
     def cols(j):
         return pl.ds(pl.multiple_of(j * rows, rows), rows)
 
+    def store_grad(at, value):
+        for part in range(feat // HALF):
+            start = (at * (feat // HALF) + part) * feat
+            grads_ref[pl.ds(start, feat), :] = value[:, part * HALF : (part + 1) * HALF].astype(LOW)
+
+    def store_rows(at, h, value):
+        for part in range(feat // HALF):
+            start = (at * (feat // HALF) + part) * feat + h * size
+            grads_ref[pl.ds(pl.multiple_of(start, size), size), :] = value[
+                :, part * HALF : (part + 1) * HALF
+            ].astype(LOW)
+
     for k in range(kind_count):
         wkt[pl.ds(k * feat, feat), :] = kw_ref[k].astype(F32).T.astype(LOW)
         wvt[pl.ds(k * feat, feat), :] = vw_ref[k].astype(F32).T.astype(LOW)
 
-    x_t = xt_ref[...]
     q_full = jnp.zeros((feat, rows), F32)
     for k in range(kind_count):
         q_full = jnp.where(kinds_f == k, tn(qw_ref[k], x_t), q_full)
@@ -524,7 +586,7 @@
         qh[h] = q_full[h * size : (h + 1) * size].astype(LOW)
 
     def query_head(h, carry):
-        raw = nn(att_ref[h], qh[h])
+        raw = tn(att_ref[h], qh[h])
 
         def rel_rows(r):
             return (raw[r * size : (r + 1) * size] * factor_ref[r, h]).astype(LOW).astype(F32)
@@ -534,15 +596,25 @@
         cite_t = jnp.concatenate([cite, jnp.zeros((HALF - size, rows), F32)], axis=0)
         qt2[h, :, 0:rows] = slot_t.astype(LOW)
         qt2[h, :, rows:] = cite_t.astype(LOW)
-        qs[h, 0:rows, :] = slot_t.T.astype(LOW)
-        qs[h, rows:, :] = cite_t.T.astype(LOW)
+        qs[h, 0:rows, 0:HALF] = slot_t.T.astype(LOW)
+        qs[h, rows:, 0:HALF] = cite_t.T.astype(LOW)
         return carry
 
     lax.fori_loop(0, heads, query_head, 0)
 
-    def expand(j, carry):
-        src = jnp.broadcast_to(metas_ref[j, 0:1, :], (size, rows))
-        block = shifted_ref[j]
+    def expand(i, carry):
+        j = flip(me, i)
+
+        @pl.when(i > 0)
+        def _():
+            hand_on(j, 1, 0).wait_recv()
+
+        @pl.when((i > 0) & (i % 2 == 0))
+        def _():
+            hand_on(j, 1, i + 1).start()
+
+        src = jnp.broadcast_to(source_row(j, 0), (size, rows))
+        block = shifted[j, 0:feat, :]
         for k in range(kind_count):
             key = nn(wkt[pl.ds(k * feat, feat), :], block)
             value = nn(wvt[pl.ds(k * feat, feat), :], block)
@@ -556,9 +628,11 @@
         return carry
 
     lax.fori_loop(0, n_blk, expand, 0)
+    for send_at in range(1, n_blk):
+        hand_on(me, 1, send_at).wait_send()
 
     def score_block(h, j):
-        both = nn(qs[h], kt[j, h])
+        both = nn(qs[h, :, 0:HALF], kt[j, h])
         code = codes_ref[:, cols(j)]
         val = jnp.where(code == 2, both[rows:], both[:rows])
         val = jnp.where(code > 0, val, NEG_FILL)
@@ -645,7 +719,7 @@
             lambda s: u_slot[s * size : (s + 1) * size], u_cite, kinds, kind_count, rel_count
         )
         urel[h] = jnp.concatenate(rel, axis=0).astype(LOW)
-        agg[pl.ds(h * size, size), :] = tn(msg_ref[h], urel[h])
+        agg[pl.ds(h * size, size), :] = nn(msg_ref[h], urel[h])
     agg_t = agg[...]
     slope = 0.7978845608028654
     inner = jnp.tanh(slope * (agg_t + 0.044715 * agg_t * agg_t * agg_t))
@@ -653,7 +727,6 @@
     gelu_back = 0.5 * (1.0 + inner) + 0.5 * agg_t * (1.0 - inner * inner) * slope * (
         1.0 + 3.0 * 0.044715 * agg_t * agg_t
     )
-    x_f = x_t.astype(F32)
     gate = jnp.zeros((feat, rows), F32)
     branch = jnp.zeros((feat, rows), F32)
     for k in range(kind_count):
@@ -679,20 +752,20 @@
     skip_row = (
         jnp.sum(grad_mix * (branch - x_f), axis=0, keepdims=True) * gate_row * (1.0 - gate_row)
     )
-    base_ref[...] = (1.0 - gate) * grad_mix
+    base[...] = (1.0 - gate) * grad_mix
     grad_branch = (gate * grad_mix).astype(LOW)
     grad_act = jnp.zeros((feat, rows), F32)
     for k in range(kind_count):
         masked = pick(kinds_f, k, grad_branch.astype(F32)).astype(LOW)
-        og_ref[k] = nt(act_t, masked)
+        store_grad(3 * kind_count + k, nt(act_t, masked))
         grad_act = grad_act + nn(ow_ref[k], masked)
     agg[...] = gelu_back * grad_act
 
     def grad_head(h, carry):
         grad_agg = agg[pl.ds(pl.multiple_of(h * size, size), size), :].astype(LOW)
-        msga_ref[pl.ds(pl.multiple_of(h * size, size), size), :] = nt(grad_agg, urel[h])
+        store_rows(4 * kind_count + 1, h, nt(grad_agg, urel[h]))
         inv = inv_row(h, size)
-        grad_u = nn(msg_ref[h], grad_agg)
+        grad_u = tn(msg_ref[h], grad_agg)
 
         def rel_rows(r):
             return grad_u[r * size : (r + 1) * size] * inv
@@ -713,10 +786,10 @@
             [delta_hi, delta - delta_hi, jnp.zeros((HALF - 2, rows), F32)], axis=0
         )
         tail_t = tail.T.astype(LOW)
-        gs[h, 0:rows, 0:HALF] = slot_f.T.astype(LOW)
-        gs[h, rows:, 0:HALF] = cite_f.T.astype(LOW)
-        gs[h, 0:rows, HALF:] = tail_t[:, 0:16]
-        gs[h, rows:, HALF:] = tail_t[:, 0:16]
+        qs[h, 0:rows, 0:HALF] = slot_f.T.astype(LOW)
+        qs[h, rows:, 0:HALF] = cite_f.T.astype(LOW)
+        qs[h, 0:rows, HALF:] = tail_t[:, 0:16]
+        qs[h, rows:, HALF:] = tail_t[:, 0:16]
         acc[h] = jnp.zeros(acc.shape[1:], F32)
         return carry
 
@@ -724,13 +797,21 @@
 
     slot_id = lax.broadcasted_iota(jnp.int32, (HALF, rows), 0) // size
 
-    def back_block(j, carry):
-        src = jnp.broadcast_to(metas_ref[j, 0:1, :], (HALF, rows))
+    pack_ref[...] = jnp.zeros_like(pack_ref)
+
+    def send_back(j):
+        return remote(
+            shift_out.at[j], shift_in.at[me], back_send, back_recv, j, me, (j, rep)
+        )
+
+    def back_block(i, carry):
+        j = flip(me, n_blk - 1 - i)
+        src = jnp.broadcast_to(source_row(j, 0), (HALF, rows))
         own = slot_id == src
 
         def back_head(h, carry):
             pair = probs[j, h]
-            grad = pair * nn(gs[h], vx[j, h]).astype(LOW)
+            grad = pair * nn(qs[h], vx[j, h]).astype(LOW)
             d_key = jnp.where(own, nn(qt2[h], grad), 0.0).astype(LOW)
             d_value = jnp.where(own, nn(gt2[h], pair), 0.0).astype(LOW)
             for k in range(kind_count):
@@ -741,47 +822,45 @@
             return carry
 
         lax.fori_loop(0, heads, back_head, 0)
+        total = jnp.zeros((feat, rows), F32)
+        for k in range(kind_count):
+            at = pl.ds(k * feat, feat)
+            total = total + nn(kw_ref[k], dka[at, cols(j)]) + nn(vw_ref[k], dva[at, cols(j)])
+        low = total.astype(LOW)
+        shift_out[j] = low
+
+        @pl.when(i < n_blk - 1)
+        def _():
+            send_back(j).start()
+
+        pack_ref[0:levels, :] = pack_ref[0:levels, :] + nt(gap_hot(source_row(j, 1), levels), low)
         return carry
 
     lax.fori_loop(0, n_blk, back_block, 0)
 
-    level_count = 16
-    table = jnp.zeros((feat, level_count), F32)
     for k in range(kind_count):
         at = pl.ds(k * feat, feat)
         k_sum = jnp.zeros((feat, feat), F32)
         v_sum = jnp.zeros((feat, feat), F32)
         for j in range(n_blk):
-            k_sum = k_sum + nt(shifted_ref[j], dka[at, pl.ds(j * rows, rows)])
-            v_sum = v_sum + nt(shifted_ref[j], dva[at, pl.ds(j * rows, rows)])
-        kg_ref[k] = k_sum
-        vg_ref[k] = v_sum
-    pack_ref[...] = jnp.zeros_like(pack_ref)
-
-    def shift_block(j, carry):
-        total = jnp.zeros((feat, rows), F32)
-        for k in range(kind_count):
-            at = pl.ds(k * feat, feat)
-            total = total + nn(kw_ref[k], dka[at, cols(j)]) + nn(vw_ref[k], dva[at, cols(j)])
-        low = total.astype(LOW)
-        gsh_ref[j] = low
-        gaps = jnp.broadcast_to(metas_ref[j, 1:2, :], (level_count, rows))
-        hot = (lax.broadcasted_iota(jnp.int32, gaps.shape, 0) == gaps).astype(F32).astype(LOW)
-        pack_ref[:, 0:level_count] = pack_ref[:, 0:level_count] + nt(low, hot)
-        return carry
-
-    lax.fori_loop(0, n_blk, shift_block, 0)
-    wide = lax.broadcasted_iota(jnp.int32, (feat, HALF), 1)
-    row_at = lax.broadcasted_iota(jnp.int32, (feat, HALF), 0)
-    pack = pack_ref[...]
-    pack = jnp.where(wide == level_count, jnp.broadcast_to(gain_col, (feat, HALF)), pack)
-    pack = jnp.where(wide == level_count + 1, jnp.broadcast_to(bias_col, (feat, HALF)), pack)
+            k_sum = k_sum + nt(shifted[j, 0:feat, :], dka[at, pl.ds(j * rows, rows)])
+            v_sum = v_sum + nt(shifted[j, 0:feat, :], dva[at, pl.ds(j * rows, rows)])
+        store_grad(kind_count + k, k_sum)
+        store_grad(2 * kind_count + k, v_sum)
+    pair = jnp.where(
+        lane == 0,
+        jnp.broadcast_to(gain_col, (feat, HALF)),
+        jnp.where(lane == 1, jnp.broadcast_to(bias_col, (feat, HALF)), 0.0),
+    ).T
+    spot = lax.broadcasted_iota(jnp.int32, (1, rows), 1)
+    skips = jnp.zeros((1, rows), F32)
     for k in range(kind_count):
-        mine = jnp.sum(pick(kinds[0:1], k, skip_row), axis=1, keepdims=True)
-        pack = jnp.where(
-            (wide == level_count + 2) & (row_at == k), jnp.broadcast_to(mine, (feat, HALF)), pack
-        )
-    pack_ref[...] = pack
+        skips = jnp.where(
+            spot == k, jnp.sum(pick(kinds[0:1], k, skip_row), axis=1, keepdims=True), skips
+        )
+    pack_ref[levels : levels + 8, :] = jnp.concatenate(
+        [pair[0:2], skips, jnp.zeros((5, rows), F32)], axis=0
+    )
 
     def query_back(h, carry):
         slot = acc[h, :, 0:rows]
@@ -794,19 +873,203 @@
         )
         rel = [part.astype(LOW) for part in rel]
         at = pl.ds(pl.multiple_of(h * size, size), size)
-        atta_ref[at, :] = nt(qh[h], jnp.concatenate(rel, axis=0))
+        store_rows(4 * kind_count, h, nt(qh[h], jnp.concatenate(rel, axis=0)))
         raw = [(part.astype(F32) * factor_ref[r, h]).astype(LOW) for r, part in enumerate(rel)]
-        agg[at, :] = tn(att_ref[h], jnp.concatenate(raw, axis=0))
+        agg[at, :] = nn(att_ref[h], jnp.concatenate(raw, axis=0))
         return carry
 
     lax.fori_loop(0, heads, query_back, 0)
     grad_q = agg[...].astype(LOW).astype(F32)
-    base = base_ref[...]
+    total = base[...] + shift_out[me].astype(F32)
     for k in range(kind_count):
         masked = pick(kinds_f, k, grad_q).astype(LOW)
-        qg_ref[k] = nt(x_t, masked)
-        base = base + nn(qw_ref[k], masked)
-    base_ref[...] = base
+        store_grad(k, nt(x_t, masked))
+        total = total + nn(qw_ref[k], masked)
+    for mask in range(1, n_blk):
+        j = flip(me, mask)
+        send_back(j).wait_send()
+        remote(shift_in.at[j], shift_in.at[j], back_send, back_recv, j, j, (j, rep)).wait_recv()
+        total = total + shift_in[j].astype(F32)
+    input_ref[...] = total.T.astype(LOW)
+
+
+def reduce_kernel(
+    grads_ref,
+    pack_ref,
+    att_ref,
+    time_ref,
+    factor_ref,
+    qg_ref,
+    kg_ref,
+    vg_ref,
+    og_ref,
+    attg_ref,
+    msgg_ref,
+    prior_ref,
+    rte_ref,
+    small_ref,
+    work,
+    full,
+    core_in,
+    plane_in,
+    line_in,
+    pack_in,
+    pack_work,
+    sends,
+    recvs,
+):
+    me = lax.axis_index("blk")
+    rep = lax.axis_index("rep")
+    z, y, x, core = me // 2, me % 2, rep // 2, rep % 2
+    by_core = (me, rep + 1 - 2 * core)
+    by_x = (me, rep + 2 - 4 * x)
+    by_y = (me + 1 - 2 * y, rep)
+    by_z = [(((z + step) % 4) * 2 + y, rep) for step in (1, 2, 3)]
+    greet([by_core, by_x, by_y] + by_z)
+    total = grads_ref.shape[0]
+    half, quarter = total // 2, total // 4
+    count = iter(range(sends.shape[0]))
+
+    def send(src, dst, device):
+        at = next(count)
+        copy = remote(src, dst, sends, recvs, at, at, device)
+        copy.start()
+        return copy
+
+    def rows_of(ref, start, size):
+        return ref.at[pl.ds(pl.multiple_of(start, 16), size), :]
+
+    def load(ref, start, size):
+        return ref[pl.ds(pl.multiple_of(start, 16), size), :].astype(F32)
+
+    def add_in(start, size, *parts):
+        value = load(work, start, size)
+        for part in parts:
+            value = value + part
+        work[pl.ds(pl.multiple_of(start, 16), size), :] = value.astype(LOW)
+
+    mine = core * half
+    a = send(rows_of(grads_ref, half - mine, half), core_in, by_core)
+    b = send(pack_ref, pack_in.at[0], by_core)
+    a.wait()
+    b.wait()
+    work[...] = (load(grads_ref, mine, half) + core_in[...].astype(F32)).astype(LOW)
+    pack_work[0] = pack_ref[...] + pack_in[0]
+    size = quarter // 2
+    starts = [x * size, quarter + y * size]
+    away = [size - x * size, quarter + size - y * size]
+    copies = [
+        send(rows_of(work, away[0], size), plane_in.at[0], by_x),
+        send(rows_of(work, away[1], size), plane_in.at[1], by_y),
+        send(pack_work.at[0], pack_in.at[1], by_x),
+    ]
+    for copy in copies:
+        copy.wait()
+    for s in range(2):
+        add_in(starts[s], size, plane_in[s].astype(F32))
+    pack_work[1] = pack_work[0] + pack_in[1]
+    size = size // 2
+    turn = [y, x]
+    copies = [
+        send(
+            rows_of(work, starts[s] + size - turn[s] * size, size),
+            plane_in.at[2 + s, pl.ds(0, size), :],
+            (by_y, by_x)[s],
+        )
+        for s in range(2)
+    ]
+    copies.append(send(pack_work.at[1], pack_in.at[2], by_y))
+    for copy in copies:
+        copy.wait()
+    starts = [starts[s] + turn[s] * size for s in range(2)]
+    for s in range(2):
+        add_in(starts[s], size, plane_in[2 + s, 0:size, :].astype(F32))
+    pack_work[2] = pack_work[1] + pack_in[2]
+    size = size // 4
+    copies = []
+    for step in (2, 3, 1):
+        for s in range(2):
+            there = starts[s] + ((z + step) % 4) * size
+            copies.append(
+                send(rows_of(work, there, size), line_in.at[s, step - 1], by_z[step - 1])
+            )
+        copies.append(send(pack_work.at[2], pack_in.at[2 + step], by_z[step - 1]))
+    for copy in copies:
+        copy.wait()
+    small = pack_work[2] + pack_in[3] + pack_in[4] + pack_in[5]
+    starts = [starts[s] + z * size for s in range(2)]
+    for s in range(2):
+        value = load(work, starts[s], size)
+        for step in range(3):
+            value = value + line_in[s, step].astype(F32)
+        full[pl.ds(pl.multiple_of(mine + starts[s], 16), size), :] = value.astype(LOW)
+
+    def share(start, size, device):
+        return send(rows_of(full, start, size), rows_of(full, start, size), device)
+
+    copies = [
+        share(mine + starts[s], size, by_z[step - 1]) for step in (2, 3, 1) for s in range(2)
+    ]
+    for copy in copies:
+        copy.wait()
+    starts = [starts[s] - z * size for s in range(2)]
+    size = size * 4
+    copies = [share(mine + starts[s], size, (by_y, by_x)[s]) for s in range(2)]
+    for copy in copies:
+        copy.wait()
+    starts = [starts[s] - turn[s] * size for s in range(2)]
+    size = size * 2
+    copies = [share(mine + starts[s], size, (by_x, by_y)[s]) for s in range(2)]
+    early = [share(mine + starts[s], size, by_core) for s in range(2)]
+    for copy in copies:
+        copy.wait()
+    late = [share(mine + away[s], size, by_core) for s in range(2)]
+    for copy in early + late:
+        copy.wait()
+
+    kind_count, feat = qg_ref.shape[:2]
+    rel_count, heads, width = attg_ref.shape[:3]
+    parts = feat // HALF
+
+    def whole(at):
+        return jnp.concatenate(
+            [full[pl.ds((at * parts + p) * feat, feat), :].astype(F32) for p in range(parts)],
+            axis=1,
+        )
+
+    for m, ref in enumerate((qg_ref, kg_ref, vg_ref, og_ref)):
+        for k in range(kind_count):
+            ref[k] = whole(m * kind_count + k)
+    att = whole(4 * kind_count)
+    msg = whole(4 * kind_count + 1).T
+    for r in range(rel_count):
+        for h in range(heads):
+            block = (slice(h * width, (h + 1) * width), slice(r * width, (r + 1) * width))
+            attg_ref[r, h] = att[block] * factor_ref[r, h]
+            msgg_ref[r, h] = msg[block[::-1]]
+    prod = (att * att_ref[...].astype(F32)).reshape(heads, width, feat)
+    prod = jnp.sum(prod, axis=1)
+    spread = (
+        lax.broadcasted_iota(jnp.int32, (feat, rel_count), 0) // width
+        == lax.broadcasted_iota(jnp.int32, (feat, rel_count), 1)
+    ).astype(F32).astype(LOW)
+    prior = jnp.zeros((rel_count, heads), F32)
+    for _ in range(3):
+        low = prod.astype(LOW)
+        prior = prior + lax.dot_general(
+            spread, low, (((0,), (1,)), ((), ())), preferred_element_type=F32
+        )
+        prod = prod - low.astype(F32)
+    prior_ref[...] = prior * (1.0 / math.sqrt(width))
+    levels = time_ref.shape[1]
+    rte = jnp.zeros(rte_ref.shape, F32)
+    rest = small[0:levels]
+    for _ in range(3):
+        low = rest.astype(LOW)
+        rte = rte + nn(time_ref[...], low)
+        rest = rest - low.astype(F32)
+    rte_ref[...] = rte
+    small_ref[...] = small[levels:]
 
 
 def fast_body(
@@ -838,47 +1101,45 @@
     )
     vmem = pl.BlockSpec(memory_space=pltpu.VMEM)
     smem = pl.BlockSpec(memory_space=pltpu.SMEM)
-    shifted, x_t = pl.pallas_call(
-        prep_kernel,
-        out_shape=[jax.ShapeDtypeStruct((feat, rows), LOW)] * 2,
-        in_specs=[vmem] * 4,
-        out_specs=[vmem] * 2,
-        name="prep",
-    )(features, meta, rte_w, time_low.T)
-    shifted_all = lax.all_gather(shifted, "blk")
-    meta_all = lax.all_gather(meta, "blk")
-    att_rows = rel_att.transpose(1, 0, 3, 2).reshape(heads, rel_count * size, size)
-    msg_rows = rel_msg.transpose(1, 0, 2, 3).reshape(heads, rel_count * size, size)
+    att_flat = rel_att.transpose(1, 2, 0, 3).reshape(feat, rel_count * size)
+    msg_flat = rel_msg.transpose(1, 3, 0, 2).reshape(feat, rel_count * size)
     factor = rel_prior / math.sqrt(size)
     gate = jax.nn.sigmoid(skip_logit)
+    square = (feat, feat)
+    grad_rows = (4 * kind_count + 2) * (feat // HALF) * feat
 
     def shape(dims, kind):
         return jax.ShapeDtypeStruct(dims, kind)
 
-    square = (feat, feat)
-    outs = pl.pallas_call(
+    layer_out, input_grad, grads, pack = pl.pallas_call(
         layer_kernel,
         out_shape=[
             shape((rows, feat), LOW),
-            shape((feat, rows), F32),
-            shape((n_blk, feat, rows), LOW),
-        ]
-        + [shape((kind_count,) + square, F32)] * 4
-        + [shape(square, F32)] * 2
-        + [shape((feat, HALF), F32)],
+            shape((rows, feat), LOW),
+            shape((grad_rows, HALF), LOW),
+            shape((LEVELS + 8, feat), F32),
+        ],
         in_specs=[vmem] * 12 + [smem] * 2 + [vmem] * 2,
-        out_specs=[vmem] * 10,
+        out_specs=[vmem] * 4,
         scratch_shapes=[
+            pltpu.VMEM((n_blk, feat + 16, rows), LOW),
+            pltpu.VMEM((feat, rows), LOW),
+            pltpu.VMEM((feat, rows), F32),
+            pltpu.VMEM((n_blk, feat, rows), LOW),
+            pltpu.VMEM((n_blk, feat, rows), LOW),
+            pltpu.SemaphoreType.DMA((n_blk,)),
+            pltpu.SemaphoreType.DMA((n_blk,)),
+            pltpu.SemaphoreType.DMA((n_blk,)),
+            pltpu.SemaphoreType.DMA((n_blk,)),
             pltpu.VMEM((n_blk, heads, HALF, rows), LOW),
             pltpu.VMEM((n_blk, heads, HALF + 16, rows), LOW),
             pltpu.VMEM((2, n_blk, rows, rows), F32),
             pltpu.VMEM((n_blk, heads, 2 * rows, rows), LOW),
             pltpu.VMEM((4, rows, HALF), F32),
             pltpu.VMEM((3, rows, HALF), F32),
-            pltpu.VMEM((heads, 2 * rows, HALF), LOW),
+            pltpu.VMEM((heads, 2 * rows, HALF + 16), LOW),
             pltpu.VMEM((heads, HALF, 2 * rows), LOW),
             pltpu.VMEM((heads, size, rows), LOW),
-            pltpu.VMEM((heads, 2 * rows, HALF + 16), LOW),
             pltpu.VMEM((heads, HALF, 2 * rows), LOW),
             pltpu.VMEM((heads, HALF, 2 * rows), F32),
             pltpu.VMEM((heads, rel_count * size, rows), LOW),
@@ -889,51 +1150,61 @@
             pltpu.VMEM((kind_count * feat, feat), LOW),
             pltpu.VMEM(square, F32),
         ],
-        compiler_params=pltpu.CompilerParams(vmem_limit_bytes=VMEM_CAP),
+        compiler_params=pltpu.CompilerParams(
+            vmem_limit_bytes=VMEM_CAP, collective_id=0, has_side_effects=True
+        ),
         name="layer",
     )(
-        x_t,
-        shifted_all,
+        features,
         meta,
-        meta_all,
+        rte_w,
+        time_low.T,
         edge_codes,
         cotangent,
         query_w,
         key_w,
         value_w,
         out_w,
-        att_rows,
-        msg_rows,
+        att_flat.reshape(heads, size, rel_count * size),
+        msg_flat.reshape(heads, size, rel_count * size),
         factor,
         gate,
         ln_gain[:, None],
         ln_bias[:, None],
     )
-    layer_out, base, gsh, qg, kg, vg, og, att_a, msg_a, pack = outs
-    own = lax.psum_scatter(gsh.astype(F32), "blk", scatter_dimension=0)
-    input_grad = (base + own).T.astype(LOW)
-    qg, kg, vg, og, att_a, msg_a, pack = lax.psum(
-        (qg, kg, vg, og, att_a, msg_a, pack), ("blk", "rep")
-    )
-    att_grad = att_a.reshape(heads, size, rel_count, size).transpose(2, 0, 1, 3)
-    prior_grad = jnp.sum(att_grad * rel_att.astype(F32), axis=(2, 3)) / math.sqrt(size)
-    att_grad = att_grad * factor[:, :, None, None]
-    msg_grad = msg_a.reshape(heads, size, rel_count, size).transpose(2, 0, 3, 1)
-    rte_grad = jnp.dot(time_low.astype(F32).T, pack[:, :LEVELS].T, precision=HIGH)
+    quarter = grad_rows // 4
+    outs = pl.pallas_call(
+        reduce_kernel,
+        out_shape=[shape((kind_count,) + square, F32)] * 4
+        + [shape(rel_att.shape, F32)] * 2
+        + [shape(rel_prior.shape, F32), shape(square, F32), shape((8, feat), F32)],
+        in_specs=[vmem] * 4 + [smem],
+        out_specs=[vmem] * 9,
+        scratch_shapes=[
+            pltpu.VMEM((grad_rows // 2, HALF), LOW),
+            pltpu.VMEM((grad_rows, HALF), LOW),
+            pltpu.VMEM((grad_rows // 2, HALF), LOW),
+            pltpu.VMEM((4, quarter // 2, HALF), LOW),
+            pltpu.VMEM((2, 3, quarter // 16, HALF), LOW),
+            pltpu.VMEM((6, LEVELS + 8, feat), F32),
+            pltpu.VMEM((3, LEVELS + 8, feat), F32),
+            pltpu.SemaphoreType.DMA((40,)),
+            pltpu.SemaphoreType.DMA((40,)),
+        ],
+        compiler_params=pltpu.CompilerParams(
+            vmem_limit_bytes=VMEM_CAP, collective_id=1, has_side_effects=True
+        ),
+        name="reduce",
+    )(grads, pack, att_flat, time_low.T, factor)
+    small = outs[8]
     return (
         layer_out,
         input_grad,
-        qg,
-        kg,
-        vg,
-        og,
-        att_grad,
-        msg_grad,
-        prior_grad,
-        pack[:kind_count, LEVELS + 2],
-        rte_grad,
-        pack[:, LEVELS],
-        pack[:, LEVELS + 1],
+        *outs[:7],
+        small[2, :kind_count],
+        outs[7],
+        small[0],
+        small[1],
     )
 
 
@@ -972,5 +1243,5 @@
         P(),
         P(),
     )
-    plan = fast_body if mesh.shape["blk"] <= 8 else body
+    plan = fast_body if tuple(mesh.shape.values()) == (8, 4) else body
     return jax.shard_map(plan, mesh=mesh, in_specs=in_specs, out_specs=out_specs, check_vma=False)

time: 404 us -> 202 us (0.50)
  waiting for transfers between devices: 224 us -> 0 us
  Pallas kernels: 102 us -> 176 us
  blocking collectives: 34.3 us -> 0 us
  between operations: 13.9 us -> 0.73 us
  other arithmetic: 8.19 us -> 3.97 us
    psum x1 -> x0, waiting for transfers between devices: 157 us -> none  [fast_body(): lax.psum((qg, kg, vg, og, att_a, msg_a, pack), ('blk', 'rep'))]
    reduce_scatter x1 -> x0, waiting for transfers between devices: 64 us -> none  [fast_body(): own = lax.psum_scatter(gsh.astype(F32), 'blk', scatter_dimension=0)]
    pallas_call x1, Pallas kernels: 2.08 us -> 54.1 us  [fast_body(): pl.pallas_call(reduce_kernel, out_shape=[shape((kind_count,) + square, F3...]
    all_gather x1 -> x0, blocking collectives: 34.3 us -> none  [fast_body(): meta_all = lax.all_gather(meta, 'blk')]
    pallas_call x1, Pallas kernels: 99.9 us -> 122 us  [fast_body(): pl.pallas_call(layer_kernel, out_shape=[shape((rows, feat), LOW), shape((...]
    unnamed x40 -> x30, local copies, waits for them, and re-layouts: 6.82 us -> 9.78 us
  transfers between devices with their start and end apart: 3 -> 0, of which waited for: 3 -> 0; matrix products, arithmetic and copies ran while one was open for 4% -> 0% of each run, Pallas kernels for 0% -> 0%
where the time goes in v2:
time: 202 us; the launch traced here: 201 us
  Pallas kernels  176 us (87%)
  local copies, waits for them, and re-layouts  21 us (10%)
  other arithmetic  3.97 us (2%)
    pallas_call x1, Pallas kernels, fast_body(): pl.pallas_call(layer_kernel, out_shape=[shape((rows, feat), LOW), shape((...  122 us
    pallas_call x1, Pallas kernels, fast_body(): pl.pallas_call(reduce_kernel, out_shape=[shape((kind_count,) + square, F3...  54.1 us
    unnamed x30, local copies, waits for them, and re-layouts  9.78 us

profile of v2, /device:TPU:0, one launch (start us, length us, event | category | flops | bytes accessed | tf_op | source)
XLA Modules:
  0.0 201.4 jit_solution(628970845265240195)
XLA Ops:
  0.7 1.2 add_divide_fusion.gate_ref
  2.0 1.3 broadcast_multiply_fusion.factor_ref
  3.3 1.4 add_add_fusion.meta_ref
  4.7 0.8 copy.38
  5.5 1.5 copy.41.gain_ref
  6.9 1.5 copy.42.bias_ref
  8.4 1.4 copy.39
  9.8 1.0 reshape.97.att_ref
  10.8 1.0 reshape_reshape.6.att_ref
  12.2 1.0 reshape_reshape.7.msg_ref
  13.2 121.6 %layer.1 = (bf16[256,256]{1,0:T(8,128)(2,1)}, bf16[256,256]{1,0:T(8,128)(2,1)}, bf16[9216,128]{1,0:T(8,128)(2,1)}, f32[24,256]{1,0:T(8,128)}) custom-call(bf16[256,256]{1,0:T(8,128)(2,1)} %x_ref.1, s32[8,256]{1,0:T(8,128)} %add_add_fusion.meta_ref, bf16[256,256]{1,0:T(8,128)(2,1)} %rte_ref.1, bf16[256,16]{1,0:T(8,128)(2,1)} %bitcast.20, ...), custom_call_target="tpu_custom_call" | custom-call | tf_op jit(solution)/shard_map/layer/pallas_call | solution.py:1114
  134.9 54.1 %reduce.1 = (f32[4,256,256]{2,1,0:T(8,128)}, f32[4,256,256]{2,1,0:T(8,128)}, f32[4,256,256]{2,1,0:T(8,128)}, f32[4,256,256]{2,1,0:T(8,128)}, f32[8,8,32,32]{3,2,...) custom-call(bf16[9216,128]{1,0:T(8,128)(2,1)} %get-tuple-element.28.grads_ref, ...), custom_call_target="tpu_custom_call" | custom-call | tf_op jit(solution)/shard_map/reduce/pallas_call | solution.py:1176
  189.0 1.3 slice_bitcast_fusion
  190.3 1.3 fusion
  191.6 0.7 copy.54
  192.3 0.7 copy.55
  192.9 2.3 %copy.56 = f32[4,256,256]{2,1,0:T(8,128)} copy(f32[4,256,256]{2,1,0:T(8,128)} %get-tuple-element.58) | data formatting | bytes 2097152
  195.2 1.0 copy.57
  196.2 1.0 copy.58
  197.2 1.0 copy.59
  198.1 1.0 copy.60
  199.1 1.0 copy.61
  200.1 0.6 copy.62
  200.7 0.7 copy.63
  (26 shorter events, 0.5 us)
Async XLA Ops:
  0.6 11.2 %copy-start.5 = (bf16[8,8,32,32]{3,2,1,0:T(8,128)(2,1)S(1)}, bf16[8,8,32,32]{3,2,1,0:T(8,128)(2,1)}, u32[]{:S(2)}) copy-start(bf16[8,8,32,32]{3,2,1,0:T(8,128)(2,1)} %param.27) | copy-start | bytes 393220
  134.8 56.8 %copy-start.8 = (bf16[256,256]{1,0:T(8,128)(2,1)S(1)}, bf16[256,256]{1,0:T(8,128)(2,1)}, u32[]{:S(2)}) copy-start(bf16[256,256]{1,0:T(8,128)(2,1)} %get-tuple-element.56) | copy-start | bytes 393220
  134.8 57.4 %copy-start.7 = (bf16[256,256]{1,0:T(8,128)(2,1)S(1)}, bf16[256,256]{1,0:T(8,128)(2,1)}, u32[]{:S(2)}) copy-start(bf16[256,256]{1,0:T(8,128)(2,1)} %get-tuple-element.57) | copy-start | bytes 393220
  189.0 6.2 %copy-start.4 = (f32[4,256,256]{2,1,0:T(8,128)S(1)}, f32[4,256,256]{2,1,0:T(8,128)}, u32[]{:S(2)}) copy-start(f32[4,256,256]{2,1,0:T(8,128)} %get-tuple-element.59) | copy-start | bytes 3145732
  191.6 4.6 %copy-start.3 = (f32[4,256,256]{2,1,0:T(8,128)S(1)}, f32[4,256,256]{2,1,0:T(8,128)}, u32[]{:S(2)}) copy-start(f32[4,256,256]{2,1,0:T(8,128)} %get-tuple-element.60) | copy-start | bytes 3145732
  195.2 1.9 copy-start.2
  196.2 1.9 copy-start.1
  197.2 2.0 copy-start
  198.1 1.9 copy-start.9
  198.1 2.5 %copy-start.6 = (f32[256,256]{1,0:T(8,128)S(1)}, f32[256,256]{1,0:T(8,128)}, u32[]{:S(2)}) copy-start(f32[256,256]{1,0:T(8,128)} %get-tuple-element.66) | copy-start | bytes 786436

commit v3 on v2

--- a/solution.py
+++ b/solution.py
@@ -470,30 +470,40 @@
 
 def layer_kernel(
     x_ref,
-    meta_ref,
+    kind_ref,
+    gap_ref,
+    valid_ref,
     rte_ref,
     time_ref,
-    codes_ref,
+    codes_hbm,
     cot_ref,
-    qw_ref,
-    kw_ref,
-    vw_ref,
-    ow_ref,
+    qw_hbm,
+    kw_hbm,
+    vw_hbm,
+    ow_hbm,
     att_ref,
     msg_ref,
-    factor_ref,
-    gate_ref,
+    prior_ref,
+    skip_ref,
     gain_ref,
     bias_ref,
     out_ref,
     input_ref,
     grads_ref,
     pack_ref,
+    att_flat,
+    codes,
+    qw,
+    kw,
+    vw,
+    ow,
+    msg_flat,
     shifted,
     xt,
     base,
     shift_out,
     shift_in,
+    load_sem,
     gather_send,
     gather_recv,
     back_send,
@@ -509,30 +519,40 @@
     qh,
     gt2,
     acc,
-    urel,
-    dka,
-    dva,
     two,
-    wkt,
-    wvt,
     agg,
+    flat,
+    grad_even,
+    grad_odd,
 ):
     rows, feat = x_ref.shape
     n_blk = shifted.shape[0]
     levels = time_ref.shape[1]
+    kind_count = qw.shape[0]
+    rel_count, heads, size = att_ref.shape[:3]
+    group = heads // 2
     me = lax.axis_index("blk")
     rep = lax.axis_index("rep")
+    loads = [
+        pltpu.make_async_copy(src, dst, load_sem.at[at])
+        for at, (src, dst) in enumerate(
+            ((kw_hbm, kw), (vw_hbm, vw), (qw_hbm, qw), (codes_hbm, codes), (ow_hbm, ow))
+        )
+    ]
+    for load in loads:
+        load.start()
     greet([(flip(me, mask), rep) for mask in range(1, n_blk)])
+
     x_f = x_ref[...].astype(F32).T
     x_t = x_f.astype(LOW)
     xt[...] = x_t
     table = tn(rte_ref[...], time_ref[...])
     table_hi = table.astype(LOW)
     table_lo = (table - table_hi.astype(F32)).astype(LOW)
-    hot = gap_hot(meta_ref[1:2, :], levels)
+    hot = gap_hot(gap_ref[...], levels)
     shifted[me, 0:feat, :] = (x_f + nn(table_hi, hot) + nn(table_lo, hot)).astype(LOW)
     shifted[me, feat:, :] = jnp.concatenate(
-        [meta_ref[...].astype(F32), jnp.zeros((8, rows), F32)], axis=0
+        [kind_ref[...].astype(F32), gap_ref[...].astype(F32), jnp.zeros((14, rows), F32)], axis=0
     ).astype(LOW)
 
     def hand_on(block, mask, send_at):
@@ -551,45 +571,53 @@
 
     def source_row(j, row):
         return shifted[j, feat : feat + 16, :].astype(F32)[row : row + 1].astype(jnp.int32)
-    kind_count = qw_ref.shape[0]
-    heads, size = qh.shape[0], qh.shape[1]
-    rel_count = att_ref.shape[2] // size
-    kinds = jnp.broadcast_to(meta_ref[0:1, :], (size, rows))
-    kinds_f = jnp.broadcast_to(meta_ref[0:1, :], (feat, rows))
-    valid_f = jnp.broadcast_to(meta_ref[2:3, :], (feat, rows)).astype(F32)
+
+    kinds = jnp.broadcast_to(kind_ref[...], (size, rows))
+    kinds_f = jnp.broadcast_to(kind_ref[...], (feat, rows))
+    valid_f = jnp.broadcast_to(valid_ref[...], (feat, rows)).astype(F32)
     lane = lax.broadcasted_iota(jnp.int32, (rows, HALF), 1)
     ones_pad = (lax.broadcasted_iota(jnp.int32, (16, rows), 0) < 2).astype(F32).astype(LOW)
+    scale = 1.0 / math.sqrt(size)
 
     def cols(j):
         return pl.ds(pl.multiple_of(j * rows, rows), rows)
 
-    def store_grad(at, value):
-        for part in range(feat // HALF):
-            start = (at * (feat // HALF) + part) * feat
-            grads_ref[pl.ds(start, feat), :] = value[:, part * HALF : (part + 1) * HALF].astype(LOW)
-
-    def store_rows(at, h, value):
-        for part in range(feat // HALF):
-            start = (at * (feat // HALF) + part) * feat + h * size
-            grads_ref[pl.ds(pl.multiple_of(start, size), size), :] = value[
-                :, part * HALF : (part + 1) * HALF
-            ].astype(LOW)
-
-    for k in range(kind_count):
-        wkt[pl.ds(k * feat, feat), :] = kw_ref[k].astype(F32).T.astype(LOW)
-        wvt[pl.ds(k * feat, feat), :] = vw_ref[k].astype(F32).T.astype(LOW)
-
+    def store_part(start, value):
+        grads_ref[pl.ds(start, value.shape[0]), :] = value.astype(LOW)
+
+    for r in range(rel_count):
+        for h in range(heads):
+            flat[h * size : (h + 1) * size, r * size : (r + 1) * size] = att_ref[r, h].astype(F32)
+    att_flat[...] = flat[...].astype(LOW)
+    for r in range(rel_count):
+        for h in range(heads):
+            flat[r * size : (r + 1) * size, h * size : (h + 1) * size] = msg_ref[r, h].astype(F32)
+    msg_flat[...] = flat[...].T.astype(LOW)
+
+    def turned(m, k):
+        return probs.at[0, 2 * m + k // 2, pl.ds((k % 2) * feat, feat), :]
+
+    for m, (load, ref) in enumerate(((loads[0], kw), (loads[1], vw))):
+        load.wait()
+        for k in range(kind_count):
+            turned(m, k)[...] = ref[k].astype(F32).T.astype(LOW)
+
+    loads[2].wait()
     q_full = jnp.zeros((feat, rows), F32)
     for k in range(kind_count):
-        q_full = jnp.where(kinds_f == k, tn(qw_ref[k], x_t), q_full)
+        q_full = jnp.where(kinds_f == k, tn(qw[k], x_t), q_full)
     for h in range(heads):
         qh[h] = q_full[h * size : (h + 1) * size].astype(LOW)
 
+    def head_rows(ref, h):
+        return ref[pl.ds(pl.multiple_of(h * size, size), size), :]
+
     def query_head(h, carry):
-        raw = tn(att_ref[h], qh[h])
+        raw = tn(head_rows(att_flat, h), qh[h])
 
         def rel_rows(r):
-            return (raw[r * size : (r + 1) * size] * factor_ref[r, h]).astype(LOW).astype(F32)
+            part = raw[r * size : (r + 1) * size] * (prior_ref[r, h] * scale)
+            return part.astype(LOW).astype(F32)
 
         slots, cite = to_slots(rel_rows, kinds, kind_count)
         slot_t = jnp.concatenate(slots, axis=0)
@@ -600,9 +628,22 @@
         qs[h, rows:, 0:HALF] = cite_t.T.astype(LOW)
         return carry
 
-    lax.fori_loop(0, heads, query_head, 0)
-
-    def expand(i, carry):
+    lax.fori_loop(0, heads, query_head, 0, unroll=2)
+    loads[3].wait()
+    mx[...] = jnp.full(mx.shape, NEG_FILL, F32)
+
+    def keep_scores(h, j, both, second, edge):
+        val = jnp.where(second, both[rows:], both[:rows])
+        val = jnp.where(edge, val, NEG_FILL)
+        if h < group:
+            sbuf[j, pl.ds(h * rows, rows), :] = val
+        else:
+            high = val.astype(LOW)
+            probs[j, h, 0:rows, :] = high
+            probs[j, h, rows:, :] = (val - high.astype(F32)).astype(LOW)
+        mx[h] = jnp.maximum(mx[h], jnp.maximum(val[:, :HALF], val[:, HALF:]))
+
+    def arrive(i, carry):
         j = flip(me, i)
 
         @pl.when(i > 0)
@@ -616,98 +657,67 @@
         src = jnp.broadcast_to(source_row(j, 0), (size, rows))
         block = shifted[j, 0:feat, :]
         for k in range(kind_count):
-            key = nn(wkt[pl.ds(k * feat, feat), :], block)
-            value = nn(wvt[pl.ds(k * feat, feat), :], block)
+            key = nn(turned(0, k)[...], block)
+            value = nn(turned(1, k)[...], block)
             for h in range(heads):
                 part = slice(h * size, (h + 1) * size)
                 kt[j, h, pl.ds(k * size, size), :] = pick(src, k, key[part]).astype(LOW)
                 vx[j, h, pl.ds(k * size, size), :] = pick(src, k, value[part]).astype(LOW)
         for h in range(heads):
             vx[j, h, pl.ds(HALF, 16), :] = ones_pad
-        two[j] = (codes_ref[:, cols(j)] == 2).astype(F32).astype(LOW)
+        code = codes[:, cols(j)]
+        second = code == 2
+        edge = code > 0
+        two[j] = second.astype(F32).astype(LOW)
+        before = None
+        for h in range(heads + 1):
+            both = nn(qs[h, :, 0:HALF], kt[j, h]) if h < heads else None
+            if h > 0:
+                keep_scores(h - 1, j, before, second, edge)
+            before = both
         return carry
 
-    lax.fori_loop(0, n_blk, expand, 0)
+    lax.fori_loop(0, n_blk, arrive, 0)
     for send_at in range(1, n_blk):
         hand_on(me, 1, send_at).wait_send()
 
-    def score_block(h, j):
-        both = nn(qs[h, :, 0:HALF], kt[j, h])
-        code = codes_ref[:, cols(j)]
-        val = jnp.where(code == 2, both[rows:], both[:rows])
-        val = jnp.where(code > 0, val, NEG_FILL)
-        sbuf[h % 2, j] = val
-        top = jnp.maximum(val[:, :HALF], val[:, HALF:])
-        for c in range(2 * HALF, rows, HALF):
-            top = jnp.maximum(top, val[:, c : c + HALF])
-        mx[h % 2] = jnp.maximum(mx[h % 2], top)
-
-    def prob_block(h, j):
-        top = sm[h % 2]
-        val = jnp.exp(sbuf[h % 2, j] - jnp.concatenate([top] * (rows // HALF), axis=1))
-        total = val[:, :HALF]
-        for c in range(HALF, rows, HALF):
-            total = total + val[:, c : c + HALF]
-        mx[2 + h % 2] = mx[2 + h % 2] + total
+    def prob_block(h, j, top):
+        if h < group:
+            val = sbuf[j, pl.ds(h * rows, rows), :]
+        else:
+            val = probs[j, h, 0:rows, :].astype(F32) + probs[j, h, rows:, :].astype(F32)
+        val = jnp.exp(val - top)
         low = val.astype(LOW)
         second = low * two[j]
         probs[j, h, 0:rows, :] = low - second
         probs[j, h, rows:, :] = second
-        acc[h] = acc[h] + nt(vx[j, h, 0:HALF, :], probs[j, h])
-
-    def open_head(h):
-        mx[h % 2] = jnp.full((rows, HALF), NEG_FILL, F32)
-
-    def close_scores(h):
-        top = jnp.max(mx[h % 2], axis=1, keepdims=True)
-        sm[h % 2] = jnp.broadcast_to(jnp.maximum(top, 0.1 * NEG_FILL), (rows, HALF))
-        mx[2 + h % 2] = jnp.zeros((rows, HALF), F32)
-        acc[h] = jnp.zeros(acc.shape[1:], F32)
-
-    def close_probs(h):
-        total = jnp.sum(mx[2 + h % 2], axis=1, keepdims=True)
-        sm[2] = jnp.where(lane == h, jnp.broadcast_to(total, (rows, HALF)), sm[2])
-
-    sm[2] = jnp.zeros((rows, HALF), F32)
-    open_head(0)
-
-    def first(j, carry):
-        score_block(0, j)
-        return carry
-
-    lax.fori_loop(0, n_blk, first, 0)
-
-    def forward_head(h, carry):
-        close_scores(h)
-        open_head(h + 1)
-
-        def step(j, carry):
-            score_block(h + 1, j)
-            prob_block(h, j)
-            return carry
-
-        lax.fori_loop(0, n_blk, step, 0)
-        close_probs(h)
-        return carry
-
-    lax.fori_loop(0, heads - 1, forward_head, 0)
-    close_scores(heads - 1)
-
-    def last(j, carry):
-        prob_block(heads - 1, j)
-        return carry
-
-    lax.fori_loop(0, n_blk, last, 0)
-    close_probs(heads - 1)
-
-    denom = jnp.maximum(sm[2].T, 1.0)
-    inverse = 1.0 / denom
-    sm[2, 0:HALF, :] = inverse[:, 0:HALF]
-    sm[2, HALF : 2 * HALF, :] = inverse[:, HALF : 2 * HALF]
+        return val[:, :HALF] + val[:, HALF:]
+
+    totals = jnp.zeros((rows, HALF), F32)
+    for h in range(heads):
+        top = jnp.max(mx[h], axis=1, keepdims=True)
+        top = jnp.broadcast_to(jnp.maximum(top, 0.1 * NEG_FILL), (rows, rows))
+        value_sum = None
+        total = None
+        for j in range(n_blk + 1):
+            if j < n_blk:
+                part = prob_block(h, j, top)
+                total = part if total is None else total + part
+            if j > 0:
+                part = nt(vx[j - 1, h, 0:HALF, :], probs[j - 1, h])
+                value_sum = part if value_sum is None else value_sum + part
+        acc[h] = value_sum
+        total = jnp.sum(total, axis=1, keepdims=True)
+        totals = jnp.where(lane == h, jnp.broadcast_to(total, (rows, HALF)), totals)
+
+    inverse = 1.0 / jnp.maximum(totals.T, 1.0)
+    sm[...] = inverse[0:heads]
 
     def inv_row(h, count):
-        row = jnp.concatenate([sm[2, pl.ds(h, 1), :], sm[2, pl.ds(HALF + h, 1), :]], axis=1)
-        return jnp.broadcast_to(row, (count, rows))
+        return jnp.broadcast_to(sm[pl.ds(h, 1), :], (count, rows))
+
+    def rel_part(h):
+        return sbuf[h // group, pl.ds((h % group) * feat, feat), :].astype(LOW)
 
     for h in range(heads):
         inv = inv_row(h, HALF)
@@ -718,8 +728,10 @@
         rel = to_relations(
             lambda s: u_slot[s * size : (s + 1) * size], u_cite, kinds, kind_count, rel_count
         )
-        urel[h] = jnp.concatenate(rel, axis=0).astype(LOW)
-        agg[pl.ds(h * size, size), :] = nn(msg_ref[h], urel[h])
+        rel = jnp.concatenate(rel, axis=0)
+        sbuf[h // group, pl.ds((h % group) * feat, feat), :] = rel
+        agg[pl.ds(h * size, size), :] = nn(head_rows(msg_flat, h), rel.astype(LOW))
+    loads[4].wait()
     agg_t = agg[...]
     slope = 0.7978845608028654
     inner = jnp.tanh(slope * (agg_t + 0.044715 * agg_t * agg_t * agg_t))
@@ -727,18 +739,21 @@
     gelu_back = 0.5 * (1.0 + inner) + 0.5 * agg_t * (1.0 - inner * inner) * slope * (
         1.0 + 3.0 * 0.044715 * agg_t * agg_t
     )
-    gate = jnp.zeros((feat, rows), F32)
+    skip = jnp.zeros((1, rows), F32)
     branch = jnp.zeros((feat, rows), F32)
     for k in range(kind_count):
-        gate = jnp.where(kinds_f == k, gate_ref[k], gate)
-        branch = jnp.where(kinds_f == k, tn(ow_ref[k], act_t), branch)
+        skip = jnp.where(kinds[0:1] == k, skip_ref[k], skip)
+        branch = jnp.where(kinds_f == k, tn(ow[k], act_t), branch)
+    gate_row = 1.0 / (1.0 + jnp.exp(-skip))
+    gate = jnp.broadcast_to(gate_row, (feat, rows))
     mixed = gate * branch + (1.0 - gate) * x_f
     centered = mixed - jnp.mean(mixed, axis=0, keepdims=True)
     inv_std = lax.rsqrt(jnp.mean(centered * centered, axis=0, keepdims=True) + LN_EPS)
     normed = centered * inv_std
-    gain = gain_ref[...]
-    out_t = valid_f * (normed * gain + bias_ref[...])
-    out_ref[...] = out_t.T.astype(LOW)
+    affine = jnp.concatenate([gain_ref[...], bias_ref[...], jnp.zeros((HALF - 2, feat), F32)], axis=0).T
+    gain = jnp.broadcast_to(affine[:, 0:1], (feat, rows))
+    bias = jnp.broadcast_to(affine[:, 1:2], (feat, rows))
+    out_ref[...] = (valid_f * (normed * gain + bias)).T.astype(LOW)
     grad_y = cot_ref[...].astype(F32).T * valid_f
     gain_col = jnp.sum(grad_y * normed, axis=1, keepdims=True)
     bias_col = jnp.sum(grad_y, axis=1, keepdims=True)
@@ -748,24 +763,27 @@
         - jnp.mean(grad_norm, axis=0, keepdims=True)
         - normed * jnp.mean(grad_norm * normed, axis=0, keepdims=True)
     )
-    gate_row = gate[0:1]
     skip_row = (
         jnp.sum(grad_mix * (branch - x_f), axis=0, keepdims=True) * gate_row * (1.0 - gate_row)
     )
     base[...] = (1.0 - gate) * grad_mix
-    grad_branch = (gate * grad_mix).astype(LOW)
+    grad_branch = gate * grad_mix
     grad_act = jnp.zeros((feat, rows), F32)
     for k in range(kind_count):
-        masked = pick(kinds_f, k, grad_branch.astype(F32)).astype(LOW)
-        store_grad(3 * kind_count + k, nt(act_t, masked))
-        grad_act = grad_act + nn(ow_ref[k], masked)
+        masked = pick(kinds_f, k, grad_branch).astype(LOW)
+        out_grad = nt(act_t, masked)
+        store_part(out_at(k, 0), out_grad[:, :HALF])
+        store_part(out_at(k, 1), out_grad[:, HALF:])
+        grad_act = grad_act + nn(ow[k], masked)
     agg[...] = gelu_back * grad_act
 
-    def grad_head(h, carry):
-        grad_agg = agg[pl.ds(pl.multiple_of(h * size, size), size), :].astype(LOW)
-        store_rows(4 * kind_count + 1, h, nt(grad_agg, urel[h]))
+    for h in range(heads):
+        grad_agg = agg[pl.ds(h * size, size), :].astype(LOW)
+        msg_grad = nt(grad_agg, rel_part(h))
+        store_part(msg_at(0) + h * size, msg_grad[:, :HALF])
+        store_part(msg_at(1) + h * size, msg_grad[:, HALF:])
         inv = inv_row(h, size)
-        grad_u = tn(msg_ref[h], grad_agg)
+        grad_u = tn(head_rows(msg_flat, h), grad_agg)
 
         def rel_rows(r):
             return grad_u[r * size : (r + 1) * size] * inv
@@ -791,11 +809,33 @@
         qs[h, 0:rows, HALF:] = tail_t[:, 0:16]
         qs[h, rows:, HALF:] = tail_t[:, 0:16]
         acc[h] = jnp.zeros(acc.shape[1:], F32)
+
+    slot_id = lax.broadcasted_iota(jnp.int32, (HALF, rows), 0) // size
+
+    def own_slots(j):
+        return slot_id == jnp.broadcast_to(source_row(j, 0), (HALF, rows))
+
+    def value_block(j, carry):
+        own = own_slots(j)
+        for h in range(heads):
+            part = jnp.where(own, nn(gt2[h], probs[j, h]), 0.0)
+            for k in range(kind_count):
+                sbuf[j, pl.ds(k * feat + h * size, size), :] = part[k * size : (k + 1) * size]
+        total = None
+        for k in range(kind_count):
+            part = nn(vw[k], sbuf[j, pl.ds(k * feat, feat), :].astype(LOW))
+            total = part if total is None else total + part
+        shift_out[j] = total.astype(LOW)
         return carry
 
-    lax.fori_loop(0, heads, grad_head, 0)
-
-    slot_id = lax.broadcasted_iota(jnp.int32, (HALF, rows), 0) // size
+    lax.fori_loop(0, n_blk, value_block, 0, unroll=2)
+    for k in range(kind_count):
+        total = None
+        for j in range(n_blk):
+            part = nt(shifted[j, 0:feat, :], sbuf[j, pl.ds(k * feat, feat), :].astype(LOW))
+            total = part if total is None else total + part
+        store_part(value_at(k, 0), total[:, :HALF])
+        store_part(value_at(k, 1), total[:, HALF:])
 
     pack_ref[...] = jnp.zeros_like(pack_ref)
 
@@ -804,49 +844,76 @@
             shift_out.at[j], shift_in.at[me], back_send, back_recv, j, me, (j, rep)
         )
 
-    def back_block(i, carry):
-        j = flip(me, n_blk - 1 - i)
-        src = jnp.broadcast_to(source_row(j, 0), (HALF, rows))
-        own = slot_id == src
-
-        def back_head(h, carry):
-            pair = probs[j, h]
-            grad = pair * nn(qs[h], vx[j, h]).astype(LOW)
-            d_key = jnp.where(own, nn(qt2[h], grad), 0.0).astype(LOW)
-            d_value = jnp.where(own, nn(gt2[h], pair), 0.0).astype(LOW)
-            for k in range(kind_count):
-                at = pl.ds(pl.multiple_of(k * feat + h * size, size), size)
-                dka[at, cols(j)] = d_key[k * size : (k + 1) * size]
-                dva[at, cols(j)] = d_value[k * size : (k + 1) * size]
-            acc[h] = acc[h] + nt(kt[j, h], grad)
+    grad_bufs = (grad_even, grad_odd)
+    for g in range(2):
+        half = slice(g * HALF, (g + 1) * HALF)
+        key_cat = jnp.concatenate([kw[k, :, half] for k in range(kind_count)], axis=1)
+
+        def score_grads(i, carry, g=g, key_cat=key_cat):
+            j = flip(me, n_blk - 1 - i)
+            own = own_slots(j)
+            for u in range(group + 1):
+                h = g * group + u
+                if u < group:
+                    grad_bufs[h % 2][...] = probs[j, h] * nn(qs[h], vx[j, h]).astype(LOW)
+                if u > 0:
+                    grad = grad_bufs[(h - 1) % 2][...]
+                    part = jnp.where(own, nn(qt2[h - 1], grad), 0.0)
+                    for k in range(kind_count):
+                        at = pl.ds(k * HALF + (u - 1) * size, size)
+                        sbuf[j, at, :] = part[k * size : (k + 1) * size]
+                    acc[h - 1] = acc[h - 1] + nt(kt[j, h - 1], grad)
+            total = shift_out[j].astype(F32) + nn(
+                key_cat, sbuf[j, pl.ds(0, kind_count * HALF), :].astype(LOW)
+            )
+            low = total.astype(LOW)
+            shift_out[j] = low
+            if g == 1:
+
+                @pl.when(i < n_blk - 1)
+                def _():
+                    send_back(j).start()
+
+                gaps = gap_hot(source_row(j, 1), levels)
+                pack_ref[0:levels, :] = pack_ref[0:levels, :] + nt(gaps, low)
             return carry
 
-        lax.fori_loop(0, heads, back_head, 0)
-        total = jnp.zeros((feat, rows), F32)
+        lax.fori_loop(0, n_blk, score_grads, 0)
+        total = None
+        for j in range(n_blk):
+            part = nt(
+                shifted[j, 0:feat, :], sbuf[j, pl.ds(0, kind_count * HALF), :].astype(LOW)
+            )
+            total = part if total is None else total + part
         for k in range(kind_count):
-            at = pl.ds(k * feat, feat)
-            total = total + nn(kw_ref[k], dka[at, cols(j)]) + nn(vw_ref[k], dva[at, cols(j)])
-        low = total.astype(LOW)
-        shift_out[j] = low
-
-        @pl.when(i < n_blk - 1)
-        def _():
-            send_back(j).start()
-
-        pack_ref[0:levels, :] = pack_ref[0:levels, :] + nt(gap_hot(source_row(j, 1), levels), low)
-        return carry
-
-    lax.fori_loop(0, n_blk, back_block, 0)
-
-    for k in range(kind_count):
-        at = pl.ds(k * feat, feat)
-        k_sum = jnp.zeros((feat, feat), F32)
-        v_sum = jnp.zeros((feat, feat), F32)
-        for j in range(n_blk):
-            k_sum = k_sum + nt(shifted[j, 0:feat, :], dka[at, pl.ds(j * rows, rows)])
-            v_sum = v_sum + nt(shifted[j, 0:feat, :], dva[at, pl.ds(j * rows, rows)])
-        store_grad(kind_count + k, k_sum)
-        store_grad(2 * kind_count + k, v_sum)
+            store_part(key_at(k, g), total[:, k * HALF : (k + 1) * HALF])
+        grad_q = []
+        for h in range(g * group, (g + 1) * group):
+            slot = acc[h, :, 0:rows]
+            rel = to_relations(
+                lambda s: slot[s * size : (s + 1) * size],
+                acc[h, 0:size, rows:],
+                kinds,
+                kind_count,
+                rel_count,
+            )
+            rel = [part.astype(LOW) for part in rel]
+            att_grad = nt(qh[h], jnp.concatenate(rel, axis=0))
+            store_part(att_at(0) + h * size, att_grad[:, :HALF])
+            store_part(att_at(1) + h * size, att_grad[:, HALF:])
+            raw = [
+                (part.astype(F32) * (prior_ref[r, h] * scale)).astype(LOW)
+                for r, part in enumerate(rel)
+            ]
+            grad_q.append(nn(head_rows(att_flat, h), jnp.concatenate(raw, axis=0)))
+        grad_q = jnp.concatenate(grad_q, axis=0).astype(LOW).astype(F32)
+        total = base[...]
+        for k in range(kind_count):
+            masked = pick(kinds_f[0:HALF], k, grad_q).astype(LOW)
+            store_part(query_at(k, g), nt(xt[...], masked))
+            total = total + nn(qw[k, :, half], masked)
+        base[...] = total
+
     pair = jnp.where(
         lane == 0,
         jnp.broadcast_to(gain_col, (feat, HALF)),
@@ -861,30 +928,7 @@
     pack_ref[levels : levels + 8, :] = jnp.concatenate(
         [pair[0:2], skips, jnp.zeros((5, rows), F32)], axis=0
     )
-
-    def query_back(h, carry):
-        slot = acc[h, :, 0:rows]
-        rel = to_relations(
-            lambda s: slot[s * size : (s + 1) * size],
-            acc[h, 0:size, rows:],
-            kinds,
-            kind_count,
-            rel_count,
-        )
-        rel = [part.astype(LOW) for part in rel]
-        at = pl.ds(pl.multiple_of(h * size, size), size)
-        store_rows(4 * kind_count, h, nt(qh[h], jnp.concatenate(rel, axis=0)))
-        raw = [(part.astype(F32) * factor_ref[r, h]).astype(LOW) for r, part in enumerate(rel)]
-        agg[at, :] = nn(att_ref[h], jnp.concatenate(raw, axis=0))
-        return carry
-
-    lax.fori_loop(0, heads, query_back, 0)
-    grad_q = agg[...].astype(LOW).astype(F32)
     total = base[...] + shift_out[me].astype(F32)
-    for k in range(kind_count):
-        masked = pick(kinds_f, k, grad_q).astype(LOW)
-        store_grad(k, nt(x_t, masked))
-        total = total + nn(qw_ref[k], masked)
     for mask in range(1, n_blk):
         j = flip(me, mask)
         send_back(j).wait_send()
@@ -893,23 +937,39 @@
     input_ref[...] = total.T.astype(LOW)
 
 
+def out_at(k, half):
+    return (2 * k + half) * 256
+
+
+def msg_at(half):
+    return 2048 + half * 256
+
+
+def value_at(k, half):
+    return 2560 + (2 * k + half) * 256
+
+
+def query_at(k, half):
+    return 4608 + (8 * half + k) * 256
+
+
+def key_at(k, half):
+    return 4608 + (8 * half + 4 + k) * 256
+
+
+def att_at(half):
+    return 8704 + half * 256
+
+
+GRAD_ROWS = 9216
+
+
 def reduce_kernel(
     grads_ref,
     pack_ref,
-    att_ref,
-    time_ref,
-    factor_ref,
-    qg_ref,
-    kg_ref,
-    vg_ref,
-    og_ref,
-    attg_ref,
-    msgg_ref,
-    prior_ref,
-    rte_ref,
+    full,
     small_ref,
     work,
-    full,
     core_in,
     plane_in,
     line_in,
@@ -1026,28 +1086,52 @@
     late = [share(mine + away[s], size, by_core) for s in range(2)]
     for copy in early + late:
         copy.wait()
-
+    small_ref[...] = small
+
+
+def finish_kernel(
+    full,
+    small_ref,
+    att_flat,
+    time_ref,
+    prior_ref,
+    out_in,
+    input_in,
+    out_ref,
+    input_ref,
+    qg_ref,
+    kg_ref,
+    vg_ref,
+    og_ref,
+    attg_ref,
+    msgg_ref,
+    priorg_ref,
+    skip_ref,
+    rte_ref,
+    gain_ref,
+    bias_ref,
+):
+    out_ref[...] = out_in[...]
+    input_ref[...] = input_in[...]
     kind_count, feat = qg_ref.shape[:2]
     rel_count, heads, width = attg_ref.shape[:3]
-    parts = feat // HALF
-
-    def whole(at):
-        return jnp.concatenate(
-            [full[pl.ds((at * parts + p) * feat, feat), :].astype(F32) for p in range(parts)],
-            axis=1,
-        )
-
-    for m, ref in enumerate((qg_ref, kg_ref, vg_ref, og_ref)):
+    scale = 1.0 / math.sqrt(width)
+
+    def part(start):
+        return full[pl.ds(start, feat), :].astype(F32)
+
+    for ref, at in ((qg_ref, query_at), (kg_ref, key_at), (vg_ref, value_at), (og_ref, out_at)):
         for k in range(kind_count):
-            ref[k] = whole(m * kind_count + k)
-    att = whole(4 * kind_count)
-    msg = whole(4 * kind_count + 1).T
+            for half in range(2):
+                ref[k, :, half * HALF : (half + 1) * HALF] = part(at(k, half))
+    att = jnp.concatenate([part(att_at(0)), part(att_at(1))], axis=1)
+    msg = jnp.concatenate([part(msg_at(0)), part(msg_at(1))], axis=1).T
     for r in range(rel_count):
         for h in range(heads):
             block = (slice(h * width, (h + 1) * width), slice(r * width, (r + 1) * width))
-            attg_ref[r, h] = att[block] * factor_ref[r, h]
+            attg_ref[r, h] = att[block] * (prior_ref[r, h] * scale)
             msgg_ref[r, h] = msg[block[::-1]]
-    prod = (att * att_ref[...].astype(F32)).reshape(heads, width, feat)
+    prod = (att * att_flat[...].astype(F32)).reshape(heads, width, feat)
     prod = jnp.sum(prod, axis=1)
     spread = (
         lax.broadcasted_iota(jnp.int32, (feat, rel_count), 0) // width
@@ -1060,8 +1144,9 @@
             spread, low, (((0,), (1,)), ((), ())), preferred_element_type=F32
         )
         prod = prod - low.astype(F32)
-    prior_ref[...] = prior * (1.0 / math.sqrt(width))
+    priorg_ref[...] = prior * scale
     levels = time_ref.shape[1]
+    small = small_ref[...]
     rte = jnp.zeros(rte_ref.shape, F32)
     rest = small[0:levels]
     for _ in range(3):
@@ -1069,7 +1154,82 @@
         rte = rte + nn(time_ref[...], low)
         rest = rest - low.astype(F32)
     rte_ref[...] = rte
-    small_ref[...] = small[levels:]
+    gain_ref[...] = small[levels : levels + 1]
+    bias_ref[...] = small[levels + 1 : levels + 2]
+    skip_ref[...] = small[levels + 2 : levels + 3, 0:kind_count]
+
+
+def layer_call(n_blk, *args):
+    rows, feat = args[0].shape
+    kind_count = args[8].shape[0]
+    rel_count, heads, size = args[12].shape[:3]
+    vmem = pl.BlockSpec(memory_space=pltpu.VMEM)
+    smem = pl.BlockSpec(memory_space=pltpu.SMEM)
+    hbm = pl.BlockSpec(memory_space=pl.ANY)
+    square = (feat, feat)
+    weight = pltpu.VMEM((kind_count,) + square, LOW)
+
+    def shape(dims, kind):
+        return jax.ShapeDtypeStruct(dims, kind)
+
+    return pl.pallas_call(
+        layer_kernel,
+        out_shape=[
+            shape((rows, feat), LOW),
+            shape((rows, feat), LOW),
+            shape((GRAD_ROWS, HALF), LOW),
+            shape((LEVELS + 8, feat), F32),
+            shape(square, LOW),
+        ],
+        in_specs=[vmem] * 6 + [hbm, vmem] + [hbm] * 4 + [vmem] * 2 + [smem] * 2 + [vmem] * 2,
+        out_specs=[vmem] * 5,
+        scratch_shapes=[
+            pltpu.VMEM((rows, n_blk * rows), jnp.int32),
+            weight,
+            weight,
+            weight,
+            weight,
+            pltpu.VMEM(square, LOW),
+            pltpu.VMEM((n_blk, feat + 16, rows), LOW),
+            pltpu.VMEM((feat, rows), LOW),
+            pltpu.VMEM((feat, rows), F32),
+            pltpu.VMEM((n_blk, feat, rows), LOW),
+            pltpu.VMEM((n_blk, feat, rows), LOW),
+            pltpu.SemaphoreType.DMA((5,)),
+            pltpu.SemaphoreType.DMA((n_blk,)),
+            pltpu.SemaphoreType.DMA((n_blk,)),
+            pltpu.SemaphoreType.DMA((n_blk,)),
+            pltpu.SemaphoreType.DMA((n_blk,)),
+            pltpu.VMEM((n_blk, heads, HALF, rows), LOW),
+            pltpu.VMEM((n_blk, heads, HALF + 16, rows), LOW),
+            pltpu.VMEM((n_blk, heads // 2 * rows, rows), F32),
+            pltpu.VMEM((n_blk, heads, 2 * rows, rows), LOW),
+            pltpu.VMEM((heads, rows, HALF), F32),
+            pltpu.VMEM((heads, rows), F32),
+            pltpu.VMEM((heads, 2 * rows, HALF + 16), LOW),
+            pltpu.VMEM((heads, HALF, 2 * rows), LOW),
+            pltpu.VMEM((heads, size, rows), LOW),
+            pltpu.VMEM((heads, HALF, 2 * rows), LOW),
+            pltpu.VMEM((heads, HALF, 2 * rows), F32),
+            pltpu.VMEM((n_blk, rows, rows), LOW),
+            pltpu.VMEM(square, F32),
+            pltpu.VMEM(square, F32),
+            pltpu.VMEM((2 * rows, rows), LOW),
+            pltpu.VMEM((2 * rows, rows), LOW),
+        ],
+        compiler_params=pltpu.CompilerParams(
+            vmem_limit_bytes=VMEM_CAP, collective_id=0, has_side_effects=True
+        ),
+        name="layer",
+    )(*args)
+
+
+def time_columns(level_count, feat_width):
+    positions = np.arange(level_count, dtype=np.float32)[:, None]
+    steps = np.arange(feat_width // 2, dtype=np.float32)[None, :]
+    phases = positions / np.power(np.float32(10000.0), np.float32(2.0) * steps / feat_width)
+    table = np.stack([np.sin(phases), np.cos(phases)], axis=2).reshape(level_count, feat_width)
+    return jnp.asarray(np.ascontiguousarray(table.T), LOW)
 
 
 def fast_body(
@@ -1094,96 +1254,44 @@
     rows, feat = features.shape
     n_blk = lax.axis_size("blk")
     kind_count = query_w.shape[0]
-    rel_count, heads, size = rel_att.shape[:3]
-    time_low = time_table(LEVELS, feat).astype(LOW)
-    meta = jnp.concatenate(
-        [node_type[None], time_gap[None], node_valid[None], jnp.zeros((5, rows), jnp.int32)], axis=0
-    )
+    time_low = time_columns(LEVELS, feat)
     vmem = pl.BlockSpec(memory_space=pltpu.VMEM)
     smem = pl.BlockSpec(memory_space=pltpu.SMEM)
-    att_flat = rel_att.transpose(1, 2, 0, 3).reshape(feat, rel_count * size)
-    msg_flat = rel_msg.transpose(1, 3, 0, 2).reshape(feat, rel_count * size)
-    factor = rel_prior / math.sqrt(size)
-    gate = jax.nn.sigmoid(skip_logit)
     square = (feat, feat)
-    grad_rows = (4 * kind_count + 2) * (feat // HALF) * feat
 
     def shape(dims, kind):
         return jax.ShapeDtypeStruct(dims, kind)
 
-    layer_out, input_grad, grads, pack = pl.pallas_call(
-        layer_kernel,
-        out_shape=[
-            shape((rows, feat), LOW),
-            shape((rows, feat), LOW),
-            shape((grad_rows, HALF), LOW),
-            shape((LEVELS + 8, feat), F32),
-        ],
-        in_specs=[vmem] * 12 + [smem] * 2 + [vmem] * 2,
-        out_specs=[vmem] * 4,
-        scratch_shapes=[
-            pltpu.VMEM((n_blk, feat + 16, rows), LOW),
-            pltpu.VMEM((feat, rows), LOW),
-            pltpu.VMEM((feat, rows), F32),
-            pltpu.VMEM((n_blk, feat, rows), LOW),
-            pltpu.VMEM((n_blk, feat, rows), LOW),
-            pltpu.SemaphoreType.DMA((n_blk,)),
-            pltpu.SemaphoreType.DMA((n_blk,)),
-            pltpu.SemaphoreType.DMA((n_blk,)),
-            pltpu.SemaphoreType.DMA((n_blk,)),
-            pltpu.VMEM((n_blk, heads, HALF, rows), LOW),
-            pltpu.VMEM((n_blk, heads, HALF + 16, rows), LOW),
-            pltpu.VMEM((2, n_blk, rows, rows), F32),
-            pltpu.VMEM((n_blk, heads, 2 * rows, rows), LOW),
-            pltpu.VMEM((4, rows, HALF), F32),
-            pltpu.VMEM((3, rows, HALF), F32),
-            pltpu.VMEM((heads, 2 * rows, HALF + 16), LOW),
-            pltpu.VMEM((heads, HALF, 2 * rows), LOW),
-            pltpu.VMEM((heads, size, rows), LOW),
-            pltpu.VMEM((heads, HALF, 2 * rows), LOW),
-            pltpu.VMEM((heads, HALF, 2 * rows), F32),
-            pltpu.VMEM((heads, rel_count * size, rows), LOW),
-            pltpu.VMEM((kind_count * feat, n_blk * rows), LOW),
-            pltpu.VMEM((kind_count * feat, n_blk * rows), LOW),
-            pltpu.VMEM((n_blk, rows, rows), LOW),
-            pltpu.VMEM((kind_count * feat, feat), LOW),
-            pltpu.VMEM((kind_count * feat, feat), LOW),
-            pltpu.VMEM(square, F32),
-        ],
-        compiler_params=pltpu.CompilerParams(
-            vmem_limit_bytes=VMEM_CAP, collective_id=0, has_side_effects=True
-        ),
-        name="layer",
-    )(
+    layer_out, input_grad, grads, pack, att_flat = layer_call(
+        n_blk,
         features,
-        meta,
+        node_type[None],
+        time_gap[None],
+        node_valid[None],
         rte_w,
-        time_low.T,
+        time_low,
         edge_codes,
         cotangent,
         query_w,
         key_w,
         value_w,
         out_w,
-        att_flat.reshape(heads, size, rel_count * size),
-        msg_flat.reshape(heads, size, rel_count * size),
-        factor,
-        gate,
-        ln_gain[:, None],
-        ln_bias[:, None],
-    )
-    quarter = grad_rows // 4
-    outs = pl.pallas_call(
+        rel_att,
+        rel_msg,
+        rel_prior,
+        skip_logit,
+        ln_gain[None],
+        ln_bias[None],
+    )
+    quarter = GRAD_ROWS // 4
+    full, small = pl.pallas_call(
         reduce_kernel,
-        out_shape=[shape((kind_count,) + square, F32)] * 4
-        + [shape(rel_att.shape, F32)] * 2
-        + [shape(rel_prior.shape, F32), shape(square, F32), shape((8, feat), F32)],
-        in_specs=[vmem] * 4 + [smem],
-        out_specs=[vmem] * 9,
+        out_shape=[shape(grads.shape, LOW), shape(pack.shape, F32)],
+        in_specs=[vmem] * 2,
+        out_specs=[vmem] * 2,
         scratch_shapes=[
-            pltpu.VMEM((grad_rows // 2, HALF), LOW),
-            pltpu.VMEM((grad_rows, HALF), LOW),
-            pltpu.VMEM((grad_rows // 2, HALF), LOW),
+            pltpu.VMEM((GRAD_ROWS // 2, HALF), LOW),
+            pltpu.VMEM((GRAD_ROWS // 2, HALF), LOW),
             pltpu.VMEM((4, quarter // 2, HALF), LOW),
             pltpu.VMEM((2, 3, quarter // 16, HALF), LOW),
             pltpu.VMEM((6, LEVELS + 8, feat), F32),
@@ -1195,17 +1303,25 @@
             vmem_limit_bytes=VMEM_CAP, collective_id=1, has_side_effects=True
         ),
         name="reduce",
-    )(grads, pack, att_flat, time_low.T, factor)
-    small = outs[8]
-    return (
-        layer_out,
-        input_grad,
-        *outs[:7],
-        small[2, :kind_count],
-        outs[7],
-        small[0],
-        small[1],
-    )
+    )(grads, pack)
+    outs = pl.pallas_call(
+        finish_kernel,
+        out_shape=[shape(layer_out.shape, LOW), shape(input_grad.shape, LOW)]
+        + [shape((kind_count,) + square, F32)] * 4
+        + [shape(rel_att.shape, F32)] * 2
+        + [
+            shape(rel_prior.shape, F32),
+            shape((1, kind_count), F32),
+            shape(square, F32),
+            shape((1, feat), F32),
+            shape((1, feat), F32),
+        ],
+        in_specs=[vmem] * 4 + [smem] + [vmem] * 2,
+        out_specs=[vmem] * 13,
+        compiler_params=pltpu.CompilerParams(vmem_limit_bytes=VMEM_CAP),
+        name="finish",
+    )(full, small, att_flat, time_low, rel_prior, layer_out, input_grad)
+    return (*outs[:9], outs[9][0], outs[10], outs[11][0], outs[12][0])
 
 
 def solution(mesh):

time: 202 us -> 141 us (0.70)
  Pallas kernels: 176 us -> 140 us
  local copies, waits for them, and re-layouts: 21 us -> 0 us
  other arithmetic: 3.97 us -> 0 us
    pallas_call x2 -> x3, Pallas kernels: 176 us -> 140 us  [the longest x1 84.1 us: layer_call(): pl.pallas_call(layer_kernel, out_shape=[shape((rows, feat), LOW), shape((...]
    unnamed x30 -> x0, local copies, waits for them, and re-layouts: 9.78 us -> none
    broadcast_in_dim x3 -> x0, local copies, waits for them, and re-layouts: 2.95 us -> none  [the longest x1 1.47 us: fast_body(): ln_bias[:, None]]
    another operation x3 -> x0, local copies, waits for them, and re-layouts: 2.8 us -> none  [the longest x1 1.02 us: fast_body(): msg_flat.reshape(heads, size, rel_count * size)]
    div x2 -> x0, other arithmetic: 2.52 us -> none  [the longest x1 1.28 us: fast_body(): factor = rel_prior / math.sqrt(size)]
where the time goes in v3:
time: 141 us
  Pallas kernels  140 us (99%)
    pallas_call x1, Pallas kernels, layer_call(): pl.pallas_call(layer_kernel, out_shape=[shape((rows, feat), LOW), shape((...  84.1 us
    pallas_call x1, Pallas kernels, fast_body(): pl.pallas_call(reduce_kernel, out_shape=[shape(grads.shape, LOW), shape(p...  50.7 us
    pallas_call x1, Pallas kernels, fast_body(): pl.pallas_call(finish_kernel, out_shape=[shape(layer_out.shape, LOW), sha...  5.08 us

profile of v3, /device:TPU:0, one launch (start us, length us, event | category | flops | bytes accessed | tf_op | source)
XLA Modules:
  0.0 140.7 jit_solution(14500558240129556833)
XLA Ops:
  0.7 84.1 %layer.1 = (bf16[256,256]{1,0:T(8,128)(2,1)}, bf16[256,256]{1,0:T(8,128)(2,1)}, bf16[9216,128]{1,0:T(8,128)(2,1)}, f32[24,256]{1,0:T(8,128)}, bf16[256,256]{1,0:T(8,128)(2,1)}) custom-call(bf16[256,256]{1,0:T(8,128)(2,1)} %x_ref.1, s32[1,256]{1,0:T(1,128)} %bitcast.8, s32[1,256]{1,0:T(1,128)} %bitcast.9, s32[1,256]{1,0:T(1,128)} %bitcast.10, ...), custom_call_target="tpu_custom_call" | custom-call | tf_op jit(solution)/shard_map/layer/pallas_call | solution.py:1175
  84.8 50.7 %reduce.1 = (bf16[9216,128]{1,0:T(8,128)(2,1)}, f32[24,256]{1,0:T(8,128)}) custom-call(bf16[9216,128]{1,0:T(8,128)(2,1)} %get-tuple-element.33.grads_ref, f32[24,256]{1,0:T(8,128)} %get-tuple-element.34.pack_ref), custom_call_target="tpu_custom_call" | custom-call | tf_op jit(solution)/shard_map/reduce/pallas_call | solution.py:1287
  135.4 5.1 %finish.1 = (bf16[256,256]{1,0:T(8,128)(2,1)}, bf16[256,256]{1,0:T(8,128)(2,1)}, f32[4,256,256]{2,1,0:T(8,128)}, f32[4,256,256]{2,1,0:T(8,128)}, f32[4,256,256]{...) custom-call(bf16[9216,128]{1,0:T(8,128)(2,1)} %get-tuple-element.35., ...), custom_call_target="tpu_custom_call" | custom-call | tf_op jit(solution)/shard_map/finish/pallas_call | solution.py:1307

commit v4 on v3

--- a/solution.py
+++ b/solution.py
@@ -390,7 +390,8 @@
 HALF = 128
 F32 = jnp.float32
 LOW = jnp.bfloat16
-VMEM_CAP = 65000 * 2**10
+VMEM_CAP = 65400 * 2**10
+PROB_UNROLL = 2
 
 
 def nn(a, b):
@@ -466,6 +467,191 @@
             barrier, inc=1, device_id=device, device_id_type=pl.DeviceIdType.MESH
         )
     pl.semaphore_wait(barrier, len(devices))
+
+
+def out_at(k, half):
+    return (2 * k + half) * 256
+
+
+def msg_at(half):
+    return 2048 + half * 256
+
+
+def query_at(k, half):
+    return 2560 + (12 * half + k) * 256
+
+
+def key_at(k, half):
+    return 2560 + (12 * half + 4 + k) * 256
+
+
+def value_at(k, half):
+    return 2560 + (12 * half + 8 + k) * 256
+
+
+def att_at(half):
+    return 8704 + half * 256
+
+
+SUM_PARTS = ((0, (512, 768)), (2560, (768, 768)), (5632, (768, 1024)))
+SUM_TICKS = (
+    ((0, 0, 1), (2, 0, 2), (3, 0, 3)),
+    ((0, 0, 4), (1, 1, 1), (2, 0, 5), (2, 1, 2), (3, 0, 6), (3, 1, 3)),
+)
+GRAD_ROWS = 9216
+
+
+def span(start, size):
+    return pl.ds(start if isinstance(start, int) else pl.multiple_of(start, 16), size)
+
+
+def summation(part, refs, places, pack):
+    grads, full, core_in, first_in, second_in, line_in, sends, recvs = refs
+    (z, y, x, core), by_core, by_x, by_y, by_z = places
+    base, streams = SUM_PARTS[part]
+    half = sum(streams)
+    ahead = sum(sum(SUM_PARTS[before][1]) for before in range(part))
+    count = iter(range(32 * part, 32 * part + 32))
+    mine = base + core * half
+    begin = (mine, mine + streams[0])
+    landing = (ahead, ahead + streams[0])
+    pending = []
+
+    def send(src, dst, device):
+        at = next(count)
+
+        def copy():
+            return remote(src(), dst(), sends, recvs, at, at, device)
+
+        copy().start()
+        pending.append(copy)
+
+    def settle():
+        for copy in pending:
+            copy().wait()
+        pending.clear()
+
+    def piece(ref, start, size):
+        return lambda: ref.at[span(start, size), :]
+
+    def small(ref, at):
+        return lambda: ref.at[at]
+
+    def load(ref, start, size):
+        return ref[span(start, size), :].astype(F32)
+
+    def add_in(start, size, ref, at):
+        value = load(grads, start, size) + load(ref, at, size)
+        grads[span(start, size), :] = value.astype(LOW)
+
+    turns = ((x, y), (y, x))
+    ways = ((by_x, by_y), (by_y, by_x))
+    firsts = [size // 2 for size in streams]
+    seconds = [size // 4 for size in streams]
+    lines = [size // 16 for size in streams]
+    at_first = [begin[s] + turns[s][0] * firsts[s] for s in range(2)]
+    at_second = [at_first[s] + turns[s][1] * seconds[s] for s in range(2)]
+    at_line = [at_second[s] + z * lines[s] for s in range(2)]
+    other_z = [(z + step) % 4 for step in (1, 2, 3)]
+    aways = [
+        [begin[s] + firsts[s] - turns[s][0] * firsts[s] for s in range(2)],
+        [at_first[s] + seconds[s] - turns[s][1] * seconds[s] for s in range(2)],
+    ]
+    there_core = base + half - core * half
+    line_there = [[at_second[s] + other_z[i] * lines[s] for i in range(3)] for s in range(2)]
+    line_land = [3 * landing[s] // 16 for s in range(2)]
+
+    def cores():
+        send(piece(grads, there_core, half), piece(core_in, ahead, half), by_core)
+        if pack:
+            send(small(pack[0], 0), small(pack[1], 0), by_core)
+
+    def plane_one():
+        settle()
+        add_in(mine, half, core_in, ahead)
+        for s in range(2):
+            send(
+                piece(grads, aways[0][s], firsts[s]),
+                piece(first_in, landing[s] // 2, firsts[s]),
+                ways[s][0],
+            )
+        if pack:
+            pack[0][1] = pack[0][0] + pack[1][0]
+            send(small(pack[0], 1), small(pack[1], 1), by_x)
+
+    def plane_two():
+        settle()
+        for s in range(2):
+            add_in(at_first[s], firsts[s], first_in, landing[s] // 2)
+        for s in range(2):
+            send(
+                piece(grads, aways[1][s], seconds[s]),
+                piece(second_in, landing[s] // 4, seconds[s]),
+                ways[s][1],
+            )
+        if pack:
+            pack[0][2] = pack[0][1] + pack[1][1]
+            send(small(pack[0], 2), small(pack[1], 2), by_y)
+
+    def line():
+        settle()
+        for s in range(2):
+            add_in(at_second[s], seconds[s], second_in, landing[s] // 4)
+        for step in (2, 3, 1):
+            for s in range(2):
+                land = line_land[s] + (step - 1) * lines[s]
+                send(
+                    piece(grads, line_there[s][step - 1], lines[s]),
+                    piece(line_in, land, lines[s]),
+                    by_z[step - 1],
+                )
+        if pack:
+            pack[0][3] = pack[0][2] + pack[1][2]
+            for step in (2, 3, 1):
+                send(small(pack[0], 3), small(pack[1], 2 + step), by_z[step - 1])
+
+    def share(start, size, device):
+        send(piece(full, start, size), piece(full, start, size), device)
+
+    def line_back():
+        settle()
+        for s in range(2):
+            value = load(grads, at_line[s], lines[s])
+            for step in range(3):
+                value = value + load(line_in, line_land[s] + step * lines[s], lines[s])
+            full[span(at_line[s], lines[s]), :] = value.astype(LOW)
+        for step in (2, 3, 1):
+            for s in range(2):
+                share(at_line[s], lines[s], by_z[step - 1])
+        if pack:
+            pack[2][...] = pack[0][3] + pack[1][3] + pack[1][4] + pack[1][5]
+
+    def plane_two_back():
+        settle()
+        for s in range(2):
+            share(at_second[s], seconds[s], ways[s][1])
+
+    def plane_one_back():
+        settle()
+        for s in range(2):
+            share(at_first[s], firsts[s], ways[s][0])
+
+    def cores_back():
+        settle()
+        for s in range(2):
+            share(begin[s], streams[s], by_core)
+
+    return [
+        cores,
+        plane_one,
+        plane_two,
+        line,
+        line_back,
+        plane_two_back,
+        plane_one_back,
+        cores_back,
+        settle,
+    ]
 
 
 def layer_kernel(
@@ -489,8 +675,8 @@
     bias_ref,
     out_ref,
     input_ref,
-    grads_ref,
-    pack_ref,
+    full,
+    small_ref,
     att_flat,
     codes,
     qw,
@@ -502,26 +688,35 @@
     xt,
     base,
     shift_out,
-    shift_in,
+    plane_back,
+    line_back,
     load_sem,
     gather_send,
     gather_recv,
     back_send,
     back_recv,
+    grads,
+    core_in,
+    first_in,
+    second_in,
+    line_in,
+    pack,
+    pack_in,
+    sum_send,
+    sum_recv,
     kt,
     vx,
     sbuf,
     probs,
-    mx,
     sm,
     qs,
+    tails,
     qt2,
     qh,
     gt2,
     acc,
     two,
     agg,
-    flat,
     grad_even,
     grad_odd,
 ):
@@ -541,7 +736,9 @@
     ]
     for load in loads:
         load.start()
-    greet([(flip(me, mask), rep) for mask in range(1, n_blk)])
+    by_core = (me, rep + 1 - 2 * (rep % 2))
+    by_x = (me, rep + 2 - 4 * (rep // 2))
+    greet([(flip(me, mask), rep) for mask in range(1, n_blk)] + [by_core, by_x])
 
     x_f = x_ref[...].astype(F32).T
     x_t = x_f.astype(LOW)
@@ -583,16 +780,16 @@
         return pl.ds(pl.multiple_of(j * rows, rows), rows)
 
     def store_part(start, value):
-        grads_ref[pl.ds(start, value.shape[0]), :] = value.astype(LOW)
+        grads[pl.ds(start, value.shape[0]), :] = value.astype(LOW)
 
     for r in range(rel_count):
         for h in range(heads):
-            flat[h * size : (h + 1) * size, r * size : (r + 1) * size] = att_ref[r, h].astype(F32)
-    att_flat[...] = flat[...].astype(LOW)
+            agg[h * size : (h + 1) * size, r * size : (r + 1) * size] = att_ref[r, h].astype(F32)
+    att_flat[...] = agg[...].astype(LOW)
     for r in range(rel_count):
         for h in range(heads):
-            flat[r * size : (r + 1) * size, h * size : (h + 1) * size] = msg_ref[r, h].astype(F32)
-    msg_flat[...] = flat[...].T.astype(LOW)
+            agg[r * size : (r + 1) * size, h * size : (h + 1) * size] = msg_ref[r, h].astype(F32)
+    msg_flat[...] = agg[...].T.astype(LOW)
 
     def turned(m, k):
         return probs.at[0, 2 * m + k // 2, pl.ds((k % 2) * feat, feat), :]
@@ -624,13 +821,13 @@
         cite_t = jnp.concatenate([cite, jnp.zeros((HALF - size, rows), F32)], axis=0)
         qt2[h, :, 0:rows] = slot_t.astype(LOW)
         qt2[h, :, rows:] = cite_t.astype(LOW)
-        qs[h, 0:rows, 0:HALF] = slot_t.T.astype(LOW)
-        qs[h, rows:, 0:HALF] = cite_t.T.astype(LOW)
+        qs[h, 0:rows, :] = slot_t.T.astype(LOW)
+        qs[h, rows:, :] = cite_t.T.astype(LOW)
         return carry
 
     lax.fori_loop(0, heads, query_head, 0, unroll=2)
     loads[3].wait()
-    mx[...] = jnp.full(mx.shape, NEG_FILL, F32)
+    acc[:, :, 0:rows] = jnp.full((heads, HALF, rows), NEG_FILL, F32)
 
     def keep_scores(h, j, both, second, edge):
         val = jnp.where(second, both[rows:], both[:rows])
@@ -641,7 +838,10 @@
             high = val.astype(LOW)
             probs[j, h, 0:rows, :] = high
             probs[j, h, rows:, :] = (val - high.astype(F32)).astype(LOW)
-        mx[h] = jnp.maximum(mx[h], jnp.maximum(val[:, :HALF], val[:, HALF:]))
+        top = jnp.maximum(val[:, :HALF], val[:, HALF:])
+        for part in range(rows // HALF):
+            at = slice(part * HALF, (part + 1) * HALF)
+            acc[h, :, at] = jnp.maximum(acc[h, :, at], top[at])
 
     def arrive(i, carry):
         j = flip(me, i)
@@ -663,15 +863,13 @@
                 part = slice(h * size, (h + 1) * size)
                 kt[j, h, pl.ds(k * size, size), :] = pick(src, k, key[part]).astype(LOW)
                 vx[j, h, pl.ds(k * size, size), :] = pick(src, k, value[part]).astype(LOW)
-        for h in range(heads):
-            vx[j, h, pl.ds(HALF, 16), :] = ones_pad
         code = codes[:, cols(j)]
         second = code == 2
         edge = code > 0
         two[j] = second.astype(F32).astype(LOW)
         before = None
         for h in range(heads + 1):
-            both = nn(qs[h, :, 0:HALF], kt[j, h]) if h < heads else None
+            both = nn(qs[h], kt[j, h]) if h < heads else None
             if h > 0:
                 keep_scores(h - 1, j, before, second, edge)
             before = both
@@ -681,9 +879,9 @@
     for send_at in range(1, n_blk):
         hand_on(me, 1, send_at).wait_send()
 
-    def prob_block(h, j, top):
-        if h < group:
-            val = sbuf[j, pl.ds(h * rows, rows), :]
+    def prob_block(h, j, top, kept):
+        if kept:
+            val = sbuf[j, pl.ds(pl.multiple_of(h * rows, rows), rows), :]
         else:
             val = probs[j, h, 0:rows, :].astype(F32) + probs[j, h, rows:, :].astype(F32)
         val = jnp.exp(val - top)
@@ -693,28 +891,41 @@
         probs[j, h, rows:, :] = second
         return val[:, :HALF] + val[:, HALF:]
 
-    totals = jnp.zeros((rows, HALF), F32)
-    for h in range(heads):
-        top = jnp.max(mx[h], axis=1, keepdims=True)
+    sm[...] = jnp.zeros((rows, HALF), F32)
+
+    def prob_head(h, kept):
+        top = jnp.concatenate([acc[h, :, 0:HALF], acc[h, :, HALF:rows]], axis=0)
+        top = jnp.max(top, axis=1, keepdims=True)
         top = jnp.broadcast_to(jnp.maximum(top, 0.1 * NEG_FILL), (rows, rows))
         value_sum = None
         total = None
         for j in range(n_blk + 1):
             if j < n_blk:
-                part = prob_block(h, j, top)
+                part = prob_block(h, j, top, kept)
                 total = part if total is None else total + part
             if j > 0:
-                part = nt(vx[j - 1, h, 0:HALF, :], probs[j - 1, h])
+                part = nt(vx[j - 1, h], probs[j - 1, h])
                 value_sum = part if value_sum is None else value_sum + part
         acc[h] = value_sum
         total = jnp.sum(total, axis=1, keepdims=True)
-        totals = jnp.where(lane == h, jnp.broadcast_to(total, (rows, HALF)), totals)
-
-    inverse = 1.0 / jnp.maximum(totals.T, 1.0)
-    sm[...] = inverse[0:heads]
+        sm[...] = jnp.where(lane == h, jnp.broadcast_to(total, (rows, HALF)), sm[...])
+
+    for kept in (True, False):
+
+        def prob_pair(pair, carry, kept=kept):
+            for u in range(PROB_UNROLL):
+                prob_head((0 if kept else group) + PROB_UNROLL * pair + u, kept)
+            return carry
+
+        lax.fori_loop(0, group // PROB_UNROLL, prob_pair, 0)
+
+    inverse = 1.0 / jnp.maximum(sm[...].T, 1.0)
+    sm[0:heads, :] = inverse[0:heads, 0:HALF]
+    sm[heads : 2 * heads, :] = inverse[0:heads, HALF:]
 
     def inv_row(h, count):
-        return jnp.broadcast_to(sm[pl.ds(h, 1), :], (count, rows))
+        row = jnp.concatenate([sm[pl.ds(h, 1), :], sm[pl.ds(heads + h, 1), :]], axis=1)
+        return jnp.broadcast_to(row, (count, rows))
 
     def rel_part(h):
         return sbuf[h // group, pl.ds((h % group) * feat, feat), :].astype(LOW)
@@ -804,89 +1015,125 @@
             [delta_hi, delta - delta_hi, jnp.zeros((HALF - 2, rows), F32)], axis=0
         )
         tail_t = tail.T.astype(LOW)
-        qs[h, 0:rows, 0:HALF] = slot_f.T.astype(LOW)
-        qs[h, rows:, 0:HALF] = cite_f.T.astype(LOW)
-        qs[h, 0:rows, HALF:] = tail_t[:, 0:16]
-        qs[h, rows:, HALF:] = tail_t[:, 0:16]
+        qs[h, 0:rows, :] = slot_f.T.astype(LOW)
+        qs[h, rows:, :] = cite_f.T.astype(LOW)
+        tails[h] = tail_t[:, 0:16]
         acc[h] = jnp.zeros(acc.shape[1:], F32)
 
+    refs = (grads, full, core_in, first_in, second_in, line_in, sum_send, sum_recv)
+    by_y = (flip(me, 1), rep)
+    by_z = [(((me // 2 + step) % 4) * 2 + me % 2, rep) for step in (1, 2, 3)]
+    places = ((me // 2, me % 2, rep // 2, rep % 2), by_core, by_x, by_y, by_z)
+    sums = [summation(part, refs, places, None) for part in range(2)]
+    sums.append(summation(2, refs, places, (pack, pack_in, small_ref)))
+    sums[0][0]()
+
     slot_id = lax.broadcasted_iota(jnp.int32, (HALF, rows), 0) // size
-
-    def own_slots(j):
-        return slot_id == jnp.broadcast_to(source_row(j, 0), (HALF, rows))
-
-    def value_block(j, carry):
-        own = own_slots(j)
-        for h in range(heads):
-            part = jnp.where(own, nn(gt2[h], probs[j, h]), 0.0)
-            for k in range(kind_count):
-                sbuf[j, pl.ds(k * feat + h * size, size), :] = part[k * size : (k + 1) * size]
-        total = None
-        for k in range(kind_count):
-            part = nn(vw[k], sbuf[j, pl.ds(k * feat, feat), :].astype(LOW))
-            total = part if total is None else total + part
+    pack[0] = jnp.zeros(pack.shape[1:], F32)
+
+    def along_y(m):
+        return remote(
+            shift_out.at[flip(me, m + 1)],
+            plane_back.at[m // 2],
+            back_send,
+            back_recv,
+            m // 2,
+            m // 2,
+            by_y,
+        )
+
+    def along_z(m):
+        at = n_blk // 2 + m // 2
+        return remote(
+            shift_out.at[flip(me, m)],
+            line_back.at[m // 2],
+            back_send,
+            back_recv,
+            at,
+            at,
+            (flip(me, m), rep),
+        )
+
+    def pass_on(m):
+        along_y(m).wait_recv()
+        j = flip(me, m)
+        total = shift_out[j].astype(F32) + plane_back[m // 2].astype(F32)
         shift_out[j] = total.astype(LOW)
-        return carry
-
-    lax.fori_loop(0, n_blk, value_block, 0, unroll=2)
-    for k in range(kind_count):
-        total = None
-        for j in range(n_blk):
-            part = nt(shifted[j, 0:feat, :], sbuf[j, pl.ds(k * feat, feat), :].astype(LOW))
-            total = part if total is None else total + part
-        store_part(value_at(k, 0), total[:, :HALF])
-        store_part(value_at(k, 1), total[:, HALF:])
-
-    pack_ref[...] = jnp.zeros_like(pack_ref)
-
-    def send_back(j):
-        return remote(
-            shift_out.at[j], shift_in.at[me], back_send, back_recv, j, me, (j, rep)
-        )
+        along_z(m).start()
 
     grad_bufs = (grad_even, grad_odd)
     for g in range(2):
         half = slice(g * HALF, (g + 1) * HALF)
-        key_cat = jnp.concatenate([kw[k, :, half] for k in range(kind_count)], axis=1)
-
-        def score_grads(i, carry, g=g, key_cat=key_cat):
-            j = flip(me, n_blk - 1 - i)
-            own = own_slots(j)
-            for u in range(group + 1):
+
+        def block_pair(pair, carry, g=g, half=half):
+            m = n_blk - 2 - 2 * pair
+            blocks = (flip(me, m + 1), flip(me, m))
+            owns = [slot_id == jnp.broadcast_to(source_row(j, 0), (HALF, rows)) for j in blocks]
+
+            def keep(at, u, kind, part):
+                for k in range(kind_count):
+                    start = (2 * k + kind) * HALF + u * size
+                    sbuf[blocks[at], pl.ds(start, size), :] = part[k * size : (k + 1) * size]
+
+            def score_part(at, u):
                 h = g * group + u
-                if u < group:
-                    grad_bufs[h % 2][...] = probs[j, h] * nn(qs[h], vx[j, h]).astype(LOW)
-                if u > 0:
-                    grad = grad_bufs[(h - 1) % 2][...]
-                    part = jnp.where(own, nn(qt2[h - 1], grad), 0.0)
-                    for k in range(kind_count):
-                        at = pl.ds(k * HALF + (u - 1) * size, size)
-                        sbuf[j, at, :] = part[k * size : (k + 1) * size]
-                    acc[h - 1] = acc[h - 1] + nt(kt[j, h - 1], grad)
-            total = shift_out[j].astype(F32) + nn(
-                key_cat, sbuf[j, pl.ds(0, kind_count * HALF), :].astype(LOW)
-            )
-            low = total.astype(LOW)
-            shift_out[j] = low
+                both = jnp.concatenate([tails[h], tails[h]], axis=0)
+                left = jnp.concatenate([qs[h], both], axis=1)
+                right = jnp.concatenate([vx[blocks[at], h], ones_pad], axis=0)
+                grad_bufs[u % 2][...] = probs[blocks[at], h] * nn(left, right).astype(LOW)
+                keep(at, u, 1, jnp.where(owns[at], nn(gt2[h], probs[blocks[at], h]), 0.0))
+
+            def key_part(at, u):
+                h = g * group + u
+                grad = grad_bufs[u % 2][...]
+                keep(at, u, 0, jnp.where(owns[at], nn(qt2[h], grad), 0.0))
+                acc[h] = acc[h] + nt(kt[blocks[at], h], grad)
+
+            units = [(at, u) for at in range(2) for u in range(group)]
+            for i in range(len(units) + 1):
+                if i < len(units):
+                    score_part(*units[i])
+                if i > 0:
+                    key_part(*units[i - 1])
+            for at in range(2):
+                j = blocks[at]
+                total = None
+                for k in range(kind_count):
+                    weights = jnp.concatenate([kw[k, :, half], vw[k, :, half]], axis=1)
+                    part = nn(weights, sbuf[j, pl.ds(k * feat, feat), :].astype(LOW))
+                    total = part if total is None else total + part
+                if g == 1:
+                    total = total + shift_out[j].astype(F32)
+                low = total.astype(LOW)
+                shift_out[j] = low
+                if g == 1:
+                    gaps = gap_hot(source_row(j, 1), levels)
+                    pack[0, 0:levels, :] = pack[0, 0:levels, :] + nt(gaps, low)
+                    if at == 0:
+                        along_y(m).start()
             if g == 1:
 
-                @pl.when(i < n_blk - 1)
+                @pl.when(pair > 0)
                 def _():
-                    send_back(j).start()
-
-                gaps = gap_hot(source_row(j, 1), levels)
-                pack_ref[0:levels, :] = pack_ref[0:levels, :] + nt(gaps, low)
+                    pass_on(m + 2)
+
+            for when, part, step in SUM_TICKS[g]:
+
+                @pl.when(pair == when)
+                def _(part=part, step=step):
+                    sums[part][step]()
+
             return carry
 
-        lax.fori_loop(0, n_blk, score_grads, 0)
-        total = None
-        for j in range(n_blk):
-            part = nt(
-                shifted[j, 0:feat, :], sbuf[j, pl.ds(0, kind_count * HALF), :].astype(LOW)
-            )
-            total = part if total is None else total + part
+        lax.fori_loop(0, n_blk // 2, block_pair, 0)
+
         for k in range(kind_count):
-            store_part(key_at(k, g), total[:, k * HALF : (k + 1) * HALF])
+            total = None
+            for j in range(n_blk):
+                part = nt(shifted[j, 0:feat, :], sbuf[j, pl.ds(k * feat, feat), :].astype(LOW))
+                total = part if total is None else total + part
+            store_part(key_at(k, g), total[:, :HALF])
+            store_part(value_at(k, g), total[:, HALF:])
         grad_q = []
         for h in range(g * group, (g + 1) * group):
             slot = acc[h, :, 0:rows]
@@ -913,6 +1160,8 @@
             store_part(query_at(k, g), nt(xt[...], masked))
             total = total + nn(qw[k, :, half], masked)
         base[...] = total
+        if g == 0:
+            sums[1][0]()
 
     pair = jnp.where(
         lane == 0,
@@ -925,168 +1174,34 @@
         skips = jnp.where(
             spot == k, jnp.sum(pick(kinds[0:1], k, skip_row), axis=1, keepdims=True), skips
         )
-    pack_ref[levels : levels + 8, :] = jnp.concatenate(
+    pack[0, levels : levels + 8, :] = jnp.concatenate(
         [pair[0:2], skips, jnp.zeros((5, rows), F32)], axis=0
     )
-    total = base[...] + shift_out[me].astype(F32)
-    for mask in range(1, n_blk):
-        j = flip(me, mask)
-        send_back(j).wait_send()
-        remote(shift_in.at[j], shift_in.at[j], back_send, back_recv, j, j, (j, rep)).wait_recv()
-        total = total + shift_in[j].astype(F32)
+    sums[2][0]()
+    along_y(0).wait_recv()
+    total = base[...] + shift_out[me].astype(F32) + plane_back[0].astype(F32)
+    sums[0][7]()
+    sums[1][4]()
+    sums[2][1]()
+    for m in (2, 4, 6):
+        along_z(m).wait_recv()
+        total = total + line_back[m // 2].astype(F32)
     input_ref[...] = total.T.astype(LOW)
-
-
-def out_at(k, half):
-    return (2 * k + half) * 256
-
-
-def msg_at(half):
-    return 2048 + half * 256
-
-
-def value_at(k, half):
-    return 2560 + (2 * k + half) * 256
-
-
-def query_at(k, half):
-    return 4608 + (8 * half + k) * 256
-
-
-def key_at(k, half):
-    return 4608 + (8 * half + 4 + k) * 256
-
-
-def att_at(half):
-    return 8704 + half * 256
-
-
-GRAD_ROWS = 9216
-
-
-def reduce_kernel(
-    grads_ref,
-    pack_ref,
-    full,
-    small_ref,
-    work,
-    core_in,
-    plane_in,
-    line_in,
-    pack_in,
-    pack_work,
-    sends,
-    recvs,
-):
-    me = lax.axis_index("blk")
-    rep = lax.axis_index("rep")
-    z, y, x, core = me // 2, me % 2, rep // 2, rep % 2
-    by_core = (me, rep + 1 - 2 * core)
-    by_x = (me, rep + 2 - 4 * x)
-    by_y = (me + 1 - 2 * y, rep)
-    by_z = [(((z + step) % 4) * 2 + y, rep) for step in (1, 2, 3)]
-    greet([by_core, by_x, by_y] + by_z)
-    total = grads_ref.shape[0]
-    half, quarter = total // 2, total // 4
-    count = iter(range(sends.shape[0]))
-
-    def send(src, dst, device):
-        at = next(count)
-        copy = remote(src, dst, sends, recvs, at, at, device)
-        copy.start()
-        return copy
-
-    def rows_of(ref, start, size):
-        return ref.at[pl.ds(pl.multiple_of(start, 16), size), :]
-
-    def load(ref, start, size):
-        return ref[pl.ds(pl.multiple_of(start, 16), size), :].astype(F32)
-
-    def add_in(start, size, *parts):
-        value = load(work, start, size)
-        for part in parts:
-            value = value + part
-        work[pl.ds(pl.multiple_of(start, 16), size), :] = value.astype(LOW)
-
-    mine = core * half
-    a = send(rows_of(grads_ref, half - mine, half), core_in, by_core)
-    b = send(pack_ref, pack_in.at[0], by_core)
-    a.wait()
-    b.wait()
-    work[...] = (load(grads_ref, mine, half) + core_in[...].astype(F32)).astype(LOW)
-    pack_work[0] = pack_ref[...] + pack_in[0]
-    size = quarter // 2
-    starts = [x * size, quarter + y * size]
-    away = [size - x * size, quarter + size - y * size]
-    copies = [
-        send(rows_of(work, away[0], size), plane_in.at[0], by_x),
-        send(rows_of(work, away[1], size), plane_in.at[1], by_y),
-        send(pack_work.at[0], pack_in.at[1], by_x),
-    ]
-    for copy in copies:
-        copy.wait()
-    for s in range(2):
-        add_in(starts[s], size, plane_in[s].astype(F32))
-    pack_work[1] = pack_work[0] + pack_in[1]
-    size = size // 2
-    turn = [y, x]
-    copies = [
-        send(
-            rows_of(work, starts[s] + size - turn[s] * size, size),
-            plane_in.at[2 + s, pl.ds(0, size), :],
-            (by_y, by_x)[s],
-        )
-        for s in range(2)
-    ]
-    copies.append(send(pack_work.at[1], pack_in.at[2], by_y))
-    for copy in copies:
-        copy.wait()
-    starts = [starts[s] + turn[s] * size for s in range(2)]
-    for s in range(2):
-        add_in(starts[s], size, plane_in[2 + s, 0:size, :].astype(F32))
-    pack_work[2] = pack_work[1] + pack_in[2]
-    size = size // 4
-    copies = []
-    for step in (2, 3, 1):
-        for s in range(2):
-            there = starts[s] + ((z + step) % 4) * size
-            copies.append(
-                send(rows_of(work, there, size), line_in.at[s, step - 1], by_z[step - 1])
-            )
-        copies.append(send(pack_work.at[2], pack_in.at[2 + step], by_z[step - 1]))
-    for copy in copies:
-        copy.wait()
-    small = pack_work[2] + pack_in[3] + pack_in[4] + pack_in[5]
-    starts = [starts[s] + z * size for s in range(2)]
-    for s in range(2):
-        value = load(work, starts[s], size)
-        for step in range(3):
-            value = value + line_in[s, step].astype(F32)
-        full[pl.ds(pl.multiple_of(mine + starts[s], 16), size), :] = value.astype(LOW)
-
-    def share(start, size, device):
-        return send(rows_of(full, start, size), rows_of(full, start, size), device)
-
-    copies = [
-        share(mine + starts[s], size, by_z[step - 1]) for step in (2, 3, 1) for s in range(2)
-    ]
-    for copy in copies:
-        copy.wait()
-    starts = [starts[s] - z * size for s in range(2)]
-    size = size * 4
-    copies = [share(mine + starts[s], size, (by_y, by_x)[s]) for s in range(2)]
-    for copy in copies:
-        copy.wait()
-    starts = [starts[s] - turn[s] * size for s in range(2)]
-    size = size * 2
-    copies = [share(mine + starts[s], size, (by_x, by_y)[s]) for s in range(2)]
-    early = [share(mine + starts[s], size, by_core) for s in range(2)]
-    for copy in copies:
-        copy.wait()
-    late = [share(mine + away[s], size, by_core) for s in range(2)]
-    for copy in early + late:
-        copy.wait()
-    small_ref[...] = small
+    sums[0][8]()
+    sums[2][2]()
+    sums[1][5]()
+    sums[2][3]()
+    sums[1][6]()
+    sums[2][4]()
+    sums[1][7]()
+    sums[2][5]()
+    sums[1][8]()
+    for step in (6, 7, 8):
+        sums[2][step]()
+    for m in (0, 2, 4, 6):
+        along_y(m).wait_send()
+        if m > 0:
+            along_z(m).wait_send()
 
 
 def finish_kernel(
@@ -1194,25 +1309,34 @@
             pltpu.VMEM((feat, rows), LOW),
             pltpu.VMEM((feat, rows), F32),
             pltpu.VMEM((n_blk, feat, rows), LOW),
-            pltpu.VMEM((n_blk, feat, rows), LOW),
+            pltpu.VMEM((n_blk // 2, feat, rows), LOW),
+            pltpu.VMEM((n_blk // 2, feat, rows), LOW),
             pltpu.SemaphoreType.DMA((5,)),
             pltpu.SemaphoreType.DMA((n_blk,)),
             pltpu.SemaphoreType.DMA((n_blk,)),
             pltpu.SemaphoreType.DMA((n_blk,)),
             pltpu.SemaphoreType.DMA((n_blk,)),
+            pltpu.VMEM((GRAD_ROWS, HALF), LOW),
+            pltpu.VMEM((GRAD_ROWS // 2, HALF), LOW),
+            pltpu.VMEM((GRAD_ROWS // 4, HALF), LOW),
+            pltpu.VMEM((GRAD_ROWS // 8, HALF), LOW),
+            pltpu.VMEM((3 * GRAD_ROWS // 32, HALF), LOW),
+            pltpu.VMEM((4, LEVELS + 8, feat), F32),
+            pltpu.VMEM((6, LEVELS + 8, feat), F32),
+            pltpu.SemaphoreType.DMA((96,)),
+            pltpu.SemaphoreType.DMA((96,)),
             pltpu.VMEM((n_blk, heads, HALF, rows), LOW),
-            pltpu.VMEM((n_blk, heads, HALF + 16, rows), LOW),
+            pltpu.VMEM((n_blk, heads, HALF, rows), LOW),
             pltpu.VMEM((n_blk, heads // 2 * rows, rows), F32),
             pltpu.VMEM((n_blk, heads, 2 * rows, rows), LOW),
-            pltpu.VMEM((heads, rows, HALF), F32),
-            pltpu.VMEM((heads, rows), F32),
-            pltpu.VMEM((heads, 2 * rows, HALF + 16), LOW),
+            pltpu.VMEM((rows, HALF), F32),
+            pltpu.VMEM((heads, 2 * rows, HALF), LOW),
+            pltpu.VMEM((heads, rows, 16), LOW),
             pltpu.VMEM((heads, HALF, 2 * rows), LOW),
             pltpu.VMEM((heads, size, rows), LOW),
             pltpu.VMEM((heads, HALF, 2 * rows), LOW),
             pltpu.VMEM((heads, HALF, 2 * rows), F32),
             pltpu.VMEM((n_blk, rows, rows), LOW),
-            pltpu.VMEM(square, F32),
             pltpu.VMEM(square, F32),
             pltpu.VMEM((2 * rows, rows), LOW),
             pltpu.VMEM((2 * rows, rows), LOW),
@@ -1262,7 +1386,7 @@
     def shape(dims, kind):
         return jax.ShapeDtypeStruct(dims, kind)
 
-    layer_out, input_grad, grads, pack, att_flat = layer_call(
+    layer_out, input_grad, full, small, att_flat = layer_call(
         n_blk,
         features,
         node_type[None],
@@ -1283,27 +1407,6 @@
         ln_gain[None],
         ln_bias[None],
     )
-    quarter = GRAD_ROWS // 4
-    full, small = pl.pallas_call(
-        reduce_kernel,
-        out_shape=[shape(grads.shape, LOW), shape(pack.shape, F32)],
-        in_specs=[vmem] * 2,
-        out_specs=[vmem] * 2,
-        scratch_shapes=[
-            pltpu.VMEM((GRAD_ROWS // 2, HALF), LOW),
-            pltpu.VMEM((GRAD_ROWS // 2, HALF), LOW),
-            pltpu.VMEM((4, quarter // 2, HALF), LOW),
-            pltpu.VMEM((2, 3, quarter // 16, HALF), LOW),
-            pltpu.VMEM((6, LEVELS + 8, feat), F32),
-            pltpu.VMEM((3, LEVELS + 8, feat), F32),
-            pltpu.SemaphoreType.DMA((40,)),
-            pltpu.SemaphoreType.DMA((40,)),
-        ],
-        compiler_params=pltpu.CompilerParams(
-            vmem_limit_bytes=VMEM_CAP, collective_id=1, has_side_effects=True
-        ),
-        name="reduce",
-    )(grads, pack)
     outs = pl.pallas_call(
         finish_kernel,
         out_shape=[shape(layer_out.shape, LOW), shape(input_grad.shape, LOW)]

time: 141 us -> 114 us (0.81)
  Pallas kernels: 140 us -> 113 us
    pallas_call x1 -> x0, Pallas kernels: 50.7 us -> none  [fast_body(): pl.pallas_call(reduce_kernel, out_shape=[shape(grads.shape, LOW), shape(p...]
    pallas_call x1, Pallas kernels: 84.1 us -> 108 us  [layer_call(): pl.pallas_call(layer_kernel, out_shape=[shape((rows, feat), LOW), shape((...]
where the time goes in v4:
time: 114 us
  Pallas kernels  113 us (99%)
    pallas_call x1, Pallas kernels, layer_call(): pl.pallas_call(layer_kernel, out_shape=[shape((rows, feat), LOW), shape((...  108 us
    pallas_call x1, Pallas kernels, fast_body(): pl.pallas_call(finish_kernel, out_shape=[shape(layer_out.shape, LOW), sha...  5.08 us

profile of v4, /device:TPU:0, one launch (start us, length us, event | category | flops | bytes accessed | tf_op | source)
XLA Modules:
  0.0 114.0 jit_solution(11187350173258523494)
XLA Ops:
  0.7 108.1 %layer.1 = (bf16[256,256]{1,0:T(8,128)(2,1)}, bf16[256,256]{1,0:T(8,128)(2,1)}, bf16[9216,128]{1,0:T(8,128)(2,1)}, f32[24,256]{1,0:T(8,128)}, bf16[256,256]{1,0:T(8,128)(2,1)}) custom-call(bf16[256,256]{1,0:T(8,128)(2,1)} %x_ref.1, s32[1,256]{1,0:T(1,128)} %bitcast.8, s32[1,256]{1,0:T(1,128)} %bitcast.9, s32[1,256]{1,0:T(1,128)} %bitcast.10, ...), custom_call_target="tpu_custom_call" | custom-call | tf_op jit(solution)/shard_map/layer/pallas_call | solution.py:1290
  108.8 5.1 %finish.1 = (bf16[256,256]{1,0:T(8,128)(2,1)}, bf16[256,256]{1,0:T(8,128)(2,1)}, f32[4,256,256]{2,1,0:T(8,128)}, f32[4,256,256]{2,1,0:T(8,128)}, f32[4,256,256]{...) custom-call(bf16[9216,128]{1,0:T(8,128)(2,1)} %get-tuple-element.31., ...), custom_call_target="tpu_custom_call" | custom-call | tf_op jit(solution)/shard_map/finish/pallas_call | solution.py:1410

commit v5 on v4

--- a/solution.py
+++ b/solution.py
@@ -392,6 +392,7 @@
 LOW = jnp.bfloat16
 VMEM_CAP = 65400 * 2**10
 PROB_UNROLL = 2
+GATHER_CUTS = 2
 
 
 def nn(a, b):
@@ -460,13 +461,13 @@
     )
 
 
-def greet(devices):
-    barrier = pltpu.get_barrier_semaphore()
-    for device in devices:
-        pl.semaphore_signal(
-            barrier, inc=1, device_id=device, device_id_type=pl.DeviceIdType.MESH
-        )
-    pl.semaphore_wait(barrier, len(devices))
+def greet(device):
+    pl.semaphore_signal(
+        pltpu.get_barrier_semaphore(),
+        inc=1,
+        device_id=device,
+        device_id_type=pl.DeviceIdType.MESH,
+    )
 
 
 def out_at(k, half):
@@ -477,26 +478,30 @@
     return 2048 + half * 256
 
 
+def key_at(k, half):
+    return 2560 + 3072 * half + k * 256
+
+
+def value_at(k, half):
+    return 2560 + 3072 * half + (4 + k) * 256
+
+
 def query_at(k, half):
-    return 2560 + (12 * half + k) * 256
-
-
-def key_at(k, half):
-    return 2560 + (12 * half + 4 + k) * 256
-
-
-def value_at(k, half):
-    return 2560 + (12 * half + 8 + k) * 256
+    return 2560 + 3072 * half + (8 + k) * 256
 
 
 def att_at(half):
     return 8704 + half * 256
 
 
-SUM_PARTS = ((0, (512, 768)), (2560, (768, 768)), (5632, (768, 1024)))
+SUM_PARTS = ((0, (512, 768)), (2560, (768, 768)), (5632, (512, 512)), (7680, (256, 512)))
 SUM_TICKS = (
     ((0, 0, 1), (2, 0, 2), (3, 0, 3)),
     ((0, 0, 4), (1, 1, 1), (2, 0, 5), (2, 1, 2), (3, 0, 6), (3, 1, 3)),
+)
+SUM_TAIL = (
+    ((0, 8), (1, 5), (2, 2), (3, 2), (1, 6), (2, 3), (3, 3), (1, 7), (2, 4), (3, 4), (1, 8))
+    + tuple((part, step) for step in (5, 6, 7, 8) for part in (2, 3))
 )
 GRAD_ROWS = 9216
 
@@ -662,13 +667,13 @@
     rte_ref,
     time_ref,
     codes_hbm,
-    cot_ref,
+    cot_hbm,
     qw_hbm,
     kw_hbm,
     vw_hbm,
     ow_hbm,
-    att_ref,
-    msg_ref,
+    att_hbm,
+    msg_hbm,
     prior_ref,
     skip_ref,
     gain_ref,
@@ -678,6 +683,9 @@
     full,
     small_ref,
     att_flat,
+    att_ref,
+    msg_ref,
+    cot_ref,
     codes,
     qw,
     kw,
@@ -728,17 +736,37 @@
     group = heads // 2
     me = lax.axis_index("blk")
     rep = lax.axis_index("rep")
+    z, y = me // 2, me % 2
+    inner = ((z + 1) // 2) % 2
+    by_y = (flip(me, 1), rep)
+    by_core = (me, rep + 1 - 2 * (rep % 2))
+    by_x = (me, rep + 2 - 4 * (rep // 2))
+    for device in (by_y, by_core, by_x):
+        greet(device)
+
+    @pl.when(z < 3)
+    def _():
+        greet((me + 2, rep))
+
+    @pl.when(z > 0)
+    def _():
+        greet((me - 2, rep))
+
     loads = [
         pltpu.make_async_copy(src, dst, load_sem.at[at])
         for at, (src, dst) in enumerate(
-            ((kw_hbm, kw), (vw_hbm, vw), (qw_hbm, qw), (codes_hbm, codes), (ow_hbm, ow))
+            (
+                (att_hbm, att_ref),
+                (msg_hbm, msg_ref),
+                (kw_hbm, kw),
+                (vw_hbm, vw),
+                (qw_hbm, qw),
+                (codes_hbm, codes),
+                (ow_hbm, ow),
+                (cot_hbm, cot_ref),
+            )
         )
     ]
-    for load in loads:
-        load.start()
-    by_core = (me, rep + 1 - 2 * (rep % 2))
-    by_x = (me, rep + 2 - 4 * (rep // 2))
-    greet([(flip(me, mask), rep) for mask in range(1, n_blk)] + [by_core, by_x])
 
     x_f = x_ref[...].astype(F32).T
     x_t = x_f.astype(LOW)
@@ -752,19 +780,57 @@
         [kind_ref[...].astype(F32), gap_ref[...].astype(F32), jnp.zeros((14, rows), F32)], axis=0
     ).astype(LOW)
 
-    def hand_on(block, mask, send_at):
+    edges = [feat * c // GATHER_CUTS for c in range(GATHER_CUTS)] + [feat + 16]
+
+    def move(block, cut, send_at, device):
+        at = pl.ds(edges[cut], edges[cut + 1] - edges[cut])
         return remote(
-            shifted.at[block],
-            shifted.at[block],
+            shifted.at[block, at, :],
+            shifted.at[block, at, :],
             gather_send,
             gather_recv,
-            send_at,
-            block,
-            (flip(me, mask), rep),
+            send_at * GATHER_CUTS + cut,
+            block * GATHER_CUTS + cut,
+            device,
         )
 
-    for mask in (1, 2, 6, 4):
-        hand_on(me, mask, mask).start()
+    def other_z(n):
+        order = ((1, 2, 1, 2), (2, 0, 3, 1), (3, 3, 0, 0))
+        table = sum(row[i] * 4 ** (4 * r + i) for r, row in enumerate(order) for i in range(4))
+        power = (1 + 3 * (z % 2)) * (1 + 15 * (z // 2)) * (1 + 255 * (n // 2)) * (1 + 255 * (n // 3))
+        own = (3 - n) // 3
+        return own * z + (1 - own) * ((table // power) % 4)
+
+    def own_moves(act):
+        for cut in range(GATHER_CUTS):
+
+            @pl.when(z < 3)
+            def _():
+                act(move(me, cut, 0, (me + 2, rep)))
+
+            @pl.when(z > 0)
+            def _():
+                act(move(me, cut, 1, (me - 2, rep)))
+
+            act(move(me, cut, 2, by_y))
+
+    def hand_on(n, act, wait):
+        there = other_z(n)
+        step = 2 * ((z - there + 3) // 4) - 1
+        block = 2 * there + y
+        for cut in range(GATHER_CUTS):
+            if wait:
+                move(block, cut, 0, by_y).wait_recv()
+            act(move(block, cut, 2 + n, by_y))
+
+            @pl.when((z + step >= 0) & (z + step <= 3))
+            def _():
+                act(move(block, cut, 5 + n, (me + 2 * step, rep)))
+
+    pl.semaphore_wait(pltpu.get_barrier_semaphore(), 4 + inner)
+    own_moves(lambda copy: copy.start())
+    for load in loads:
+        load.start()
 
     def source_row(j, row):
         return shifted[j, feat : feat + 16, :].astype(F32)[row : row + 1].astype(jnp.int32)
@@ -782,6 +848,8 @@
     def store_part(start, value):
         grads[pl.ds(start, value.shape[0]), :] = value.astype(LOW)
 
+    loads[0].wait()
+    loads[1].wait()
     for r in range(rel_count):
         for h in range(heads):
             agg[h * size : (h + 1) * size, r * size : (r + 1) * size] = att_ref[r, h].astype(F32)
@@ -794,12 +862,12 @@
     def turned(m, k):
         return probs.at[0, 2 * m + k // 2, pl.ds((k % 2) * feat, feat), :]
 
-    for m, (load, ref) in enumerate(((loads[0], kw), (loads[1], vw))):
+    for m, (load, ref) in enumerate(((loads[2], kw), (loads[3], vw))):
         load.wait()
         for k in range(kind_count):
             turned(m, k)[...] = ref[k].astype(F32).T.astype(LOW)
 
-    loads[2].wait()
+    loads[4].wait()
     q_full = jnp.zeros((feat, rows), F32)
     for k in range(kind_count):
         q_full = jnp.where(kinds_f == k, tn(qw[k], x_t), q_full)
@@ -826,7 +894,7 @@
         return carry
 
     lax.fori_loop(0, heads, query_head, 0, unroll=2)
-    loads[3].wait()
+    loads[5].wait()
     acc[:, :, 0:rows] = jnp.full((heads, HALF, rows), NEG_FILL, F32)
 
     def keep_scores(h, j, both, second, edge):
@@ -843,17 +911,7 @@
             at = slice(part * HALF, (part + 1) * HALF)
             acc[h, :, at] = jnp.maximum(acc[h, :, at], top[at])
 
-    def arrive(i, carry):
-        j = flip(me, i)
-
-        @pl.when(i > 0)
-        def _():
-            hand_on(j, 1, 0).wait_recv()
-
-        @pl.when((i > 0) & (i % 2 == 0))
-        def _():
-            hand_on(j, 1, i + 1).start()
-
+    def arrive(j):
         src = jnp.broadcast_to(source_row(j, 0), (size, rows))
         block = shifted[j, 0:feat, :]
         for k in range(kind_count):
@@ -873,11 +931,46 @@
             if h > 0:
                 keep_scores(h - 1, j, before, second, edge)
             before = both
-        return carry
-
-    lax.fori_loop(0, n_blk, arrive, 0)
-    for send_at in range(1, n_blk):
-        hand_on(me, 1, send_at).wait_send()
+
+    def start(copy):
+        copy.start()
+
+    def two_blocks(n, carry):
+        there = other_z(n)
+
+        def one(line, inside):
+            block = 2 * there + (y + line) % 2
+
+            @pl.when(line == 1)
+            def _():
+                @pl.when(n == 0)
+                def _():
+                    hand_on(1, start, True)
+
+                @pl.when((n == 0) & (inner == 1))
+                def _():
+                    hand_on(2, start, True)
+
+                @pl.when(n == 1)
+                def _():
+                    hand_on(2 + inner, start, True)
+
+                @pl.when((n == 2) & (inner == 0))
+                def _():
+                    hand_on(3, start, True)
+
+                for cut in range(GATHER_CUTS):
+                    move(block, cut, 0, by_y).wait_recv()
+
+            arrive(block)
+            return inside
+
+        return lax.fori_loop(0, 2, one, carry)
+
+    lax.fori_loop(0, n_blk // 2, two_blocks, 0)
+    own_moves(lambda copy: copy.wait_send())
+    for n in range(1, n_blk // 2):
+        hand_on(n, lambda copy: copy.wait_send(), False)
 
     def prob_block(h, j, top, kept):
         if kept:
@@ -942,7 +1035,8 @@
         rel = jnp.concatenate(rel, axis=0)
         sbuf[h // group, pl.ds((h % group) * feat, feat), :] = rel
         agg[pl.ds(h * size, size), :] = nn(head_rows(msg_flat, h), rel.astype(LOW))
-    loads[4].wait()
+    loads[6].wait()
+    loads[7].wait()
     agg_t = agg[...]
     slope = 0.7978845608028654
     inner = jnp.tanh(slope * (agg_t + 0.044715 * agg_t * agg_t * agg_t))
@@ -1021,11 +1115,10 @@
         acc[h] = jnp.zeros(acc.shape[1:], F32)
 
     refs = (grads, full, core_in, first_in, second_in, line_in, sum_send, sum_recv)
-    by_y = (flip(me, 1), rep)
     by_z = [(((me // 2 + step) % 4) * 2 + me % 2, rep) for step in (1, 2, 3)]
     places = ((me // 2, me % 2, rep // 2, rep % 2), by_core, by_x, by_y, by_z)
-    sums = [summation(part, refs, places, None) for part in range(2)]
-    sums.append(summation(2, refs, places, (pack, pack_in, small_ref)))
+    sums = [summation(part, refs, places, None) for part in range(3)]
+    sums.append(summation(3, refs, places, (pack, pack_in, small_ref)))
     sums[0][0]()
 
     slot_id = lax.broadcasted_iota(jnp.int32, (HALF, rows), 0) // size
@@ -1134,6 +1227,8 @@
                 total = part if total is None else total + part
             store_part(key_at(k, g), total[:, :HALF])
             store_part(value_at(k, g), total[:, HALF:])
+        if g == 1:
+            sums[2][0]()
         grad_q = []
         for h in range(g * group, (g + 1) * group):
             slot = acc[h, :, 0:rows]
@@ -1177,27 +1272,19 @@
     pack[0, levels : levels + 8, :] = jnp.concatenate(
         [pair[0:2], skips, jnp.zeros((5, rows), F32)], axis=0
     )
-    sums[2][0]()
-    along_y(0).wait_recv()
-    total = base[...] + shift_out[me].astype(F32) + plane_back[0].astype(F32)
+    sums[3][0]()
     sums[0][7]()
     sums[1][4]()
     sums[2][1]()
+    sums[3][1]()
+    along_y(0).wait_recv()
+    total = base[...] + shift_out[me].astype(F32) + plane_back[0].astype(F32)
     for m in (2, 4, 6):
         along_z(m).wait_recv()
         total = total + line_back[m // 2].astype(F32)
     input_ref[...] = total.T.astype(LOW)
-    sums[0][8]()
-    sums[2][2]()
-    sums[1][5]()
-    sums[2][3]()
-    sums[1][6]()
-    sums[2][4]()
-    sums[1][7]()
-    sums[2][5]()
-    sums[1][8]()
-    for step in (6, 7, 8):
-        sums[2][step]()
+    for part, step in SUM_TAIL:
+        sums[part][step]()
     for m in (0, 2, 4, 6):
         along_y(m).wait_send()
         if m > 0:
@@ -1296,9 +1383,12 @@
             shape((LEVELS + 8, feat), F32),
             shape(square, LOW),
         ],
-        in_specs=[vmem] * 6 + [hbm, vmem] + [hbm] * 4 + [vmem] * 2 + [smem] * 2 + [vmem] * 2,
+        in_specs=[vmem] * 6 + [hbm] * 8 + [smem] * 2 + [vmem] * 2,
         out_specs=[vmem] * 5,
         scratch_shapes=[
+            pltpu.VMEM((rel_count, heads, size, size), LOW),
+            pltpu.VMEM((rel_count, heads, size, size), LOW),
+            pltpu.VMEM((rows, feat), LOW),
             pltpu.VMEM((rows, n_blk * rows), jnp.int32),
             weight,
             weight,
@@ -1311,9 +1401,9 @@
             pltpu.VMEM((n_blk, feat, rows), LOW),
             pltpu.VMEM((n_blk // 2, feat, rows), LOW),
             pltpu.VMEM((n_blk // 2, feat, rows), LOW),
-            pltpu.SemaphoreType.DMA((5,)),
-            pltpu.SemaphoreType.DMA((n_blk,)),
-            pltpu.SemaphoreType.DMA((n_blk,)),
+            pltpu.SemaphoreType.DMA((8,)),
+            pltpu.SemaphoreType.DMA((9 * GATHER_CUTS,)),
+            pltpu.SemaphoreType.DMA((n_blk * GATHER_CUTS,)),
             pltpu.SemaphoreType.DMA((n_blk,)),
             pltpu.SemaphoreType.DMA((n_blk,)),
             pltpu.VMEM((GRAD_ROWS, HALF), LOW),
@@ -1323,8 +1413,8 @@
             pltpu.VMEM((3 * GRAD_ROWS // 32, HALF), LOW),
             pltpu.VMEM((4, LEVELS + 8, feat), F32),
             pltpu.VMEM((6, LEVELS + 8, feat), F32),
-            pltpu.SemaphoreType.DMA((96,)),
-            pltpu.SemaphoreType.DMA((96,)),
+            pltpu.SemaphoreType.DMA((128,)),
+            pltpu.SemaphoreType.DMA((128,)),
             pltpu.VMEM((n_blk, heads, HALF, rows), LOW),
             pltpu.VMEM((n_blk, heads, HALF, rows), LOW),
             pltpu.VMEM((n_blk, heads // 2 * rows, rows), F32),

time: 114 us -> 105 us (0.921)
  Pallas kernels: 113 us -> 104 us
    pallas_call x1, Pallas kernels: 108 us -> 98.9 us  [layer_call(): pl.pallas_call(layer_kernel, out_shape=[shape((rows, feat), LOW), shape((...]
where the time goes in v5:
time: 105 us
  Pallas kernels  104 us (99%)
    pallas_call x1, Pallas kernels, layer_call(): pl.pallas_call(layer_kernel, out_shape=[shape((rows, feat), LOW), shape((...  98.9 us
    pallas_call x1, Pallas kernels, fast_body(): pl.pallas_call(finish_kernel, out_shape=[shape(layer_out.shape, LOW), sha...  5.07 us

profile of v5, /device:TPU:0, one launch (start us, length us, event | category | flops | bytes accessed | tf_op | source)
XLA Modules:
  0.0 104.8 jit_solution(4069047909181180010)
XLA Ops:
  0.7 98.9 %layer.1 = (bf16[256,256]{1,0:T(8,128)(2,1)}, bf16[256,256]{1,0:T(8,128)(2,1)}, bf16[9216,128]{1,0:T(8,128)(2,1)}, f32[24,256]{1,0:T(8,128)}, bf16[256,256]{1,0:T(8,128)(2,1)}) custom-call(bf16[256,256]{1,0:T(8,128)(2,1)} %x_ref.1, s32[1,256]{1,0:T(1,128)} %bitcast.8, s32[1,256]{1,0:T(1,128)} %bitcast.9, s32[1,256]{1,0:T(1,128)} %bitcast.10, ...), custom_call_target="tpu_custom_call" | custom-call | tf_op jit(solution)/shard_map/layer/pallas_call | solution.py:1377
  99.6 5.1 %finish.1 = (bf16[256,256]{1,0:T(8,128)(2,1)}, bf16[256,256]{1,0:T(8,128)(2,1)}, f32[4,256,256]{2,1,0:T(8,128)}, f32[4,256,256]{2,1,0:T(8,128)}, f32[4,256,256]{...) custom-call(bf16[9216,128]{1,0:T(8,128)(2,1)} %get-tuple-element.31., ...), custom_call_target="tpu_custom_call" | custom-call | tf_op jit(solution)/shard_map/finish/pallas_call | solution.py:1500

commit v6 on v5

--- a/solution.py
+++ b/solution.py
@@ -494,15 +494,13 @@
     return 8704 + half * 256
 
 
-SUM_PARTS = ((0, (512, 768)), (2560, (768, 768)), (5632, (512, 512)), (7680, (256, 512)))
+SUM_PARTS = ((0, 2560, False), (2560, 3072, False), (5632, 2048, True), (7680, 1536, True))
 SUM_TICKS = (
     ((0, 0, 1), (2, 0, 2), (3, 0, 3)),
-    ((0, 0, 4), (1, 1, 1), (2, 0, 5), (2, 1, 2), (3, 0, 6), (3, 1, 3)),
+    ((0, 0, 4), (0, 1, 1), (2, 0, 5), (2, 1, 2), (3, 0, 6), (3, 1, 3)),
 )
-SUM_TAIL = (
-    ((0, 8), (1, 5), (2, 2), (3, 2), (1, 6), (2, 3), (3, 3), (1, 7), (2, 4), (3, 4), (1, 8))
-    + tuple((part, step) for step in (5, 6, 7, 8) for part in (2, 3))
-)
+SUM_NEXT = ((0, 7), (1, 4), (2, 1), (3, 1))
+SUM_TAIL = ((0, 8), (1, 5), (2, 2), (3, 2), (1, 6), (2, 3), (3, 3), (1, 7), (2, 4), (3, 4), (1, 8), (2, 5), (3, 5), (2, 6), (3, 6))
 GRAD_ROWS = 9216
 
 
@@ -511,15 +509,21 @@
 
 
 def summation(part, refs, places, pack):
-    grads, full, core_in, first_in, second_in, line_in, sends, recvs = refs
-    (z, y, x, core), by_core, by_x, by_y, by_z = places
-    base, streams = SUM_PARTS[part]
-    half = sum(streams)
-    ahead = sum(sum(SUM_PARTS[before][1]) for before in range(part))
-    count = iter(range(32 * part, 32 * part + 32))
+    grads, full, core_in, plane_in, line_in, sends, recvs = refs
+    (z, y, x, core), by_core, by_plane, by_z, by_y = places
+    base, rows, at_once = SUM_PARTS[part]
+    half, quarter, chunk = rows // 2, rows // 8, rows // 32
+    count = iter(range(24 * part, 24 * part + 24))
     mine = base + core * half
-    begin = (mine, mine + streams[0])
-    landing = (ahead, ahead + streams[0])
+    there_core = base + half - core * half
+    spots = [(2 * x + y + step) % 4 for step in range(4)]
+    plane_at = [mine + spot * quarter for spot in spots]
+    own_x = mine + x * 2 * quarter
+    other_x = mine + (1 - x) * 2 * quarter
+    other_y = own_x + (1 - y) * quarter
+    by_x = by_plane[1]
+    line_at = [plane_at[0] + ((z + step) % 4) * chunk for step in range(4)]
+    core_land, plane_land, line_land = base // 2, 3 * base // 8, 3 * base // 32
     pending = []
 
     def send(src, dst, device):
@@ -545,118 +549,104 @@
     def load(ref, start, size):
         return ref[span(start, size), :].astype(F32)
 
-    def add_in(start, size, ref, at):
-        value = load(grads, start, size) + load(ref, at, size)
+    def add_in(start, size, *others):
+        value = load(grads, start, size)
+        for ref, at in others:
+            value = value + load(ref, at, size)
         grads[span(start, size), :] = value.astype(LOW)
 
-    turns = ((x, y), (y, x))
-    ways = ((by_x, by_y), (by_y, by_x))
-    firsts = [size // 2 for size in streams]
-    seconds = [size // 4 for size in streams]
-    lines = [size // 16 for size in streams]
-    at_first = [begin[s] + turns[s][0] * firsts[s] for s in range(2)]
-    at_second = [at_first[s] + turns[s][1] * seconds[s] for s in range(2)]
-    at_line = [at_second[s] + z * lines[s] for s in range(2)]
-    other_z = [(z + step) % 4 for step in (1, 2, 3)]
-    aways = [
-        [begin[s] + firsts[s] - turns[s][0] * firsts[s] for s in range(2)],
-        [at_first[s] + seconds[s] - turns[s][1] * seconds[s] for s in range(2)],
-    ]
-    there_core = base + half - core * half
-    line_there = [[at_second[s] + other_z[i] * lines[s] for i in range(3)] for s in range(2)]
-    line_land = [3 * landing[s] // 16 for s in range(2)]
-
     def cores():
-        send(piece(grads, there_core, half), piece(core_in, ahead, half), by_core)
+        send(piece(grads, there_core, half), piece(core_in, core_land, half), by_core)
         if pack:
             send(small(pack[0], 0), small(pack[1], 0), by_core)
 
-    def plane_one():
+    def plane():
         settle()
-        add_in(mine, half, core_in, ahead)
-        for s in range(2):
-            send(
-                piece(grads, aways[0][s], firsts[s]),
-                piece(first_in, landing[s] // 2, firsts[s]),
-                ways[s][0],
-            )
+        for step in (2, 1, 3, 0):
+            add_in(plane_at[step], quarter, (core_in, plane_at[step] - mine + core_land))
+            if step:
+                land = plane_land + (step - 1) * quarter
+                send(
+                    piece(grads, plane_at[step], quarter),
+                    piece(plane_in, land, quarter),
+                    by_plane[step - 1],
+                )
         if pack:
             pack[0][1] = pack[0][0] + pack[1][0]
-            send(small(pack[0], 1), small(pack[1], 1), by_x)
-
-    def plane_two():
+            for step in (1, 2, 3):
+                send(small(pack[0], 1), small(pack[1], step), by_plane[step - 1])
+
+    def along_x():
         settle()
-        for s in range(2):
-            add_in(at_first[s], firsts[s], first_in, landing[s] // 2)
-        for s in range(2):
-            send(
-                piece(grads, aways[1][s], seconds[s]),
-                piece(second_in, landing[s] // 4, seconds[s]),
-                ways[s][1],
-            )
-        if pack:
-            pack[0][2] = pack[0][1] + pack[1][1]
-            send(small(pack[0], 2), small(pack[1], 2), by_y)
+        for start in (other_x, own_x):
+            add_in(start, 2 * quarter, (core_in, start - mine + core_land))
+            if start is other_x:
+                send(
+                    piece(grads, start, 2 * quarter),
+                    piece(plane_in, plane_land, 2 * quarter),
+                    by_x,
+                )
+
+    def along_y():
+        settle()
+        for start in (other_y, plane_at[0]):
+            add_in(start, quarter, (plane_in, start - own_x + plane_land))
+            if start is other_y:
+                land = plane_land + 2 * quarter
+                send(piece(grads, start, quarter), piece(plane_in, land, quarter), by_y)
 
     def line():
         settle()
-        for s in range(2):
-            add_in(at_second[s], seconds[s], second_in, landing[s] // 4)
-        for step in (2, 3, 1):
-            for s in range(2):
-                land = line_land[s] + (step - 1) * lines[s]
+        lands = range(3) if at_once else (2,)
+        for step in (2, 3, 1, 0):
+            within = line_at[step] - plane_at[0] + plane_land
+            add_in(line_at[step], chunk, *[(plane_in, within + i * quarter) for i in lands])
+            if step:
+                land = line_land + (step - 1) * chunk
                 send(
-                    piece(grads, line_there[s][step - 1], lines[s]),
-                    piece(line_in, land, lines[s]),
+                    piece(grads, line_at[step], chunk),
+                    piece(line_in, land, chunk),
                     by_z[step - 1],
                 )
         if pack:
-            pack[0][3] = pack[0][2] + pack[1][2]
+            pack[0][2] = pack[0][1] + pack[1][1] + pack[1][2] + pack[1][3]
             for step in (2, 3, 1):
-                send(small(pack[0], 3), small(pack[1], 2 + step), by_z[step - 1])
+                send(small(pack[0], 2), small(pack[1], 3 + step), by_z[step - 1])
 
     def share(start, size, device):
         send(piece(full, start, size), piece(full, start, size), device)
 
     def line_back():
         settle()
-        for s in range(2):
-            value = load(grads, at_line[s], lines[s])
-            for step in range(3):
-                value = value + load(line_in, line_land[s] + step * lines[s], lines[s])
-            full[span(at_line[s], lines[s]), :] = value.astype(LOW)
+        value = load(grads, line_at[0], chunk)
+        for step in range(3):
+            value = value + load(line_in, line_land + step * chunk, chunk)
+        full[span(line_at[0], chunk), :] = value.astype(LOW)
         for step in (2, 3, 1):
-            for s in range(2):
-                share(at_line[s], lines[s], by_z[step - 1])
+            share(line_at[0], chunk, by_z[step - 1])
         if pack:
-            pack[2][...] = pack[0][3] + pack[1][3] + pack[1][4] + pack[1][5]
-
-    def plane_two_back():
+            pack[2][...] = pack[0][2] + pack[1][4] + pack[1][5] + pack[1][6]
+
+    def plane_back():
         settle()
-        for s in range(2):
-            share(at_second[s], seconds[s], ways[s][1])
-
-    def plane_one_back():
+        for step in (2, 1, 3):
+            share(plane_at[0], quarter, by_plane[step - 1])
+
+    def back_y():
         settle()
-        for s in range(2):
-            share(at_first[s], firsts[s], ways[s][0])
+        share(plane_at[0], quarter, by_y)
+
+    def back_x():
+        settle()
+        share(own_x, 2 * quarter, by_x)
 
     def cores_back():
         settle()
-        for s in range(2):
-            share(begin[s], streams[s], by_core)
-
-    return [
-        cores,
-        plane_one,
-        plane_two,
-        line,
-        line_back,
-        plane_two_back,
-        plane_one_back,
-        cores_back,
-        settle,
-    ]
+        share(mine, half, by_core)
+
+    if at_once:
+        return [cores, plane, line, line_back, plane_back, cores_back, settle]
+    return [cores, along_x, along_y, line, line_back, back_y, back_x, cores_back, settle]
 
 
 def layer_kernel(
@@ -705,8 +695,7 @@
     back_recv,
     grads,
     core_in,
-    first_in,
-    second_in,
+    plane_in,
     line_in,
     pack,
     pack_in,
@@ -895,7 +884,7 @@
 
     lax.fori_loop(0, heads, query_head, 0, unroll=2)
     loads[5].wait()
-    acc[:, :, 0:rows] = jnp.full((heads, HALF, rows), NEG_FILL, F32)
+    acc[:, 0:rows, :] = jnp.full((heads, rows, HALF), NEG_FILL, F32)
 
     def keep_scores(h, j, both, second, edge):
         val = jnp.where(second, both[rows:], both[:rows])
@@ -907,9 +896,7 @@
             probs[j, h, 0:rows, :] = high
             probs[j, h, rows:, :] = (val - high.astype(F32)).astype(LOW)
         top = jnp.maximum(val[:, :HALF], val[:, HALF:])
-        for part in range(rows // HALF):
-            at = slice(part * HALF, (part + 1) * HALF)
-            acc[h, :, at] = jnp.maximum(acc[h, :, at], top[at])
+        acc[h, 0:rows, :] = jnp.maximum(acc[h, 0:rows, :], top)
 
     def arrive(j):
         src = jnp.broadcast_to(source_row(j, 0), (size, rows))
@@ -982,23 +969,23 @@
         second = low * two[j]
         probs[j, h, 0:rows, :] = low - second
         probs[j, h, rows:, :] = second
-        return val[:, :HALF] + val[:, HALF:]
+        return val[:, :HALF] + val[:, HALF:], jnp.concatenate([low - second, second], axis=0)
 
     sm[...] = jnp.zeros((rows, HALF), F32)
 
     def prob_head(h, kept):
-        top = jnp.concatenate([acc[h, :, 0:HALF], acc[h, :, HALF:rows]], axis=0)
-        top = jnp.max(top, axis=1, keepdims=True)
+        top = jnp.max(acc[h, 0:rows, :], axis=1, keepdims=True)
         top = jnp.broadcast_to(jnp.maximum(top, 0.1 * NEG_FILL), (rows, rows))
         value_sum = None
         total = None
         for j in range(n_blk + 1):
             if j < n_blk:
-                part = prob_block(h, j, top, kept)
+                part, now = prob_block(h, j, top, kept)
                 total = part if total is None else total + part
             if j > 0:
-                part = nt(vx[j - 1, h], probs[j - 1, h])
+                part = nt(before, vx[j - 1, h])
                 value_sum = part if value_sum is None else value_sum + part
+            before = now
         acc[h] = value_sum
         total = jnp.sum(total, axis=1, keepdims=True)
         sm[...] = jnp.where(lane == h, jnp.broadcast_to(total, (rows, HALF)), sm[...])
@@ -1025,10 +1012,11 @@
 
     for h in range(heads):
         inv = inv_row(h, HALF)
-        u_slot = acc[h, :, 0:rows] * inv
-        u_cite = acc[h, 0:size, rows:] * inv[0:size]
-        acc[h, :, 0:rows] = u_slot
-        acc[h, 0:size, rows:] = u_cite
+        u_turned = acc[h].T
+        u_slot = u_turned[:, 0:rows] * inv
+        u_cite = u_turned[0:size, rows:] * inv[0:size]
+        sbuf[2 + h // group, pl.ds((h % group) * feat, HALF), :] = u_slot
+        sbuf[2 + h // group, pl.ds((h % group) * feat + HALF, size), :] = u_cite
         rel = to_relations(
             lambda s: u_slot[s * size : (s + 1) * size], u_cite, kinds, kind_count, rel_count
         )
@@ -1100,9 +1088,14 @@
         gt2[h, :, rows:] = cite_t
         slot_f = slot_t.astype(F32)
         cite_f = cite_t.astype(F32)
+        u_at = (h % group) * feat
         delta = -(
-            jnp.sum(slot_f * acc[h, :, 0:rows], axis=0, keepdims=True)
-            + jnp.sum(cite_f[0:size] * acc[h, 0:size, rows:], axis=0, keepdims=True)
+            jnp.sum(slot_f * sbuf[2 + h // group, pl.ds(u_at, HALF), :], axis=0, keepdims=True)
+            + jnp.sum(
+                cite_f[0:size] * sbuf[2 + h // group, pl.ds(u_at + HALF, size), :],
+                axis=0,
+                keepdims=True,
+            )
         )
         delta_hi = delta.astype(LOW).astype(F32)
         tail = jnp.concatenate(
@@ -1114,9 +1107,11 @@
         tails[h] = tail_t[:, 0:16]
         acc[h] = jnp.zeros(acc.shape[1:], F32)
 
-    refs = (grads, full, core_in, first_in, second_in, line_in, sum_send, sum_recv)
+    refs = (grads, full, core_in, plane_in, line_in, sum_send, sum_recv)
     by_z = [(((me // 2 + step) % 4) * 2 + me % 2, rep) for step in (1, 2, 3)]
-    places = ((me // 2, me % 2, rep // 2, rep % 2), by_core, by_x, by_y, by_z)
+    spots = [(2 * (rep // 2) + y + step) % 4 for step in (1, 2, 3)]
+    by_plane = [(2 * z + spot % 2, 2 * (spot // 2) + rep % 2) for spot in spots]
+    places = ((z, y, rep // 2, rep % 2), by_core, by_plane, by_z, by_y)
     sums = [summation(part, refs, places, None) for part in range(3)]
     sums.append(summation(3, refs, places, (pack, pack_in, small_ref)))
     sums[0][0]()
@@ -1173,21 +1168,25 @@
                 both = jnp.concatenate([tails[h], tails[h]], axis=0)
                 left = jnp.concatenate([qs[h], both], axis=1)
                 right = jnp.concatenate([vx[blocks[at], h], ones_pad], axis=0)
-                grad_bufs[u % 2][...] = probs[blocks[at], h] * nn(left, right).astype(LOW)
+                grad_bufs[u % 2][:, at * rows : (at + 1) * rows] = probs[blocks[at], h] * nn(
+                    left, right
+                ).astype(LOW)
                 keep(at, u, 1, jnp.where(owns[at], nn(gt2[h], probs[blocks[at], h]), 0.0))
 
             def key_part(at, u):
                 h = g * group + u
-                grad = grad_bufs[u % 2][...]
+                grad = grad_bufs[u % 2][:, at * rows : (at + 1) * rows]
                 keep(at, u, 0, jnp.where(owns[at], nn(qt2[h], grad), 0.0))
-                acc[h] = acc[h] + nt(kt[blocks[at], h], grad)
-
-            units = [(at, u) for at in range(2) for u in range(group)]
-            for i in range(len(units) + 1):
+                if at == 1:
+                    keys = jnp.concatenate([kt[j, h] for j in blocks], axis=1)
+                    acc[h] = acc[h] + nt(grad_bufs[u % 2][...], keys)
+
+            units = [(at, u) for u in range(group) for at in range(2)]
+            for i in range(len(units) + 2):
                 if i < len(units):
                     score_part(*units[i])
-                if i > 0:
-                    key_part(*units[i - 1])
+                if i > 1:
+                    key_part(*units[i - 2])
             for at in range(2):
                 j = blocks[at]
                 total = None
@@ -1231,10 +1230,10 @@
             sums[2][0]()
         grad_q = []
         for h in range(g * group, (g + 1) * group):
-            slot = acc[h, :, 0:rows]
+            slot = acc[h].T
             rel = to_relations(
-                lambda s: slot[s * size : (s + 1) * size],
-                acc[h, 0:size, rows:],
+                lambda s: slot[s * size : (s + 1) * size, 0:rows],
+                slot[0:size, rows:],
                 kinds,
                 kind_count,
                 rel_count,
@@ -1273,10 +1272,8 @@
         [pair[0:2], skips, jnp.zeros((5, rows), F32)], axis=0
     )
     sums[3][0]()
-    sums[0][7]()
-    sums[1][4]()
-    sums[2][1]()
-    sums[3][1]()
+    for part, step in SUM_NEXT:
+        sums[part][step]()
     along_y(0).wait_recv()
     total = base[...] + shift_out[me].astype(F32) + plane_back[0].astype(F32)
     for m in (2, 4, 6):
@@ -1408,13 +1405,12 @@
             pltpu.SemaphoreType.DMA((n_blk,)),
             pltpu.VMEM((GRAD_ROWS, HALF), LOW),
             pltpu.VMEM((GRAD_ROWS // 2, HALF), LOW),
-            pltpu.VMEM((GRAD_ROWS // 4, HALF), LOW),
-            pltpu.VMEM((GRAD_ROWS // 8, HALF), LOW),
+            pltpu.VMEM((3 * GRAD_ROWS // 8, HALF), LOW),
             pltpu.VMEM((3 * GRAD_ROWS // 32, HALF), LOW),
-            pltpu.VMEM((4, LEVELS + 8, feat), F32),
-            pltpu.VMEM((6, LEVELS + 8, feat), F32),
-            pltpu.SemaphoreType.DMA((128,)),
-            pltpu.SemaphoreType.DMA((128,)),
+            pltpu.VMEM((3, LEVELS + 8, feat), F32),
+            pltpu.VMEM((7, LEVELS + 8, feat), F32),
+            pltpu.SemaphoreType.DMA((96,)),
+            pltpu.SemaphoreType.DMA((96,)),
             pltpu.VMEM((n_blk, heads, HALF, rows), LOW),
             pltpu.VMEM((n_blk, heads, HALF, rows), LOW),
             pltpu.VMEM((n_blk, heads // 2 * rows, rows), F32),
@@ -1425,11 +1421,11 @@
             pltpu.VMEM((heads, HALF, 2 * rows), LOW),
             pltpu.VMEM((heads, size, rows), LOW),
             pltpu.VMEM((heads, HALF, 2 * rows), LOW),
-            pltpu.VMEM((heads, HALF, 2 * rows), F32),
+            pltpu.VMEM((heads, 2 * rows, HALF), F32),
             pltpu.VMEM((n_blk, rows, rows), LOW),
             pltpu.VMEM(square, F32),
-            pltpu.VMEM((2 * rows, rows), LOW),
-            pltpu.VMEM((2 * rows, rows), LOW),
+            pltpu.VMEM((2 * rows, 2 * rows), LOW),
+            pltpu.VMEM((2 * rows, 2 * rows), LOW),
         ],
         compiler_params=pltpu.CompilerParams(
             vmem_limit_bytes=VMEM_CAP, collective_id=0, has_side_effects=True

time: 105 us -> 100 us (0.952)
  Pallas kernels: 104 us -> 99.2 us
    pallas_call x1, Pallas kernels: 98.9 us -> 94.1 us  [layer_call(): pl.pallas_call(layer_kernel, out_shape=[shape((rows, feat), LOW), shape((...]
where the time goes in v6:
time: 100 us
  Pallas kernels  99.2 us (99%)
    pallas_call x1, Pallas kernels, layer_call(): pl.pallas_call(layer_kernel, out_shape=[shape((rows, feat), LOW), shape((...  94.1 us
    pallas_call x1, Pallas kernels, fast_body(): pl.pallas_call(finish_kernel, out_shape=[shape(layer_out.shape, LOW), sha...  5.08 us

profile of v6, /device:TPU:0, one launch (start us, length us, event | category | flops | bytes accessed | tf_op | source)
XLA Modules:
  0.0 100.0 jit_solution(11784620397142524424)
XLA Ops:
  0.7 94.1 %layer.1 = (bf16[256,256]{1,0:T(8,128)(2,1)}, bf16[256,256]{1,0:T(8,128)(2,1)}, bf16[9216,128]{1,0:T(8,128)(2,1)}, f32[24,256]{1,0:T(8,128)}, bf16[256,256]{1,0:T(8,128)(2,1)}) custom-call(bf16[256,256]{1,0:T(8,128)(2,1)} %x_ref.1, s32[1,256]{1,0:T(1,128)} %bitcast.8, s32[1,256]{1,0:T(1,128)} %bitcast.9, s32[1,256]{1,0:T(1,128)} %bitcast.10, ...), custom_call_target="tpu_custom_call" | custom-call | tf_op jit(solution)/shard_map/layer/pallas_call | solution.py:1374
  94.7 5.1 %finish.1 = (bf16[256,256]{1,0:T(8,128)(2,1)}, bf16[256,256]{1,0:T(8,128)(2,1)}, f32[4,256,256]{2,1,0:T(8,128)}, f32[4,256,256]{2,1,0:T(8,128)}, f32[4,256,256]{...) custom-call(bf16[9216,128]{1,0:T(8,128)(2,1)} %get-tuple-element.31., ...), custom_call_target="tpu_custom_call" | custom-call | tf_op jit(solution)/shard_map/finish/pallas_call | solution.py:1496

commit v7 on v6

--- a/solution.py
+++ b/solution.py
@@ -12,6 +12,7 @@
 
 
 NEG_FILL = -1e30
+LOG2_E = 1.4426950408889634
 LN_EPS = 1e-05
 HIGH = lax.Precision.HIGHEST
 
@@ -887,7 +888,7 @@
     acc[:, 0:rows, :] = jnp.full((heads, rows, HALF), NEG_FILL, F32)
 
     def keep_scores(h, j, both, second, edge):
-        val = jnp.where(second, both[rows:], both[:rows])
+        val = jnp.where(second, both[rows:], both[:rows]) * LOG2_E
         val = jnp.where(edge, val, NEG_FILL)
         if h < group:
             sbuf[j, pl.ds(h * rows, rows), :] = val
@@ -964,7 +965,7 @@
             val = sbuf[j, pl.ds(pl.multiple_of(h * rows, rows), rows), :]
         else:
             val = probs[j, h, 0:rows, :].astype(F32) + probs[j, h, rows:, :].astype(F32)
-        val = jnp.exp(val - top)
+        val = jnp.exp2(val - top)
         low = val.astype(LOW)
         second = low * two[j]
         probs[j, h, 0:rows, :] = low - second

time: 100 us -> 99.9 us (level)
  no operation moved by 1% of the time
where the time goes in v7:
time: 99.9 us; the launch traced here: 99.7 us
  Pallas kernels  98.9 us (99%)
    pallas_call x1, Pallas kernels, layer_call(): pl.pallas_call(layer_kernel, out_shape=[shape((rows, feat), LOW), shape((...  93.8 us
    pallas_call x1, Pallas kernels, fast_body(): pl.pallas_call(finish_kernel, out_shape=[shape(layer_out.shape, LOW), sha...  5.07 us

profile of v7, /device:TPU:0, one launch (start us, length us, event | category | flops | bytes accessed | tf_op | source)
XLA Modules:
  0.0 99.7 jit_solution(257094062258749897)
XLA Ops:
  0.7 93.8 %layer.1 = (bf16[256,256]{1,0:T(8,128)(2,1)}, bf16[256,256]{1,0:T(8,128)(2,1)}, bf16[9216,128]{1,0:T(8,128)(2,1)}, f32[24,256]{1,0:T(8,128)}, bf16[256,256]{1,0:T(8,128)(2,1)}) custom-call(bf16[256,256]{1,0:T(8,128)(2,1)} %x_ref.1, s32[1,256]{1,0:T(1,128)} %bitcast.8, s32[1,256]{1,0:T(1,128)} %bitcast.9, s32[1,256]{1,0:T(1,128)} %bitcast.10, ...), custom_call_target="tpu_custom_call" | custom-call | tf_op jit(solution)/shard_map/layer/pallas_call | solution.py:1375
  94.5 5.1 %finish.1 = (bf16[256,256]{1,0:T(8,128)(2,1)}, bf16[256,256]{1,0:T(8,128)(2,1)}, f32[4,256,256]{2,1,0:T(8,128)}, f32[4,256,256]{2,1,0:T(8,128)}, f32[4,256,256]{...) custom-call(bf16[9216,128]{1,0:T(8,128)(2,1)} %get-tuple-element.31., ...), custom_call_target="tpu_custom_call" | custom-call | tf_op jit(solution)/shard_map/finish/pallas_call | solution.py:1497

commit v8 on v7

--- a/solution.py
+++ b/solution.py
@@ -1119,6 +1119,20 @@
 
     slot_id = lax.broadcasted_iota(jnp.int32, (HALF, rows), 0) // size
     pack[0] = jnp.zeros(pack.shape[1:], F32)
+    pair = jnp.where(
+        lane == 0,
+        jnp.broadcast_to(gain_col, (feat, HALF)),
+        jnp.where(lane == 1, jnp.broadcast_to(bias_col, (feat, HALF)), 0.0),
+    ).T
+    spot = lax.broadcasted_iota(jnp.int32, (1, rows), 1)
+    skips = jnp.zeros((1, rows), F32)
+    for k in range(kind_count):
+        skips = jnp.where(
+            spot == k, jnp.sum(pick(kinds[0:1], k, skip_row), axis=1, keepdims=True), skips
+        )
+    pack[0, levels : levels + 8, :] = jnp.concatenate(
+        [pair[0:2], skips, jnp.zeros((5, rows), F32)], axis=0
+    )
 
     def along_y(m):
         return remote(
@@ -1249,30 +1263,18 @@
             ]
             grad_q.append(nn(head_rows(att_flat, h), jnp.concatenate(raw, axis=0)))
         grad_q = jnp.concatenate(grad_q, axis=0).astype(LOW).astype(F32)
+        masked = [pick(kinds_f[0:HALF], k, grad_q).astype(LOW) for k in range(kind_count)]
+        for k in range(kind_count):
+            store_part(query_at(k, g), nt(xt[...], masked[k]))
+        if g == 1:
+            sums[3][0]()
         total = base[...]
         for k in range(kind_count):
-            masked = pick(kinds_f[0:HALF], k, grad_q).astype(LOW)
-            store_part(query_at(k, g), nt(xt[...], masked))
-            total = total + nn(qw[k, :, half], masked)
+            total = total + nn(qw[k, :, half], masked[k])
         base[...] = total
         if g == 0:
             sums[1][0]()
 
-    pair = jnp.where(
-        lane == 0,
-        jnp.broadcast_to(gain_col, (feat, HALF)),
-        jnp.where(lane == 1, jnp.broadcast_to(bias_col, (feat, HALF)), 0.0),
-    ).T
-    spot = lax.broadcasted_iota(jnp.int32, (1, rows), 1)
-    skips = jnp.zeros((1, rows), F32)
-    for k in range(kind_count):
-        skips = jnp.where(
-            spot == k, jnp.sum(pick(kinds[0:1], k, skip_row), axis=1, keepdims=True), skips
-        )
-    pack[0, levels : levels + 8, :] = jnp.concatenate(
-        [pair[0:2], skips, jnp.zeros((5, rows), F32)], axis=0
-    )
-    sums[3][0]()
     for part, step in SUM_NEXT:
         sums[part][step]()
     along_y(0).wait_recv()

time: 99.9 us -> 100 us (level)
  no operation moved by 1% of the time
where the time goes in v8:
time: 100 us; the launch traced here: 99.9 us
  Pallas kernels  99.1 us (99%)
    pallas_call x1, Pallas kernels, layer_call(): pl.pallas_call(layer_kernel, out_shape=[shape((rows, feat), LOW), shape((...  94 us
    pallas_call x1, Pallas kernels, fast_body(): pl.pallas_call(finish_kernel, out_shape=[shape(layer_out.shape, LOW), sha...  5.07 us

profile of v8, /device:TPU:0, one launch (start us, length us, event | category | flops | bytes accessed | tf_op | source)
XLA Modules:
  0.0 99.9 jit_solution(3201689857902618563)
XLA Ops:
  0.7 94.0 %layer.1 = (bf16[256,256]{1,0:T(8,128)(2,1)}, bf16[256,256]{1,0:T(8,128)(2,1)}, bf16[9216,128]{1,0:T(8,128)(2,1)}, f32[24,256]{1,0:T(8,128)}, bf16[256,256]{1,0:T(8,128)(2,1)}) custom-call(bf16[256,256]{1,0:T(8,128)(2,1)} %x_ref.1, s32[1,256]{1,0:T(1,128)} %bitcast.8, s32[1,256]{1,0:T(1,128)} %bitcast.9, s32[1,256]{1,0:T(1,128)} %bitcast.10, ...), custom_call_target="tpu_custom_call" | custom-call | tf_op jit(solution)/shard_map/layer/pallas_call | solution.py:1377
  94.7 5.1 %finish.1 = (bf16[256,256]{1,0:T(8,128)(2,1)}, bf16[256,256]{1,0:T(8,128)(2,1)}, f32[4,256,256]{2,1,0:T(8,128)}, f32[4,256,256]{2,1,0:T(8,128)}, f32[4,256,256]{...) custom-call(bf16[9216,128]{1,0:T(8,128)(2,1)} %get-tuple-element.31., ...), custom_call_target="tpu_custom_call" | custom-call | tf_op jit(solution)/shard_map/finish/pallas_call | solution.py:1499
